TPU v7x, 32 devices: a whole 2x2x4 slice. The times are simulated.
32 devices in a mesh: row: 4 (over y, core), col: 8 (over z, x).
Axes of the slice: x: 2, y: 2, z: 4, core: 2. Of those that a mesh axis runs over, the one named last changes fastest.
Arguments:
- node_features: bfloat16 [8192, 512], P('col', 'row'), may hold values from -6 to 6
- layer_weight: bfloat16 [512, 512], replicated, may hold values from -0.25 to 0.25
- tile_values: bfloat16 [4, 8, 96, 128, 128], P('row', 'col')
- tile_coords: int32 [4, 8, 96, 2], P('row', 'col'), may hold values from 0 to 15, as said below
- tile_count: int32 [4, 8], P('row', 'col'), may hold values from 32 to 96, as said below
- cotangent: bfloat16 [8192, 512], P(('row', 'col')), may hold values from -6 to 6
Outputs:
- hidden: bfloat16 [8192, 512], P(('row', 'col'))
- grad_weight: float32 [512, 512], replicated
- grad_features: bfloat16 [8192, 512], P('col', 'row')
Inputs may be any that keep to these rules, and one draw needn't show every extreme that they name: `tile_coords`: entry 0 of a slot is its destination tile within the destination block, below 16; entry 1 its source tile within the source block, below 8; the slots of one block pair name distinct positions. `tile_count`: slots at or beyond the count hold arbitrary tiles that are not part of the adjacency.
All inputs are finite; a program needn't handle non-finite values.
Results may differ from a plain program's by a relative error of at most 0.0054.
Values may be sent and summed in bfloat16 or wider, within the bound.
No kernel may reach another device: no remote copies, remote signals or barrier semaphores. Data moves between devices by JAX's collectives and lax.ppermute only.
A program may use at most 128 MiB of HBM per device.

v0:
```python
import math

import jax
import jax.numpy as jnp
from jax import lax
from jax.sharding import PartitionSpec as P


def tile_sweep(
    tile_groups, pick_groups, place_groups, live_groups, source_tiles, out_tiles, backward_dir
):
    tile_size = source_tiles.shape[1]
    width = source_tiles.shape[2]

    def one_turn(totals, inputs):
        block_tiles, picked, placed, live_block = inputs
        gathered_rows = source_tiles[picked]
        if backward_dir:
            product = jnp.einsum(
                "tab,tak->tbk", block_tiles, gathered_rows, preferred_element_type=jnp.float32
            )
        else:
            product = jnp.einsum(
                "tab,tbk->tak", block_tiles, gathered_rows, preferred_element_type=jnp.float32
            )
        product = jnp.where(live_block[:, None, None], product, jnp.float32(0.0))
        return (totals.at[placed].add(product), None)

    start_totals = jnp.zeros((out_tiles, tile_size, width), jnp.float32)
    totals, unused = lax.scan(
        one_turn, start_totals, (tile_groups, pick_groups, place_groups, live_groups)
    )
    return totals


def body(node_features, layer_weight, tile_values, tile_coords, tile_count, cotangent):
    slots = tile_values.shape[2]
    tile_size = tile_values.shape[3]
    width = layer_weight.shape[0]
    tiles = tile_values[0, 0]
    coords = tile_coords[0, 0]
    live_count = tile_count[0, 0]
    block_r = cotangent.shape[0] * lax.axis_size("col")
    block_c = node_features.shape[0]
    dest_tiles = block_r // tile_size
    source_count = block_c // tile_size
    group_size = math.gcd(slots, 16)
    group_count = slots // group_size
    is_live = jnp.arange(slots) < live_count
    tile_groups = tiles.reshape(group_count, group_size, tile_size, tile_size)
    dest_picks = coords[:, 0].reshape(group_count, group_size)
    source_picks = coords[:, 1].reshape(group_count, group_size)
    live_groups = is_live.reshape(group_count, group_size)
    shard_piece = lax.all_gather(node_features, "row", axis=1, tiled=True)
    piece_width = shard_piece.shape[1]
    source_tiles = shard_piece.reshape(source_count, tile_size, piece_width)
    totals = tile_sweep(
        tile_groups, source_picks, dest_picks, live_groups, source_tiles, dest_tiles, False
    )
    partial_value = totals.reshape(block_r, piece_width)
    aggregated = lax.psum_scatter(partial_value, "col", scatter_dimension=0, tiled=True).astype(
        jnp.bfloat16
    )
    pre_act = jnp.dot(aggregated, layer_weight, preferred_element_type=jnp.float32)
    hidden = jax.nn.elu(pre_act).astype(jnp.bfloat16)
    slope = jnp.where(pre_act > 0, jnp.float32(1.0), jnp.exp(jnp.minimum(pre_act, 0.0)))
    grad_pre = (cotangent.astype(jnp.float32) * slope).astype(jnp.bfloat16)
    weight_term = jnp.einsum("nf,ng->fg", aggregated, grad_pre, preferred_element_type=jnp.float32)
    grad_weight = lax.psum(weight_term, ("row", "col"))
    grad_agg = jnp.einsum(
        "ng,fg->nf", grad_pre, layer_weight, preferred_element_type=jnp.float32
    ).astype(jnp.bfloat16)
    block_grads = lax.all_gather(grad_agg, "col", axis=0, tiled=True)
    dest_rows = block_grads.reshape(dest_tiles, tile_size, width)
    back = tile_sweep(
        tile_groups, dest_picks, source_picks, live_groups, dest_rows, source_count, True
    )
    back = back.reshape(block_c, width)
    grad_features = lax.psum_scatter(back, "row", scatter_dimension=1, tiled=True).astype(
        jnp.bfloat16
    )
    return (hidden, grad_weight, grad_features)


def solution(mesh):
    in_specs = (
        P("col", "row"),
        P(),
        P("row", "col", None, None, None),
        P("row", "col", None, None),
        P("row", "col"),
        P(("row", "col"), None),
    )
    out_specs = (P(("row", "col"), None), P(), P("col", "row"))
    return jax.shard_map(body, mesh=mesh, in_specs=in_specs, out_specs=out_specs, check_vma=False)
```

profile of v0, /device:TPU:0, one launch (start us, length us, event | category | flops | bytes accessed | tf_op | source)
XLA Modules:
  0.0 525.0 jit_solution(16463672294989754149)
XLA Ops:
  9.6 19.6 %all-gather.3.cloned.1.call-done = bf16[1024,512]{1,0:T(8,128)(2,1)} async-done(((bf16[1024,128]{1,0:T(8,128)(2,1)}), bf16[1024,512]{1,0:T(8,128)(2,1)}) %all-gather.3.cloned.1.call-update) | async-done | bytes 1048592 | tf_op jit(solution)/shard_map/all_gather | solution.py:54
  31.7 90.6 %while.20 = (s32[]{:T(128)}, f32[16,128,512]{2,1,0:T(8,128)}, s32[6,16]{1,0:T(8,128)S(1)}, pred[6,16]{1,0:T(8,128)(4,1)S(1)}, bf16[6,16,128,128]{3,2,1,0:T(8,128...) while((s32[]{:T(128)}, f32[16,128,512]{2,1,0:T(8,128)}, s32[6,16]{1,0:T(8,128)S(1)}, ...), condition=%wide.region_2.3_spmd, body=%wide.region_0.2_spmd.sunk | while | flops 270533728 | bytes 23598156 | solution.py:30
  37.3 9.4 %scatter_fusion = f32[16,128,512]{2,1,0:T(8,128)} fusion(f32[16,128,512]{2,1,0:T(8,128)} %get-tuple-element.225, s32[16]{0:T(128)S(1)} %get-tuple-element.205, f32[16,128,512]{2,1,0:T(8,128)} %convolution_select_fusion.4), kind=kCustom, calls=%fused_computation.2.clone.1 | custom fusion | flops 1048576 | bytes 12582976 | tf_op jit(solution)/shard_map/while/body/eval_jaxpr/scatter-add | solution.py:27
  52.3 9.7 %scatter_fusion = f32[16,128,512]{2,1,0:T(8,128)} fusion(f32[16,128,512]{2,1,0:T(8,128)} %get-tuple-element.225, s32[16]{0:T(128)S(1)} %get-tuple-element.205, f32[16,128,512]{2,1,0:T(8,128)} %convolution_select_fusion.4), kind=kCustom, calls=%fused_computation.2.clone.1 | custom fusion | flops 1048576 | bytes 12582976 | tf_op jit(solution)/shard_map/while/body/eval_jaxpr/scatter-add | solution.py:27
  67.6 9.3 %scatter_fusion = f32[16,128,512]{2,1,0:T(8,128)} fusion(f32[16,128,512]{2,1,0:T(8,128)} %get-tuple-element.225, s32[16]{0:T(128)S(1)} %get-tuple-element.205, f32[16,128,512]{2,1,0:T(8,128)} %convolution_select_fusion.4), kind=kCustom, calls=%fused_computation.2.clone.1 | custom fusion | flops 1048576 | bytes 12582976 | tf_op jit(solution)/shard_map/while/body/eval_jaxpr/scatter-add | solution.py:27
  82.5 9.5 %scatter_fusion = f32[16,128,512]{2,1,0:T(8,128)} fusion(f32[16,128,512]{2,1,0:T(8,128)} %get-tuple-element.225, s32[16]{0:T(128)S(1)} %get-tuple-element.205, f32[16,128,512]{2,1,0:T(8,128)} %convolution_select_fusion.4), kind=kCustom, calls=%fused_computation.2.clone.1 | custom fusion | flops 1048576 | bytes 12582976 | tf_op jit(solution)/shard_map/while/body/eval_jaxpr/scatter-add | solution.py:27
  97.6 9.4 %scatter_fusion = f32[16,128,512]{2,1,0:T(8,128)} fusion(f32[16,128,512]{2,1,0:T(8,128)} %get-tuple-element.225, s32[16]{0:T(128)S(1)} %get-tuple-element.205, f32[16,128,512]{2,1,0:T(8,128)} %convolution_select_fusion.4), kind=kCustom, calls=%fused_computation.2.clone.1 | custom fusion | flops 1048576 | bytes 12582976 | tf_op jit(solution)/shard_map/while/body/eval_jaxpr/scatter-add | solution.py:27
  112.7 9.6 %scatter_fusion = f32[16,128,512]{2,1,0:T(8,128)} fusion(f32[16,128,512]{2,1,0:T(8,128)} %get-tuple-element.225, s32[16]{0:T(128)S(1)} %get-tuple-element.205, f32[16,128,512]{2,1,0:T(8,128)} %convolution_select_fusion.4), kind=kCustom, calls=%fused_computation.2.clone.1 | custom fusion | flops 1048576 | bytes 12582976 | tf_op jit(solution)/shard_map/while/body/eval_jaxpr/scatter-add | solution.py:27
  122.4 88.2 %reduce-scatter.3.cloned.1.call-done = f32[256,512]{1,0:T(8,128)} async-done(((f32[2048,512]{1,0:T(8,128)}), f32[256,512]{1,0:T(8,128)}) %reduce-scatter.3.cloned.1.call-update) | async-done | bytes 524304 | tf_op jit(solution)/shard_map/reduce_scatter | solution.py:61
  214.7 4.7 copy.9
  219.4 44.5 %all-gather.5.cloned.1.call-done = bf16[2048,512]{1,0:T(8,128)(2,1)} async-done(((bf16[256,512]{1,0:T(8,128)(2,1)}), bf16[2048,512]{1,0:T(8,128)(2,1)}) %all-gather.5.cloned.1.call-update) | async-done | bytes 2097168 | tf_op jit(solution)/shard_map/all_gather | solution.py:73
  264.1 85.1 %while.21 = (s32[]{:T(128)}, f32[8,128,512]{2,1,0:T(8,128)S(1)}, s32[6,16]{1,0:T(8,128)S(1)}, pred[6,16]{1,0:T(8,128)(4,1)S(1)}, bf16[6,16,128,128]{2,3,1,0:T(8,...) while((s32[]{:T(128)}, f32[8,128,512]{2,1,0:T(8,128)S(1)}, ...), condition=%wide.region_7.8_spmd, body=%wide.region_5.7_spmd.sunk | while | flops 270533728 | bytes 23598156 | solution.py:30
  267.8 4.4 convolution_select_fusion.5
  272.2 6.2 %scatter_fusion.1 = f32[8,128,512]{2,1,0:T(8,128)S(1)} fusion(f32[8,128,512]{2,1,0:T(8,128)S(1)} %get-tuple-element.249, s32[16]{0:T(128)S(1)} %get-tuple-element.214, f32[16,128,512]{2,1,0:T(8,128)} %convolution_select_fusion.5), kind=kCustom, calls=%fused_computation.3.clone.1 | custom fusion | flops 1048576 | bytes 12582976 | tf_op jit(solution)/shard_map/while/body/eval_jaxpr/scatter-add | solution.py:27
  286.3 6.1 %scatter_fusion.1 = f32[8,128,512]{2,1,0:T(8,128)S(1)} fusion(f32[8,128,512]{2,1,0:T(8,128)S(1)} %get-tuple-element.249, s32[16]{0:T(128)S(1)} %get-tuple-element.214, f32[16,128,512]{2,1,0:T(8,128)} %convolution_select_fusion.5), kind=kCustom, calls=%fused_computation.3.clone.1 | custom fusion | flops 1048576 | bytes 12582976 | tf_op jit(solution)/shard_map/while/body/eval_jaxpr/scatter-add | solution.py:27
  296.1 4.4 convolution_select_fusion.5
  300.5 6.2 %scatter_fusion.1 = f32[8,128,512]{2,1,0:T(8,128)S(1)} fusion(f32[8,128,512]{2,1,0:T(8,128)S(1)} %get-tuple-element.249, s32[16]{0:T(128)S(1)} %get-tuple-element.214, f32[16,128,512]{2,1,0:T(8,128)} %convolution_select_fusion.5), kind=kCustom, calls=%fused_computation.3.clone.1 | custom fusion | flops 1048576 | bytes 12582976 | tf_op jit(solution)/shard_map/while/body/eval_jaxpr/scatter-add | solution.py:27
  310.3 4.4 convolution_select_fusion.5
  314.7 6.2 %scatter_fusion.1 = f32[8,128,512]{2,1,0:T(8,128)S(1)} fusion(f32[8,128,512]{2,1,0:T(8,128)S(1)} %get-tuple-element.249, s32[16]{0:T(128)S(1)} %get-tuple-element.214, f32[16,128,512]{2,1,0:T(8,128)} %convolution_select_fusion.5), kind=kCustom, calls=%fused_computation.3.clone.1 | custom fusion | flops 1048576 | bytes 12582976 | tf_op jit(solution)/shard_map/while/body/eval_jaxpr/scatter-add | solution.py:27
  324.5 4.4 convolution_select_fusion.5
  328.9 6.1 %scatter_fusion.1 = f32[8,128,512]{2,1,0:T(8,128)S(1)} fusion(f32[8,128,512]{2,1,0:T(8,128)S(1)} %get-tuple-element.249, s32[16]{0:T(128)S(1)} %get-tuple-element.214, f32[16,128,512]{2,1,0:T(8,128)} %convolution_select_fusion.5), kind=kCustom, calls=%fused_computation.3.clone.1 | custom fusion | flops 1048576 | bytes 12582976 | tf_op jit(solution)/shard_map/while/body/eval_jaxpr/scatter-add | solution.py:27
  343.1 6.2 %scatter_fusion.1 = f32[8,128,512]{2,1,0:T(8,128)S(1)} fusion(f32[8,128,512]{2,1,0:T(8,128)S(1)} %get-tuple-element.249, s32[16]{0:T(128)S(1)} %get-tuple-element.214, f32[16,128,512]{2,1,0:T(8,128)} %convolution_select_fusion.5), kind=kCustom, calls=%fused_computation.3.clone.1 | custom fusion | flops 1048576 | bytes 12582976 | tf_op jit(solution)/shard_map/while/body/eval_jaxpr/scatter-add | solution.py:27
  353.1 27.6 %reduce-scatter.5.cloned.1.call-done = f32[1024,128]{1,0:T(8,128)} async-done(((f32[1024,512]{1,0:T(8,128)}), f32[1024,128]{1,0:T(8,128)}) %reduce-scatter.5.cloned.1.call-update) | async-done | bytes 524304 | tf_op jit(solution)/shard_map/reduce_scatter | solution.py:79
  382.5 133.7 %all-reduce.2.cloned.1.call-done = f32[512,512]{1,0:T(8,128)} async-done(((f32[512,512]{1,0:T(8,128)}), f32[512,512]{1,0:T(8,128)}) %all-reduce.2.cloned.1.call-update) | async-done | bytes 1048592 | tf_op jit(solution)/shard_map/psum | solution.py:69
  (87 shorter events, 80.5 us)
Async XLA Ops:
  7.2 203.4 %copy-start = (bf16[512,512]{1,0:T(8,128)(2,1)S(1)}, bf16[512,512]{1,0:T(8,128)(2,1)}, u32[]{:S(2)}) copy-start(bf16[512,512]{1,0:T(8,128)(2,1)} %param.11) | copy-start | bytes 1572868
  7.2 22.0 %all-gather.3.cloned.1.call-start = ((), (), s32[]{:S(2)}) async-start(), calls=%async_computation.2 | async-start | bytes 1310720 | tf_op jit(solution)/shard_map/all_gather | solution.py:54
  7.9 202.7 %reduce-scatter.3.cloned.1.call-start = ((), (), s32[]{:S(2)}) async-start(), calls=%async_computation.3 | async-start | bytes 4718592 | tf_op jit(solution)/shard_map/reduce_scatter | solution.py:61
  122.3 91.3 %copy-start.4 = (bf16[256,512]{1,0:T(8,128)(2,1)S(1)}, bf16[256,512]{1,0:T(8,128)(2,1)}, u32[]{:S(2)}) copy-start(bf16[256,512]{1,0:T(8,128)(2,1)} %param.15) | copy-start | bytes 786436
  122.3 141.5 %all-gather.5.cloned.1.call-start = ((), (), s32[]{:S(2)}) async-start(), calls=%async_computation.5 | async-start | bytes 2359296 | tf_op jit(solution)/shard_map/all_gather | solution.py:73
  212.8 0.8 copy-start.3
  214.6 166.1 %reduce-scatter.5.cloned.1.call-start = ((), (), s32[]{:S(2)}) async-start(), calls=%async_computation.6 | async-start | bytes 2621440 | tf_op jit(solution)/shard_map/reduce_scatter | solution.py:79
  264.1 86.6 %copy-start.2 = (f32[256,512]{1,0:T(8,128)S(1)}, f32[256,512]{1,0:T(8,128)}, u32[]{:S(2)}) copy-start(f32[256,512]{1,0:T(8,128)} %reduce-scatter.3.cloned.1.call-done) | copy-start | bytes 1572868
  349.2 1.3 copy-start.1
  350.6 165.6 %all-reduce.2.cloned.1.call-start = ((), (), s32[]{:S(2)}) async-start(), calls=%async_computation.4 | async-start | bytes 2097152 | tf_op jit(solution)/shard_map/psum | solution.py:69
Sparse Core Ops, SparseCore 0:
  9.6 19.5 all-gather.2
  122.4 88.1 reduce-scatter.2
  214.8 49.0 all-gather.4
  350.7 29.9 reduce-scatter.4
  386.3 129.8 all-reduce.1
where the time goes:
time: 527 us; the launch traced here: 525 us
  waiting for transfers between devices  314 us (60%)
  other arithmetic  95.8 us (18%)
  matrix products  54.1 us (10%)
  local copies, waits for them, and re-layouts  45.8 us (9%)
  between operations  14.5 us (3%)
    psum x1, waiting for transfers between devices, body(): grad_weight = lax.psum(weight_term, ('row', 'col'))  134 us
    scatter-add x12, other arithmetic, one_turn(): return (totals.at[placed].add(product), None)  93.8 us
    reduce_scatter x1, waiting for transfers between devices, body(): lax.psum_scatter(partial_value, 'col', scatter_dimension=0, tiled=True)  88.2 us
    all_gather x1, waiting for transfers between devices, body(): block_grads = lax.all_gather(grad_agg, 'col', axis=0, tiled=True)  44.5 us
    gather x12, local copies, waits for them, and re-layouts, one_turn(): gathered_rows = source_tiles[picked]  32.9 us
    reduce_scatter x1, waiting for transfers between devices, body(): lax.psum_scatter(back, 'row', scatter_dimension=1, tiled=True)  27.6 us
    dot_general x6, matrix products, one_turn(): jnp.einsum('tab,tak->tbk', block_tiles, gathered_rows, preferred_element_...  26.4 us
    dot_general x6, matrix products, one_turn(): jnp.einsum('tab,tbk->tak', block_tiles, gathered_rows, preferred_element_...  22 us
  transfers between devices with their start and end apart: 5, of which 5 were waited for; matrix products, arithmetic and copies ran while one was open for 2% of the time, Pallas kernels for 0%

commit v1 on v0

v1 whole, which is shorter than its diff:
```python
import functools
import math

import jax
import jax.numpy as jnp
from jax import lax
from jax.experimental import pallas as pl
from jax.experimental.pallas import tpu as pltpu
from jax.sharding import PartitionSpec as P

F32 = jnp.float32
BF16 = jnp.bfloat16
MIB = 1024 * 1024
COST, COST_S, COST_W, COST_M = 4_000_000_000, 1_000_000_000, 4_000_000_000, 4_000_000_000
SMEM = pl.BlockSpec(memory_space=pltpu.SMEM)
VMEM = pl.BlockSpec(memory_space=pltpu.VMEM)
ANYWHERE = pl.BlockSpec(memory_space=pl.ANY)


def call(kernel, out_shape, in_specs, operands, scratch=(), limit=16, before=(), cost=0):
    many = isinstance(out_shape, (tuple, list))
    count = len(operands)

    def run(*refs):
        kernel(*refs[:count], *refs[count + len(before) :])

    return pl.pallas_call(
        run,
        out_shape=tuple(out_shape) if many else out_shape,
        in_specs=list(in_specs) + [ANYWHERE] * len(before),
        out_specs=(VMEM,) * len(out_shape) if many else VMEM,
        scratch_shapes=list(scratch),
        compiler_params=pltpu.CompilerParams(vmem_limit_bytes=limit * MIB),
        cost_estimate=pl.CostEstimate(flops=cost, bytes_accessed=0, transcendentals=0),
    )(*operands, *before)


def place_tiles(
    outer,
    shard_tiles,
    count_ref,
    me_ref,
    coords_hbm,
    tiles_ref,
    features_hbm,
    near_ref,
    far_ref,
    features_ref,
    away_ref,
    coords_ref,
    tile_sem,
    in_sems,
):
    slots, tile, _ = tiles_ref.shape
    coords_copy = pltpu.make_async_copy(coords_hbm, coords_ref, in_sems.at[0])
    features_copy = pltpu.make_async_copy(features_hbm, features_ref, in_sems.at[1])
    coords_copy.start()
    features_copy.start()
    me = me_ref[0]
    count = count_ref[0]
    near_ref[...] = jnp.zeros_like(near_ref)
    far_ref[...] = jnp.zeros_like(far_ref)
    coords_copy.wait()
    shift = shard_tiles.bit_length() - 1

    def start(t, carry):
        dest = coords_ref[0, t]
        rel = lax.shift_right_logical(dest, shift) ^ me
        place, bit = 0, 2
        while bit <= outer:
            moved = (outer // bit).bit_length() - bit.bit_length()
            taken = rel & bit
            place = place | (
                lax.shift_left(taken, moved) if moved >= 0 else lax.shift_right_logical(taken, -moved)
            )
            bit *= 2
        row = lax.shift_left(place, shift) | (dest & (shard_tiles - 1))
        rows = pl.ds(pl.multiple_of(row * tile, tile), tile)
        cols = pl.ds(pl.multiple_of(coords_ref[1, t] * tile, tile), tile)

        @pl.when((rel & 1) == 0)
        def _():
            pltpu.make_async_copy(tiles_ref.at[t], near_ref.at[rows, cols], tile_sem).start()

        @pl.when((rel & 1) != 0)
        def _():
            pltpu.make_async_copy(tiles_ref.at[t], far_ref.at[rows, cols], tile_sem).start()

        return carry

    lax.fori_loop(0, count, start, 0)
    some = 1
    while some <= slots:

        @pl.when((count & some) != 0)
        def _():
            part = tiles_ref.at[pl.ds(0, some)]
            pltpu.make_async_copy(part, part, tile_sem).wait()

        some *= 2
    features_copy.wait()
    step = math.gcd(far_ref.shape[0], 256)
    for row in range(0, far_ref.shape[0], step):
        rows = pl.ds(row, step)
        away = jnp.dot(far_ref[rows, :], features_ref[...], preferred_element_type=F32)
        away_ref[rows, :] = away.astype(away_ref.dtype)


def dense_blocks(tiles, coords, count, me, features, outer, shard_rows, limit):
    slots, tile, _ = tiles.shape
    block_c, width = features.shape
    half_rows = outer * shard_rows
    return call(
        functools.partial(place_tiles, outer, shard_rows // tile),
        (
            jax.ShapeDtypeStruct((half_rows, block_c), tiles.dtype),
            jax.ShapeDtypeStruct((half_rows, block_c), tiles.dtype),
            jax.ShapeDtypeStruct(features.shape, BF16),
            jax.ShapeDtypeStruct((half_rows, width), BF16),
        ),
        [SMEM, SMEM, ANYWHERE, pl.BlockSpec(memory_space=pltpu.HBM), ANYWHERE],
        (count, me, coords, tiles, features),
        [
            pltpu.SMEM(coords.shape, jnp.int32),
            pltpu.SemaphoreType.DMA,
            pltpu.SemaphoreType.DMA((2,)),
        ],
        limit,
    )


def copy_whole(in_ref, out_ref):
    out_ref[...] = in_ref[...]


def products(unit, near_ref, far_ref, *refs):
    chunk_refs, away_refs, kept_refs = refs[:4], refs[4:6], refs[6:9]
    last_keep_ref, last_send_ref, all_ref = refs[9:]
    width = chunk_refs[0].shape[1]
    for i, chunk in enumerate(chunk_refs):
        all_ref[:, i * width : (i + 1) * width] = chunk[...]
    half_rows = near_ref.shape[0]
    step = math.gcd(unit, 256)

    def put_last(block, row, values):
        shard = row // unit
        rows = pl.ds(shard // 2 * unit + row % unit, step)
        if shard % 2 == 0:
            last_keep_ref[block, rows, :] = values
        else:
            last_send_ref[block, rows, :] = values.astype(last_send_ref.dtype)

    for row in range(0, half_rows, step):
        rows = pl.ds(row, step)
        away = jnp.dot(far_ref[rows, :], all_ref[:, width:], preferred_element_type=F32)
        for i, out in enumerate(away_refs):
            out[rows, :] = away[:, i * width : (i + 1) * width].astype(out.dtype)
        put_last(1, row, away[:, 2 * width :])
    for row in range(0, half_rows, step):
        rows = pl.ds(row, step)
        kept = jnp.dot(near_ref[rows, :], all_ref[...], preferred_element_type=F32)
        for i, out in enumerate(kept_refs):
            out[rows, :] = kept[:, i * width : (i + 1) * width]
        put_last(0, row, kept[:, 3 * width :])


def all_products(near, far, features, unit, limit):
    half_rows, block_c = near.shape
    width = features[0].shape[1]
    away = jax.ShapeDtypeStruct((half_rows, width), BF16)
    kept = jax.ShapeDtypeStruct((half_rows, width), F32)
    last = (2, half_rows // 2, width)
    outs = call(
        functools.partial(products, unit),
        [away] * 2 + [kept] * 3 + [jax.ShapeDtypeStruct(last, F32), jax.ShapeDtypeStruct(last, BF16)],
        [VMEM] * 6,
        (near, far, *features),
        [pltpu.VMEM((block_c, 4 * width), BF16)],
        limit,
    )
    return outs[:2], outs[2:5], outs[5], outs[6]


def add_and_halve(unit, kept_ref, came_ref, keep_ref, send_ref):
    rows = keep_ref.shape[-2]
    first, second = pl.ds(0, rows), pl.ds(rows, rows)
    if len(kept_ref.shape) == 2:
        keep_ref[...] = kept_ref[first, :] + came_ref[first, :].astype(F32)
        send_ref[...] = (kept_ref[second, :] + came_ref[second, :].astype(F32)).astype(send_ref.dtype)
        return
    for i in range(kept_ref.shape[0]):
        for j in range(rows // unit):
            here = pl.ds(j * unit, unit)
            even, odd = pl.ds(2 * j * unit, unit), pl.ds((2 * j + 1) * unit, unit)
            keep_ref[i, here, :] = kept_ref[i, even, :] + came_ref[i, even, :].astype(F32)
            total = kept_ref[i, odd, :] + came_ref[i, odd, :].astype(F32)
            send_ref[i, here, :] = total.astype(send_ref.dtype)


def halved(kept, came, unit, before):
    shape = kept.shape[:-2] + (kept.shape[-2] // 2, kept.shape[-1])
    return call(
        functools.partial(add_and_halve, unit),
        (jax.ShapeDtypeStruct(shape, F32), jax.ShapeDtypeStruct(shape, BF16)),
        [VMEM] * 2,
        (kept, came),
        before=before,
    )


def add_and_part(kept_ref, came_ref, keep_ref, *send_refs):
    rows = keep_ref.shape[0]
    keep_ref[...] = kept_ref[:rows, :] + came_ref[:rows, :].astype(F32)
    for i, out in enumerate(send_refs):
        part = pl.ds((i + 1) * rows, rows)
        out[...] = (kept_ref[part, :] + came_ref[part, :].astype(F32)).astype(out.dtype)


def parted(kept, came, count, before):
    shape = (kept.shape[0] // count, kept.shape[1])
    outs = call(
        add_and_part,
        [jax.ShapeDtypeStruct(shape, F32)] + [jax.ShapeDtypeStruct(shape, BF16)] * (count - 1),
        [VMEM] * 2,
        (kept, came),
        before=before,
    )
    return outs[0], outs[1:]


def add_pair(kept_ref, came_ref, keep_ref, send_ref):
    keep_ref[...] = kept_ref[0] + came_ref[0].astype(F32)
    send_ref[...] = (kept_ref[1] + came_ref[1].astype(F32)).astype(send_ref.dtype)


def join_two(first_ref, second_ref, out_ref):
    out_ref[pl.ds(0, first_ref.shape[0])] = first_ref[...]
    out_ref[pl.ds(first_ref.shape[0], first_ref.shape[0])] = second_ref[...]


def joined(first, second, before, cost=0):
    shape = (2 * first.shape[0],) + first.shape[1:]
    return call(
        join_two,
        jax.ShapeDtypeStruct(shape, first.dtype),
        [VMEM] * 2,
        (first, second),
        before=before,
        cost=cost,
    )


def mark(out_ref):
    out_ref[...] = jnp.zeros_like(out_ref)


def marked(*before, cost=0):
    return call(mark, jax.ShapeDtypeStruct((8, 128), F32), [], (), before=before, cost=cost)


def order_rows(owners, me_ref, weight_ref, out_ref):
    part = weight_ref.shape[0] // len(owners)
    for i, rels in enumerate(owners):
        piece = part // len(rels)
        for j, rel in enumerate(rels):
            source = pl.ds(pl.multiple_of((me_ref[0] ^ rel) * piece, piece), piece)
            out_ref[pl.ds(i * part + j * piece, piece), :] = weight_ref[source, :]


def dense_layer(counts, out_groups, *refs):
    total_refs, refs = refs[: sum(counts)], refs[sum(counts) :]
    rows_ref, cotangent_ref, hidden_ref, agg_ref, grad_pre_ref = refs[:5]
    grad_refs = refs[5:]
    part = rows_ref.shape[0] // len(counts)
    at = 0
    for i, count in enumerate(counts):
        total = total_refs[at][...]
        for ref in total_refs[at + 1 : at + count]:
            total = total + ref[...].astype(F32)
        agg_ref[:, i * part : (i + 1) * part] = total.astype(agg_ref.dtype)
        at += count
    pre_act = jnp.dot(agg_ref[...], rows_ref[...], preferred_element_type=F32)
    slope = jnp.exp(jnp.minimum(pre_act, 0.0))
    positive = pre_act > 0
    hidden_ref[...] = jnp.where(positive, pre_act, slope - 1.0).astype(hidden_ref.dtype)
    slope = jnp.where(positive, F32(1.0), slope)
    grad_pre = (cotangent_ref[...].astype(F32) * slope).astype(grad_pre_ref.dtype)
    grad_pre_ref[...] = grad_pre
    for members, out in zip(out_groups, grad_refs):
        for j, i in enumerate(members):
            out[0, pl.ds(j * part, part), :] = lax.dot_general(
                rows_ref[pl.ds(i * part, part), :],
                grad_pre,
                (((1,), (1,)), ((), ())),
                preferred_element_type=F32,
            ).astype(out.dtype)


def layer(totals, out_groups, weight_rows, cotangent, before):
    shard_rows, width = cotangent.shape
    part = width // len(totals)
    whole = jax.ShapeDtypeStruct((shard_rows, width), BF16)
    grads = [jax.ShapeDtypeStruct((1, len(m) * part, shard_rows), BF16) for m in out_groups]
    counts = [len(terms) for terms in totals]
    outs = call(
        functools.partial(dense_layer, counts, out_groups),
        [whole] * 3 + grads,
        [VMEM] * (sum(counts) + 2),
        (*[term for terms in totals for term in terms], weight_rows, cotangent),
        before=before,
    )
    return outs[0], outs[1], outs[2], outs[3:]


def back_products(count, near_ref, far_ref, *refs):
    rows_refs, out_refs, (left_ref, right_ref) = refs[:count], refs[count:-2], refs[-2:]
    shard_rows = rows_refs[0].shape[2]
    for k in range(left_ref.shape[1] // shard_rows):
        cols = pl.ds(k * shard_rows, shard_rows)
        if count == 2:
            left_ref[:, cols] = rows_refs[0][k]
            right_ref[:, cols] = rows_refs[1][k]
        else:
            left_ref[:, cols] = rows_refs[0][2 * k]
            right_ref[:, cols] = rows_refs[0][2 * k + 1]
    block_c = near_ref.shape[1]
    step = math.gcd(block_c, 256)
    part = out_refs[0].shape[0]
    for col in range(0, block_c, step):
        cols = pl.ds(col, step)
        total = jnp.dot(left_ref[...], near_ref[:, cols], preferred_element_type=F32)
        total = total + jnp.dot(right_ref[...], far_ref[:, cols], preferred_element_type=F32)
        for i, out in enumerate(out_refs):
            out[:, cols] = total[i * part : (i + 1) * part, :].astype(out.dtype)


def back_of(near, far, rows, dtypes, limit, before, cost=0):
    height = rows[0].shape[1]
    shape = (height // len(dtypes), near.shape[1])
    return call(
        functools.partial(back_products, len(rows)),
        [jax.ShapeDtypeStruct(shape, dtype) for dtype in dtypes],
        [VMEM] * (2 + len(rows)),
        (near, far, *rows),
        [pltpu.VMEM((height, near.shape[0]), BF16)] * 2,
        limit,
        before=before,
        cost=cost,
    )


def add_parts(places, own_ref, came_ref, *out_refs):
    piece = out_refs[0].shape[0]
    for place, out in zip(places, out_refs):
        rows = pl.ds(place * piece, piece)
        out[...] = (own_ref[rows, :] + came_ref[rows, :].astype(F32)).astype(out.dtype)


def parts_to_send(own, came, places, piece, before):
    shape = jax.ShapeDtypeStruct((piece, own.shape[1]), BF16)
    return call(
        functools.partial(add_parts, places),
        [shape] * len(places),
        [VMEM] * 2,
        (own, came),
        before=before,
    )


def finish(own_ref, came_ref, *refs):
    out_ref = refs[-1]
    piece = out_ref.shape[1]
    total = own_ref[:piece, :] + came_ref[:piece, :].astype(F32)
    for ref in refs[:-1]:
        total = total + ref[...].astype(F32)
    out_ref[...] = total.T.astype(out_ref.dtype)


def weight_terms(places, agg_ref, grad_pre_ref, *out_refs):
    width = agg_ref.shape[1]
    piece = width // sum(len(group) for group in places)
    for group, out in zip(places, out_refs):
        for i, place in enumerate(group):
            term = lax.dot_general(
                agg_ref[:, place * piece : (place + 1) * piece],
                grad_pre_ref[...],
                (((0,), (0,)), ((), ())),
                preferred_element_type=F32,
            )
            out[pl.ds(i * piece, piece), :] = term.astype(out.dtype)


def add_and_split(side_ref, kept_ref, came_ref, keep_ref, send_ref, total_ref):
    total_ref[...] = kept_ref[...] + came_ref[...]
    half = keep_ref.shape[1]
    side = side_ref[0] & 1
    for k in range(keep_ref.shape[0]):
        mine = pl.ds(pl.multiple_of((2 * k + side) * half, half), half)
        other = pl.ds(pl.multiple_of((2 * k + 1 - side) * half, half), half)
        keep_ref[k] = total_ref[mine, :]
        send_ref[k] = total_ref[other, :].astype(send_ref.dtype)


def add_and_spread(kept_ref, came_ref, keep_ref, *send_refs):
    keep_ref[...] = kept_ref[0] + came_ref[0].astype(F32)
    for k, out in enumerate(send_refs):
        out[...] = (kept_ref[k + 1] + came_ref[k + 1].astype(F32)).astype(out.dtype)


def add_all(*refs):
    terms = [ref[...].astype(F32) for ref in refs[:-1]]
    while len(terms) > 1:
        terms = [sum(terms[i + 1 : i + 2], terms[i]) for i in range(0, len(terms), 2)]
    refs[-1][...] = terms[0].astype(refs[-1].dtype)


def sum_of(terms, dtype, before, cost=0):
    return call(
        add_all,
        jax.ShapeDtypeStruct(terms[0].shape, dtype),
        [VMEM] * len(terms),
        tuple(terms),
        before=before,
        cost=cost,
    )


def stack_all(*refs):
    for i, ref in enumerate(refs[:-1]):
        refs[-1][i] = ref[...]


def place_shares(me_ref, side_ref, own_ref, other_ref, out_ref):
    half = own_ref.shape[2]
    for inner, ref in ((0, own_ref), (1, other_ref)):
        for turn in range(2):
            side = (side_ref[0] ^ turn) & 1
            for k in range(ref.shape[1]):
                place = (me_ref[0] ^ (2 * k + inner)) * 2 + side
                out_ref[pl.ds(pl.multiple_of(place * half, half), half), :] = ref[turn, k].astype(
                    out_ref.dtype
                )


def body(node_features, layer_weight, tile_values, tile_coords, tile_count, cotangent):
    n_row = lax.axis_size("row")
    n_col = lax.axis_size("col")
    ro, co = n_row // 2, n_col // 2
    my_row = lax.axis_index("row").astype(jnp.int32).reshape(1)
    my_col = lax.axis_index("col").astype(jnp.int32).reshape(1)
    shard_rows, width = cotangent.shape
    block_c, piece = node_features.shape
    limit = 12 + (4 * co * shard_rows * block_c) // MIB

    def swap(v, axis, bit):
        size = n_row if axis == "row" else n_col
        return lax.ppermute(v, axis, [(i, i ^ bit) for i in range(size)])

    halves = (range(0, ro // 2), range(ro // 2, ro))
    chunks = [(h, i) for h in range(2) for i in range(2)]
    owners = [[2 * k + i for k in halves[h]] for h, i in chunks]
    flat = [rel for rels in owners for rel in rels]

    features = []
    for h, inner in chunks:
        if inner == 0:
            parts = [swap(node_features, "row", 2 * k) if k else node_features for k in halves[h]]
            features.append(jnp.concatenate(parts, axis=1) if len(parts) > 1 else parts[0])
        else:
            features.append(None)
    features[1] = swap(features[0], "row", 1)
    near, far, own_features, first_away = dense_blocks(
        tile_values[0, 0],
        pltpu.with_memory_space_constraint(tile_coords[0, 0].T, pltpu.HBM),
        tile_count.reshape(-1),
        my_col,
        pltpu.with_memory_space_constraint(features[0], pltpu.HBM),
        co,
        shard_rows,
        max(limit, 48),
    )
    held = call(
        copy_whole,
        jax.ShapeDtypeStruct(features[2].shape, BF16),
        [VMEM],
        (features[2],),
        before=(first_away,),
    )
    features[3] = swap(held, "row", 1)
    features[0] = own_features
    away, kept, last_keep, last_send = all_products(near, far, features, shard_rows, limit)

    stages = co.bit_length() - 1
    reversed_bits = [sum(((p >> i) & 1) << (stages - 1 - i) for i in range(stages)) for p in range(co)]
    keeps = [*kept, last_keep]
    cames = [swap(v, "col", 1) for v in (first_away, *away)] + [swap(last_send, "col", n_col // 2)]
    totals = [None] * 4
    done = [0, 0, 0, 1]
    turns = [0, 1, 0, 3, 2, 1, 3] if stages == 2 else ([0, 1, 3] * stages + [2])
    weight_rows = call(
        functools.partial(order_rows, owners),
        jax.ShapeDtypeStruct(layer_weight.shape, BF16),
        [SMEM, VMEM],
        (my_row, layer_weight),
        before=(last_keep,),
    )
    last = weight_rows
    for i in turns:
        before = [last]
        if stages == 2 and i == 3 and done[3] == 1:
            before.append(cames[0])
        if i == 2:
            own, sends = parted(keeps[2], cames[2], co, before)
            last = sends[0]
            totals[2] = [own] + [
                swap(send, "col", 2 * reversed_bits[p + 1]) for p, send in enumerate(sends)
            ]
        elif i == 3 and done[3] == stages:
            shape = keeps[3].shape[1:]
            own, last = call(
                add_pair,
                (jax.ShapeDtypeStruct(shape, F32), jax.ShapeDtypeStruct(shape, BF16)),
                [VMEM] * 2,
                (keeps[3], cames[3]),
                before=before,
            )
            totals[3] = [own, swap(last, "col", 1)]
        else:
            keeps[i], last = halved(keeps[i], cames[i], shard_rows, before)
            done[i] += 1
            cames[i] = swap(last, "col", 1 << done[i] if i < 3 else n_col >> done[i])
            totals[i] = [keeps[i], cames[i]]

    out_groups = ((3,), (2,), (1, 0))
    hidden, agg, grad_pre, grads = layer(
        totals, out_groups, weight_rows, cotangent, (marked(last, cames[1]),)
    )

    places = [[flat.index(2 * k + inner) for k in range(ro)] for inner in range(2)]
    term_shape = (width // 2, width)
    weight_kept, weight_send = call(
        functools.partial(weight_terms, places),
        (jax.ShapeDtypeStruct(term_shape, F32), jax.ShapeDtypeStruct(term_shape, F32)),
        [VMEM] * 2,
        (agg, grad_pre),
    )
    state = {"w": [weight_kept, swap(weight_send, "row", 1)], "last": weight_send}

    def order(*more):
        return [state["last"], *more]

    half_share = (ro, piece // 2, width)

    def weight_core():
        keep, send = call(
            add_and_split,
            (jax.ShapeDtypeStruct(half_share, F32), jax.ShapeDtypeStruct(half_share, BF16)),
            [SMEM, VMEM, VMEM],
            (my_col, *state["w"]),
            [pltpu.VMEM((ro * piece, width), F32)],
            before=order(),
        )
        state["last"] = send
        state["w"] = [keep, swap(send, "col", 1)]

    def weight_side():
        shape = half_share[1:]
        outs = call(
            add_and_spread,
            [jax.ShapeDtypeStruct(shape, F32)] + [jax.ShapeDtypeStruct(shape, BF16)] * (ro - 1),
            [VMEM] * 2,
            tuple(state["w"]),
            before=order(),
        )
        state["last"] = outs[0]
        state["w"] = [outs[0]] + [swap(v, "row", 2 * (k + 1)) for k, v in enumerate(outs[1:])]

    def weight_line():
        total = sum_of(state["w"], BF16, order())
        state["last"] = total
        state["w"] = [total] + [swap(total, "col", 2 * k) for k in range(1, co)]

    def weight_sum():
        total = sum_of(state["w"], BF16, order(), COST_W)
        state["last"] = total
        state["w"] = [total] + [swap(total, "row", 2 * k) for k in range(1, ro)]

    def weight_stack(axis):
        total = call(
            stack_all,
            jax.ShapeDtypeStruct((len(state["w"]),) + state["w"][0].shape, BF16),
            [VMEM] * len(state["w"]),
            tuple(state["w"]),
            before=order(),
        )
        state["last"] = total
        state["w"] = [total, swap(total, axis, 1)]

    rows = {"C": grads[0], "A": grads[1], "M": grads[2]}
    bits = {"C": n_col // 2, "A": 1, "M": n_col // 2}
    came_rows = {name: swap(rows[name], "col", bits[name]) for name in rows}
    backs = {}

    def join(name, cost=0):
        first, second = rows[name], came_rows[name]
        bit = n_col // 2 if name == "A" and bits[name] == 1 else bits[name] // 2
        bits[name] = bit
        rows[name] = state["last"] = joined(first, second, order(), cost)
        if not (name == "A" and bit == 1):
            came_rows[name] = swap(rows[name], "col", bit)

    def back(members, pair, cost=0, more=()):
        dtypes = [BF16 if chunk[1] else F32 for chunk in members]
        outs = back_of(near, far, pair, dtypes, limit, order(*more), cost)
        state["last"] = outs[0]
        for chunk, out in zip(members, outs):
            backs[chunk] = swap(out, "row", 1) if chunk[1] else out

    arrived = []

    def send_parts(h):
        sent = [p for p, k in enumerate(halves[h]) if k > 0]
        if sent:
            parts = parts_to_send(backs[h, 0], backs[h, 1], sent, piece, order())
            state["last"] = parts[0]
            arrived.extend(swap(v, "row", 2 * halves[h][p]) for p, v in zip(sent, parts))

    weight_core()
    join("A")
    join("C")
    weight_side()
    join("M")
    for _ in range(stages - 1):
        join("C")
    weight_line()
    for _ in range(stages - 1):
        join("A", COST)
    back([(1, 1)], (rows["C"], came_rows["C"]))
    for _ in range(stages - 1):
        join("M")
    weight_sum()
    weight_stack("col")
    join("A", COST_S)
    back([(1, 0)], (rows["A"],))
    send_parts(1)
    back([(0, 1), (0, 0)], (rows["M"], came_rows["M"]), COST_M)
    weight_stack("row")
    send_parts(0)
    state["last"] = marked(state["last"], *arrived, cost=COST)
    grad_features = call(
        finish,
        jax.ShapeDtypeStruct((block_c, piece), BF16),
        [VMEM] * (2 + len(arrived)),
        (backs[0, 0], backs[0, 1], *arrived),
        before=order(),
    )
    grad_weight = call(
        place_shares,
        jax.ShapeDtypeStruct((width, width), F32),
        [SMEM, SMEM, VMEM, VMEM],
        (my_row, my_col, *state["w"]),
    )
    return (hidden, grad_weight, grad_features)


def solution(mesh):
    in_specs = (
        P("col", "row"),
        P(),
        P("row", "col", None, None, None),
        P("row", "col", None, None),
        P("row", "col"),
        P(("row", "col"), None),
    )
    out_specs = (P(("row", "col"), None), P(), P("col", "row"))
    return jax.shard_map(body, mesh=mesh, in_specs=in_specs, out_specs=out_specs, check_vma=False)
```

time: 527 us -> 101 us (0.19)
  waiting for transfers between devices: 314 us -> 36.1 us
  other arithmetic: 95.8 us -> 0 us
  matrix products: 54.1 us -> 0 us
  starting transfers between devices: 0.2 us -> 40.3 us
  local copies, waits for them, and re-layouts: 45.8 us -> 6.14 us
  Pallas kernels: 0 us -> 16.4 us
  between operations: 14.5 us -> 1.6 us
    psum x1 -> x0, waiting for transfers between devices: 134 us -> none  [body(): grad_weight = lax.psum(weight_term, ('row', 'col'))]
    reduce_scatter x2 -> x0, waiting for transfers between devices: 116 us -> none  [the longest x1 88.2 us: body(): lax.psum_scatter(partial_value, 'col', scatter_dimension=0, tiled=True)]
    scatter-add x12 -> x0, other arithmetic: 93.8 us -> none  [one_turn(): return (totals.at[placed].add(product), None)]
    all_gather x2 -> x0, waiting for transfers between devices: 64.1 us -> none  [the longest x1 44.5 us: body(): block_grads = lax.all_gather(grad_agg, 'col', axis=0, tiled=True)]
    dot_general x15 -> x0, matrix products: 54.1 us -> none  [the longest x6 26.4 us: one_turn(): jnp.einsum('tab,tak->tbk', block_tiles, gathered_rows, preferred_element_...]
    ppermute x0 -> x37, starting transfers between devices: none -> 40.3 us  [swap(): return lax.ppermute(v, axis, [(i, i ^ bit) for i in range(size)])]
    ppermute x0 -> x37, waiting for transfers between devices: none -> 36.1 us  [swap(): return lax.ppermute(v, axis, [(i, i ^ bit) for i in range(size)])]
    gather x12 -> x0, local copies, waits for them, and re-layouts: 32.9 us -> none  [one_turn(): gathered_rows = source_tiles[picked]]
  transfers between devices with their start and end apart: 5 -> 37, of which waited for: 5 -> 15; matrix products, arithmetic and copies ran while one was open for 2% -> 0% of each run, Pallas kernels for 0% -> 14%
where the time goes in v1:
time: 101 us
  starting transfers between devices  40.3 us (40%)
  waiting for transfers between devices  36.1 us (36%)
  Pallas kernels  16.4 us (16%)
  local copies, waits for them, and re-layouts  6.14 us (6%)
  between operations  1.6 us (2%)
    ppermute x37, starting transfers between devices, swap(): return lax.ppermute(v, axis, [(i, i ^ bit) for i in range(size)])  40.3 us
    ppermute x37, waiting for transfers between devices, swap(): return lax.ppermute(v, axis, [(i, i ^ bit) for i in range(size)])  36.1 us
    pallas_call x34, Pallas kernels, call(): pl.pallas_call(run, out_shape=tuple(out_shape) if many else out_shape, in...  16.4 us
    unnamed x24, local copies, waits for them, and re-layouts  6.14 us
  transfers between devices with their start and end apart: 37, of which 15 were waited for; matrix products, arithmetic and copies ran while one was open for 0% of the time, Pallas kernels for 14%

profile of v1, /device:TPU:0, one launch (start us, length us, event | category | flops | bytes accessed | tf_op | source)
XLA Modules:
  0.0 100.6 jit_solution(13568929279220246421)
XLA Ops:
  0.6 3.0 %collective-permute-start.1 = (bf16[1024,128]{1,0:T(8,128)(2,1)}, bf16[1024,128]{1,0:T(8,128)(2,1)S(1)}, u32[]{:S(2)}, u32[]{:S(2)}) collective-permute-start(bf16[1024,128]{1,0:T(8,128)(2,1)} %refs_4_.1), channel_id=1, source_target_pairs={{0,16},{8,24},{16,0},{24,8},{1,17},{9,25},{17,1},{25,9},{2,18},{10... | collective-permute-start | bytes 786440 | tf_op jit(solution)/shard_map/ppermute | solution.py:457
  4.3 4.3 %shard_map.85 = (bf16[1024,1024]{1,0:T(8,128)(2,1)S(1)}, bf16[1024,1024]{1,0:T(8,128)(2,1)S(1)}, bf16[1024,128]{1,0:T(8,128)(2,1)S(1)}, bf16[1024,128]{1,0:T(8,128)(2,1)}) custom-call(s32[1]{0:T(128)} %bitcast.7.refs_0_, s32[1]{0:T(128)} %bitcast.1.refs_1_.refs_0_, s32[2,96]{1,0:T(2,128)} %bitcast.9, bf16[96,128,128]{2,1,0:T(8,128)(2,1)} %bitcast.8, ...), custom_call_target="tpu_custom_call" | custom-call | tf_op jit(solution)/shard_map/pallas_call | solution.py:27
  8.7 1.5 %collective-permute-done.1.refs_0_.refs_4_ = bf16[1024,128]{1,0:T(8,128)(2,1)S(1)} collective-permute-done((bf16[1024,128]{1,0:T(8,128)(2,1)}, bf16[1024,128]{1,0:T(8,128)(2,1)S(1)}, u32[]{:S(2)}, u32[]{:S(2)}) %collective-permute-start.1) | collective-permute-done | bytes 262176 | tf_op jit(solution)/shard_map/ppermute | solution.py:457
  10.3 1.8 %collective-permute-start.3 = (bf16[1024,128]{1,0:T(8,128)(2,1)}, bf16[1024,128]{1,0:T(8,128)(2,1)}, u32[]{:S(2)}, u32[]{:S(2)}) collective-permute-start(bf16[1024,128]{1,0:T(8,128)(2,1)} %get-tuple-element.47.refs_1_), channel_id=1, source_target_pairs={{0,1},{1,0},{2,3},{3,2},{4,5},{5,4},{6,7},{7,6},{8,9},{9,8},{10,11... | collective-permute-start | bytes 786440 | tf_op jit(solution)/shard_map/ppermute | solution.py:457
  13.7 3.1 %shard_map.87 = (bf16[1024,128]{1,0:T(8,128)(2,1)}, bf16[1024,128]{1,0:T(8,128)(2,1)S(1)}, f32[1024,128]{1,0:T(8,128)S(1)}, f32[1024,128]{1,0:T(8,128)S(1)}, f32...) custom-call(bf16[1024,1024]{1,0:T(8,128)(2,1)S(1)} %get-tuple-element.44.refs_0_, ...), custom_call_target="tpu_custom_call" | custom-call | tf_op jit(solution)/shard_map/pallas_call | solution.py:27
  19.9 2.6 %collective-permute-start.9 = (bf16[2,512,128]{2,1,0:T(8,128)(2,1)}, bf16[2,512,128]{2,1,0:T(8,128)(2,1)S(1)}, u32[]{:S(2)}, u32[]{:S(2)}) collective-permute-start(bf16[2,512,128]{2,1,0:T(8,128)(2,1)} %get-tuple-element.60), channel_id=1, source_target_pairs={{0,4},{1,5},{2,6},{3,7},{4,0},{5,1},{6,2},{7,3},{8,12},{9,13},{10,... | collective-permute-start | bytes 786440 | tf_op jit(solution)/shard_map/ppermute | solution.py:457
  25.7 1.6 %collective-permute-start.4 = (bf16[512,128]{1,0:T(8,128)(2,1)S(1)}, bf16[512,128]{1,0:T(8,128)(2,1)S(1)}, u32[]{:S(2)}, u32[]{:S(2)}) collective-permute-start(bf16[512,128]{1,0:T(8,128)(2,1)S(1)} %get-tuple-element.51.refs_2_), channel_id=1, source_target_pairs={{0,2},{1,3},{2,0},{3,1},{4,6},{5,7},{6,4},{7,5},{8,10},{9,11},{10,... | collective-permute-start | bytes 393224 | tf_op jit(solution)/shard_map/ppermute | solution.py:457
  29.7 6.7 %collective-permute-done.4.refs_1_ = bf16[512,128]{1,0:T(8,128)(2,1)S(1)} collective-permute-done((bf16[512,128]{1,0:T(8,128)(2,1)S(1)}, bf16[512,128]{1,0:T(8,128)(2,1)S(1)}, u32[]{:S(2)}, u32[]{:S(2)}) %collective-permute-start.4) | collective-permute-done | bytes 131104 | tf_op jit(solution)/shard_map/ppermute | solution.py:457
  36.6 5.7 %collective-permute-done.6.refs_3_.refs_1_ = bf16[256,128]{1,0:T(8,128)(2,1)S(1)} collective-permute-done((bf16[256,128]{1,0:T(8,128)(2,1)S(1)}, bf16[256,128]{1,0:T(8,128)(2,1)S(1)}, u32[]{:S(2)}, u32[]{:S(2)}) %collective-permute-start.6) | collective-permute-done | bytes 65568 | tf_op jit(solution)/shard_map/ppermute | solution.py:457
  42.5 2.1 %collective-permute-start.12 = (bf16[256,128]{1,0:T(8,128)(2,1)S(1)}, bf16[256,128]{1,0:T(8,128)(2,1)S(1)}, u32[]{:S(2)}, u32[]{:S(2)}) collective-permute-start(bf16[256,128]{1,0:T(8,128)(2,1)S(1)} %get-tuple-element.66), channel_id=1, source_target_pairs={{0,2},{1,3},{2,0},{3,1},{4,6},{5,7},{6,4},{7,5},{8,10},{9,11},{10,... | collective-permute-start | bytes 196616 | tf_op jit(solution)/shard_map/ppermute | solution.py:457
  44.6 1.5 %collective-permute-start.11 = (bf16[256,128]{1,0:T(8,128)(2,1)S(1)}, bf16[256,128]{1,0:T(8,128)(2,1)S(1)}, u32[]{:S(2)}, u32[]{:S(2)}) collective-permute-start(bf16[256,128]{1,0:T(8,128)(2,1)S(1)} %get-tuple-element.62.refs_2_), channel_id=1, source_target_pairs={{0,4},{1,5},{2,6},{3,7},{4,0},{5,1},{6,2},{7,3},{8,12},{9,13},{10,... | collective-permute-start | bytes 196616 | tf_op jit(solution)/shard_map/ppermute | solution.py:457
  49.5 2.5 %collective-permute-done.10.refs_1_.refs_3_ = bf16[256,128]{1,0:T(8,128)(2,1)S(1)} collective-permute-done((bf16[256,128]{1,0:T(8,128)(2,1)S(1)}, bf16[256,128]{1,0:T(8,128)(2,1)S(1)}, u32[]{:S(2)}, u32[]{:S(2)}) %collective-permute-start.10) | collective-permute-done | bytes 65568 | tf_op jit(solution)/shard_map/ppermute | solution.py:457
  57.7 1.8 %collective-permute-start.22 = (bf16[1,256,256]{2,1,0:T(8,128)(2,1)S(1)}, bf16[1,256,256]{2,1,0:T(8,128)(2,1)S(1)}, u32[]{:S(2)}, u32[]{:S(2)}) collective-permute-start(bf16[1,256,256]{2,1,0:T(8,128)(2,1)S(1)} %get-tuple-element.82.refs_0_), channel_id=1, source_target_pairs={{0,4},{1,5},{2,6},{3,7},{4,0},{5,1},{6,2},{7,3},{8,12},{9,13},{10,... | collective-permute-start | bytes 393224 | tf_op jit(solution)/shard_map/ppermute | solution.py:457
  61.1 1.9 %collective-permute-start.21 = (bf16[2,128,256]{2,1,0:T(8,128)(2,1)S(1)}, bf16[2,128,256]{2,1,0:T(8,128)(2,1)S(1)}, u32[]{:S(2)}, u32[]{:S(2)}) collective-permute-start(bf16[2,128,256]{2,1,0:T(8,128)(2,1)S(1)} %shard_map.101.refs_2_.refs_0_), channel_id=1, source_target_pairs={{0,2},{1,3},{2,0},{3,1},{4,6},{5,7},{6,4},{7,5},{8,10},{9,11},{10,... | collective-permute-start | bytes 393224 | tf_op jit(solution)/shard_map/ppermute | solution.py:457
  63.9 1.6 %collective-permute-start.20 = (bf16[64,512]{1,0:T(8,128)(2,1)S(1)}, bf16[64,512]{1,0:T(8,128)(2,1)S(1)}, u32[]{:S(2)}, u32[]{:S(2)}) collective-permute-start(bf16[64,512]{1,0:T(8,128)(2,1)S(1)} %get-tuple-element.81), channel_id=1, source_target_pairs={{0,16},{8,24},{16,0},{24,8},{1,17},{9,25},{17,1},{25,9},{2,18},{10... | collective-permute-start | bytes 196616 | tf_op jit(solution)/shard_map/ppermute | solution.py:457
  65.5 1.9 %collective-permute-done.22.refs_1_ = bf16[1,256,256]{2,1,0:T(8,128)(2,1)S(1)} collective-permute-done((bf16[1,256,256]{2,1,0:T(8,128)(2,1)S(1)}, bf16[1,256,256]{2,1,0:T(8,128)(2,1)S(1)}, u32[]{:S(2)}, u32[]{:S(2)}) %collective-permute-start.22) | collective-permute-done | bytes 131104 | tf_op jit(solution)/shard_map/ppermute | solution.py:457
  69.3 3.2 %collective-permute-start.25 = (bf16[64,512]{1,0:T(8,128)(2,1)S(1)}, bf16[64,512]{1,0:T(8,128)(2,1)S(1)}, u32[]{:S(2)}, u32[]{:S(2)}) collective-permute-start(bf16[64,512]{1,0:T(8,128)(2,1)S(1)} %shard_map.105.refs_2_.refs_0_), channel_id=1, source_target_pairs={{0,6},{1,7},{2,4},{3,5},{4,2},{5,3},{6,0},{7,1},{8,14},{9,15},{10,... | collective-permute-start | bytes 196616 | tf_op jit(solution)/shard_map/ppermute | solution.py:457
  73.8 1.9 %collective-permute-done.27.refs_3_ = bf16[4,128,256]{2,1,0:T(8,128)(2,1)S(1)} collective-permute-done((bf16[4,128,256]{2,1,0:T(8,128)(2,1)S(1)}, bf16[4,128,256]{2,1,0:T(8,128)(2,1)S(1)}, u32[]{:S(2)}, u32[]{:S(2)}) %collective-permute-start.27) | collective-permute-done | bytes 262176 | tf_op jit(solution)/shard_map/ppermute | solution.py:457
  76.7 3.0 %collective-permute-done.26.refs_1_ = bf16[2,256,256]{2,1,0:T(8,128)(2,1)S(1)} collective-permute-done((bf16[2,256,256]{2,1,0:T(8,128)(2,1)S(1)}, bf16[2,256,256]{2,1,0:T(8,128)(2,1)S(1)}, u32[]{:S(2)}, u32[]{:S(2)}) %collective-permute-start.26) | collective-permute-done | bytes 262176 | tf_op jit(solution)/shard_map/ppermute | solution.py:457
  79.8 1.8 %collective-permute-start.31 = (bf16[4,256,256]{2,1,0:T(8,128)(2,1)S(1)}, bf16[4,256,256]{2,1,0:T(8,128)(2,1)S(1)}, u32[]{:S(2)}, u32[]{:S(2)}) collective-permute-start(bf16[4,256,256]{2,1,0:T(8,128)(2,1)S(1)} %shard_map.108.refs_4_.refs_2_), channel_id=1, source_target_pairs={{0,1},{1,0},{2,3},{3,2},{4,5},{5,4},{6,7},{7,6},{8,9},{9,8},{10,11... | collective-permute-start | bytes 1572872 | tf_op jit(solution)/shard_map/ppermute | solution.py:457
  81.7 1.6 %collective-permute-start.29 = (bf16[64,512]{1,0:T(8,128)(2,1)S(1)}, bf16[64,512]{1,0:T(8,128)(2,1)S(1)}, u32[]{:S(2)}, u32[]{:S(2)}) collective-permute-start(bf16[64,512]{1,0:T(8,128)(2,1)S(1)} %shard_map.109.refs_0_.refs_2_), channel_id=1, source_target_pairs={{0,16},{8,24},{16,0},{24,8},{1,17},{9,25},{17,1},{25,9},{2,18},{10... | collective-permute-start | bytes 196616 | tf_op jit(solution)/shard_map/ppermute | solution.py:457
  83.3 2.7 %collective-permute-done.29.refs_1_ = bf16[64,512]{1,0:T(8,128)(2,1)S(1)} collective-permute-done((bf16[64,512]{1,0:T(8,128)(2,1)S(1)}, bf16[64,512]{1,0:T(8,128)(2,1)S(1)}, u32[]{:S(2)}, u32[]{:S(2)}) %collective-permute-start.29) | collective-permute-done | bytes 65568 | tf_op jit(solution)/shard_map/ppermute | solution.py:457
  88.2 1.6 %collective-permute-start.36 = (bf16[128,1024]{1,0:T(8,128)(2,1)S(1)}, bf16[128,1024]{1,0:T(8,128)(2,1)S(1)}, u32[]{:S(2)}, u32[]{:S(2)}) collective-permute-start(bf16[128,1024]{1,0:T(8,128)(2,1)S(1)} %shard_map.113.refs_4_), channel_id=1, source_target_pairs={{0,16},{8,24},{16,0},{24,8},{1,17},{9,25},{17,1},{25,9},{2,18},{10... | collective-permute-start | bytes 786440 | tf_op jit(solution)/shard_map/ppermute | solution.py:457
  89.8 4.8 %collective-permute-done.31.refs_3_ = bf16[4,256,256]{2,1,0:T(8,128)(2,1)S(1)} collective-permute-done((bf16[4,256,256]{2,1,0:T(8,128)(2,1)S(1)}, bf16[4,256,256]{2,1,0:T(8,128)(2,1)S(1)}, u32[]{:S(2)}, u32[]{:S(2)}) %collective-permute-start.31) | collective-permute-done | bytes 524320 | tf_op jit(solution)/shard_map/ppermute | solution.py:457
  (108 shorter events, 34.6 us)
Async XLA Ops:
  0.6 9.5 %collective-permute-start.1 = (bf16[1024,128]{1,0:T(8,128)(2,1)}, bf16[1024,128]{1,0:T(8,128)(2,1)S(1)}, u32[]{:S(2)}, u32[]{:S(2)}) collective-permute-start(bf16[1024,128]{1,0:T(8,128)(2,1)} %refs_4_.1), channel_id=1, source_target_pairs={{0,16},{8,24},{16,0},{24,8},{1,17},{9,25},{17,1},{25,9},{2,18},{10... | collective-permute-start | bytes 786440 | tf_op jit(solution)/shard_map/ppermute | solution.py:457
  3.7 8.4 %collective-permute-start = (bf16[1024,128]{1,0:T(8,128)(2,1)}, bf16[1024,128]{1,0:T(8,128)(2,1)S(1)}, u32[]{:S(2)}, u32[]{:S(2)}) collective-permute-start(bf16[1024,128]{1,0:T(8,128)(2,1)} %refs_4_.1), channel_id=1, source_target_pairs={{0,8},{8,0},{16,24},{24,16},{1,9},{9,1},{17,25},{25,17},{2,10},{10... | collective-permute-start | bytes 786440 | tf_op jit(solution)/shard_map/ppermute | solution.py:457
  10.3 13.3 %collective-permute-start.3 = (bf16[1024,128]{1,0:T(8,128)(2,1)}, bf16[1024,128]{1,0:T(8,128)(2,1)}, u32[]{:S(2)}, u32[]{:S(2)}) collective-permute-start(bf16[1024,128]{1,0:T(8,128)(2,1)} %get-tuple-element.47.refs_1_), channel_id=1, source_target_pairs={{0,1},{1,0},{2,3},{3,2},{4,5},{5,4},{6,7},{7,6},{8,9},{9,8},{10,11... | collective-permute-start | bytes 786440 | tf_op jit(solution)/shard_map/ppermute | solution.py:457
  19.1 9.5 %collective-permute-start.5 = (bf16[1024,128]{1,0:T(8,128)(2,1)}, bf16[1024,128]{1,0:T(8,128)(2,1)}, u32[]{:S(2)}, u32[]{:S(2)}) collective-permute-start(bf16[1024,128]{1,0:T(8,128)(2,1)} %get-tuple-element.53), channel_id=1, source_target_pairs={{0,1},{1,0},{2,3},{3,2},{4,5},{5,4},{6,7},{7,6},{8,9},{9,8},{10,11... | collective-permute-start | bytes 786440 | tf_op jit(solution)/shard_map/ppermute | solution.py:457
  19.9 16.7 %collective-permute-start.9 = (bf16[2,512,128]{2,1,0:T(8,128)(2,1)}, bf16[2,512,128]{2,1,0:T(8,128)(2,1)S(1)}, u32[]{:S(2)}, u32[]{:S(2)}) collective-permute-start(bf16[2,512,128]{2,1,0:T(8,128)(2,1)} %get-tuple-element.60), channel_id=1, source_target_pairs={{0,4},{1,5},{2,6},{3,7},{4,0},{5,1},{6,2},{7,3},{8,12},{9,13},{10,... | collective-permute-start | bytes 786440 | tf_op jit(solution)/shard_map/ppermute | solution.py:457
  25.7 10.7 %collective-permute-start.4 = (bf16[512,128]{1,0:T(8,128)(2,1)S(1)}, bf16[512,128]{1,0:T(8,128)(2,1)S(1)}, u32[]{:S(2)}, u32[]{:S(2)}) collective-permute-start(bf16[512,128]{1,0:T(8,128)(2,1)S(1)} %get-tuple-element.51.refs_2_), channel_id=1, source_target_pairs={{0,2},{1,3},{2,0},{3,1},{4,6},{5,7},{6,4},{7,5},{8,10},{9,11},{10,... | collective-permute-start | bytes 393224 | tf_op jit(solution)/shard_map/ppermute | solution.py:457
  27.3 15.1 %collective-permute-start.8 = (bf16[1024,128]{1,0:T(8,128)(2,1)S(1)}, bf16[1024,128]{1,0:T(8,128)(2,1)S(1)}, u32[]{:S(2)}, u32[]{:S(2)}) collective-permute-start(bf16[1024,128]{1,0:T(8,128)(2,1)S(1)} %copy-done.11), channel_id=1, source_target_pairs={{0,1},{1,0},{2,3},{3,2},{4,5},{5,4},{6,7},{7,6},{8,9},{9,8},{10,11... | collective-permute-start | bytes 786440 | tf_op jit(solution)/shard_map/ppermute | solution.py:457
  36.5 9.6 %collective-permute-start.7 = (bf16[512,128]{1,0:T(8,128)(2,1)S(1)}, bf16[512,128]{1,0:T(8,128)(2,1)S(1)}, u32[]{:S(2)}, u32[]{:S(2)}) collective-permute-start(bf16[512,128]{1,0:T(8,128)(2,1)S(1)} %get-tuple-element.54.refs_2_), channel_id=1, source_target_pairs={{0,2},{1,3},{2,0},{3,1},{4,6},{5,7},{6,4},{7,5},{8,10},{9,11},{10,... | collective-permute-start | bytes 393224 | tf_op jit(solution)/shard_map/ppermute | solution.py:457
  42.5 9.5 %collective-permute-start.12 = (bf16[256,128]{1,0:T(8,128)(2,1)S(1)}, bf16[256,128]{1,0:T(8,128)(2,1)S(1)}, u32[]{:S(2)}, u32[]{:S(2)}) collective-permute-start(bf16[256,128]{1,0:T(8,128)(2,1)S(1)} %get-tuple-element.66), channel_id=1, source_target_pairs={{0,2},{1,3},{2,0},{3,1},{4,6},{5,7},{6,4},{7,5},{8,10},{9,11},{10,... | collective-permute-start | bytes 196616 | tf_op jit(solution)/shard_map/ppermute | solution.py:457
  44.5 7.5 %collective-permute-start.13 = (bf16[256,128]{1,0:T(8,128)(2,1)S(1)}, bf16[256,128]{1,0:T(8,128)(2,1)S(1)}, u32[]{:S(2)}, u32[]{:S(2)}) collective-permute-start(bf16[256,128]{1,0:T(8,128)(2,1)S(1)} %get-tuple-element.67), channel_id=1, source_target_pairs={{0,6},{1,7},{2,4},{3,5},{4,2},{5,3},{6,0},{7,1},{8,14},{9,15},{10,... | collective-permute-start | bytes 196616 | tf_op jit(solution)/shard_map/ppermute | solution.py:457
  44.6 7.5 %collective-permute-start.11 = (bf16[256,128]{1,0:T(8,128)(2,1)S(1)}, bf16[256,128]{1,0:T(8,128)(2,1)S(1)}, u32[]{:S(2)}, u32[]{:S(2)}) collective-permute-start(bf16[256,128]{1,0:T(8,128)(2,1)S(1)} %get-tuple-element.62.refs_2_), channel_id=1, source_target_pairs={{0,4},{1,5},{2,6},{3,7},{4,0},{5,1},{6,2},{7,3},{8,12},{9,13},{10,... | collective-permute-start | bytes 196616 | tf_op jit(solution)/shard_map/ppermute | solution.py:457
  56.8 7.1 %collective-permute-start.17 = (bf16[2,64,512]{2,1,0:T(8,128)(2,1)S(1)}, bf16[2,64,512]{2,1,0:T(8,128)(2,1)S(1)}, u32[]{:S(2)}, u32[]{:S(2)}) collective-permute-start(bf16[2,64,512]{2,1,0:T(8,128)(2,1)S(1)} %get-tuple-element.77.refs_2_), channel_id=1, source_target_pairs={{0,1},{1,0},{2,3},{3,2},{4,5},{5,4},{6,7},{7,6},{8,9},{9,8},{10,11... | collective-permute-start | bytes 393224 | tf_op jit(solution)/shard_map/ppermute | solution.py:457
  57.7 9.7 %collective-permute-start.22 = (bf16[1,256,256]{2,1,0:T(8,128)(2,1)S(1)}, bf16[1,256,256]{2,1,0:T(8,128)(2,1)S(1)}, u32[]{:S(2)}, u32[]{:S(2)}) collective-permute-start(bf16[1,256,256]{2,1,0:T(8,128)(2,1)S(1)} %get-tuple-element.82.refs_0_), channel_id=1, source_target_pairs={{0,4},{1,5},{2,6},{3,7},{4,0},{5,1},{6,2},{7,3},{8,12},{9,13},{10,... | collective-permute-start | bytes 393224 | tf_op jit(solution)/shard_map/ppermute | solution.py:457
  63.0 10.0 %collective-permute-start.28 = (bf16[2,128,256]{2,1,0:T(8,128)(2,1)S(1)}, bf16[2,128,256]{2,1,0:T(8,128)(2,1)S(1)}, u32[]{:S(2)}, u32[]{:S(2)}) collective-permute-start(bf16[2,128,256]{2,1,0:T(8,128)(2,1)S(1)} %shard_map.100.refs_2_.refs_0_), channel_id=1, source_target_pairs={{0,4},{1,5},{2,6},{3,7},{4,0},{5,1},{6,2},{7,3},{8,12},{9,13},{10,... | collective-permute-start | bytes 393224 | tf_op jit(solution)/shard_map/ppermute | solution.py:457
  67.4 12.4 %collective-permute-start.26 = (bf16[2,256,256]{2,1,0:T(8,128)(2,1)S(1)}, bf16[2,256,256]{2,1,0:T(8,128)(2,1)S(1)}, u32[]{:S(2)}, u32[]{:S(2)}) collective-permute-start(bf16[2,256,256]{2,1,0:T(8,128)(2,1)S(1)} %shard_map.103.refs_2_.refs_0_), channel_id=1, source_target_pairs={{0,2},{1,3},{2,0},{3,1},{4,6},{5,7},{6,4},{7,5},{8,10},{9,11},{10,... | collective-permute-start | bytes 786440 | tf_op jit(solution)/shard_map/ppermute | solution.py:457
  68.0 7.7 %collective-permute-start.27 = (bf16[4,128,256]{2,1,0:T(8,128)(2,1)S(1)}, bf16[4,128,256]{2,1,0:T(8,128)(2,1)S(1)}, u32[]{:S(2)}, u32[]{:S(2)}) collective-permute-start(bf16[4,128,256]{2,1,0:T(8,128)(2,1)S(1)} %shard_map.104.refs_2_), channel_id=1, source_target_pairs={{0,1},{1,0},{2,3},{3,2},{4,5},{5,4},{6,7},{7,6},{8,9},{9,8},{10,11... | collective-permute-start | bytes 786440 | tf_op jit(solution)/shard_map/ppermute | solution.py:457
  69.3 10.5 %collective-permute-start.25 = (bf16[64,512]{1,0:T(8,128)(2,1)S(1)}, bf16[64,512]{1,0:T(8,128)(2,1)S(1)}, u32[]{:S(2)}, u32[]{:S(2)}) collective-permute-start(bf16[64,512]{1,0:T(8,128)(2,1)S(1)} %shard_map.105.refs_2_.refs_0_), channel_id=1, source_target_pairs={{0,6},{1,7},{2,4},{3,5},{4,2},{5,3},{6,0},{7,1},{8,14},{9,15},{10,... | collective-permute-start | bytes 196616 | tf_op jit(solution)/shard_map/ppermute | solution.py:457
  72.5 9.1 %collective-permute-start.24 = (bf16[64,512]{1,0:T(8,128)(2,1)S(1)}, bf16[64,512]{1,0:T(8,128)(2,1)S(1)}, u32[]{:S(2)}, u32[]{:S(2)}) collective-permute-start(bf16[64,512]{1,0:T(8,128)(2,1)S(1)} %shard_map.105.refs_2_.refs_0_), channel_id=1, source_target_pairs={{0,4},{1,5},{2,6},{3,7},{4,0},{5,1},{6,2},{7,3},{8,12},{9,13},{10,... | collective-permute-start | bytes 196616 | tf_op jit(solution)/shard_map/ppermute | solution.py:457
  73.0 8.7 %collective-permute-start.23 = (bf16[64,512]{1,0:T(8,128)(2,1)S(1)}, bf16[64,512]{1,0:T(8,128)(2,1)S(1)}, u32[]{:S(2)}, u32[]{:S(2)}) collective-permute-start(bf16[64,512]{1,0:T(8,128)(2,1)S(1)} %shard_map.105.refs_2_.refs_0_), channel_id=1, source_target_pairs={{0,2},{1,3},{2,0},{3,1},{4,6},{5,7},{6,4},{7,5},{8,10},{9,11},{10,... | collective-permute-start | bytes 196616 | tf_op jit(solution)/shard_map/ppermute | solution.py:457
  75.7 11.7 %collective-permute-start.32 = (bf16[4,128,256]{2,1,0:T(8,128)(2,1)S(1)}, bf16[4,128,256]{2,1,0:T(8,128)(2,1)S(1)}, u32[]{:S(2)}, u32[]{:S(2)}) collective-permute-start(bf16[4,128,256]{2,1,0:T(8,128)(2,1)S(1)} %shard_map.106.refs_4_.refs_0_), channel_id=1, source_target_pairs={{0,2},{1,3},{2,0},{3,1},{4,6},{5,7},{6,4},{7,5},{8,10},{9,11},{10,... | collective-permute-start | bytes 786440 | tf_op jit(solution)/shard_map/ppermute | solution.py:457
  79.8 8.3 %collective-permute-start.33 = (bf16[128,1024]{1,0:T(8,128)(2,1)S(1)}, bf16[128,1024]{1,0:T(8,128)(2,1)S(1)}, u32[]{:S(2)}, u32[]{:S(2)}) collective-permute-start(bf16[128,1024]{1,0:T(8,128)(2,1)S(1)} %shard_map.107.refs_2_), channel_id=1, source_target_pairs={{0,8},{8,0},{16,24},{24,16},{1,9},{9,1},{17,25},{25,17},{2,10},{10... | collective-permute-start | bytes 786440 | tf_op jit(solution)/shard_map/ppermute | solution.py:457
  79.8 14.8 %collective-permute-start.31 = (bf16[4,256,256]{2,1,0:T(8,128)(2,1)S(1)}, bf16[4,256,256]{2,1,0:T(8,128)(2,1)S(1)}, u32[]{:S(2)}, u32[]{:S(2)}) collective-permute-start(bf16[4,256,256]{2,1,0:T(8,128)(2,1)S(1)} %shard_map.108.refs_4_.refs_2_), channel_id=1, source_target_pairs={{0,1},{1,0},{2,3},{3,2},{4,5},{5,4},{6,7},{7,6},{8,9},{9,8},{10,11... | collective-permute-start | bytes 1572872 | tf_op jit(solution)/shard_map/ppermute | solution.py:457
  86.0 11.0 %collective-permute-start.30 = (bf16[2,64,512]{2,1,0:T(8,128)(2,1)S(1)}, bf16[2,64,512]{2,1,0:T(8,128)(2,1)S(1)}, u32[]{:S(2)}, u32[]{:S(2)}) collective-permute-start(bf16[2,64,512]{2,1,0:T(8,128)(2,1)S(1)} %shard_map.110.refs_2_.refs_0_), channel_id=1, source_target_pairs={{0,1},{1,0},{2,3},{3,2},{4,5},{5,4},{6,7},{7,6},{8,9},{9,8},{10,11... | collective-permute-start | bytes 393224 | tf_op jit(solution)/shard_map/ppermute | solution.py:457
  88.2 9.0 %collective-permute-start.36 = (bf16[128,1024]{1,0:T(8,128)(2,1)S(1)}, bf16[128,1024]{1,0:T(8,128)(2,1)S(1)}, u32[]{:S(2)}, u32[]{:S(2)}) collective-permute-start(bf16[128,1024]{1,0:T(8,128)(2,1)S(1)} %shard_map.113.refs_4_), channel_id=1, source_target_pairs={{0,16},{8,24},{16,0},{24,8},{1,17},{9,25},{17,1},{25,9},{2,18},{10... | collective-permute-start | bytes 786440 | tf_op jit(solution)/shard_map/ppermute | solution.py:457
  (25 other events, 115.3 us)

commit v2 on v1

--- a/solution.py
+++ b/solution.py
@@ -11,6 +11,7 @@
 F32 = jnp.float32
 BF16 = jnp.bfloat16
 MIB = 1024 * 1024
+COST_F = 1_000_000_000
 COST, COST_S, COST_W, COST_M = 4_000_000_000, 1_000_000_000, 4_000_000_000, 4_000_000_000
 SMEM = pl.BlockSpec(memory_space=pltpu.SMEM)
 VMEM = pl.BlockSpec(memory_space=pltpu.VMEM)
@@ -40,6 +41,7 @@
     shard_tiles,
     count_ref,
     me_ref,
+    row_ref,
     coords_hbm,
     tiles_ref,
     features_hbm,
@@ -106,7 +108,7 @@
         away_ref[rows, :] = away.astype(away_ref.dtype)
 
 
-def dense_blocks(tiles, coords, count, me, features, outer, shard_rows, limit):
+def dense_blocks(tiles, coords, count, me, row, features, outer, shard_rows, limit):
     slots, tile, _ = tiles.shape
     block_c, width = features.shape
     half_rows = outer * shard_rows
@@ -118,8 +120,8 @@
             jax.ShapeDtypeStruct(features.shape, BF16),
             jax.ShapeDtypeStruct((half_rows, width), BF16),
         ),
-        [SMEM, SMEM, ANYWHERE, pl.BlockSpec(memory_space=pltpu.HBM), ANYWHERE],
-        (count, me, coords, tiles, features),
+        [SMEM, SMEM, SMEM, ANYWHERE, pl.BlockSpec(memory_space=pltpu.HBM), ANYWHERE],
+        (count, me, row, coords, tiles, features),
         [
             pltpu.SMEM(coords.shape, jnp.int32),
             pltpu.SemaphoreType.DMA,
@@ -129,82 +131,85 @@
     )
 
 
-def copy_whole(in_ref, out_ref):
-    out_ref[...] = in_ref[...]
-
-
-def products(unit, near_ref, far_ref, *refs):
-    chunk_refs, away_refs, kept_refs = refs[:4], refs[4:6], refs[6:9]
-    last_keep_ref, last_send_ref, all_ref = refs[9:]
+def products(near_ref, far_ref, *refs):
+    count = len(refs) // 3
+    chunk_refs, away_refs = refs[:count], refs[count : 2 * count - 1]
+    kept_refs, all_ref = refs[2 * count - 1 : -1], refs[-1]
     width = chunk_refs[0].shape[1]
     for i, chunk in enumerate(chunk_refs):
         all_ref[:, i * width : (i + 1) * width] = chunk[...]
     half_rows = near_ref.shape[0]
-    step = math.gcd(unit, 256)
-
-    def put_last(block, row, values):
-        shard = row // unit
-        rows = pl.ds(shard // 2 * unit + row % unit, step)
-        if shard % 2 == 0:
-            last_keep_ref[block, rows, :] = values
-        else:
-            last_send_ref[block, rows, :] = values.astype(last_send_ref.dtype)
-
+    step = math.gcd(half_rows, 256)
     for row in range(0, half_rows, step):
         rows = pl.ds(row, step)
         away = jnp.dot(far_ref[rows, :], all_ref[:, width:], preferred_element_type=F32)
         for i, out in enumerate(away_refs):
             out[rows, :] = away[:, i * width : (i + 1) * width].astype(out.dtype)
-        put_last(1, row, away[:, 2 * width :])
     for row in range(0, half_rows, step):
         rows = pl.ds(row, step)
         kept = jnp.dot(near_ref[rows, :], all_ref[...], preferred_element_type=F32)
         for i, out in enumerate(kept_refs):
             out[rows, :] = kept[:, i * width : (i + 1) * width]
-        put_last(0, row, kept[:, 3 * width :])
-
-
-def all_products(near, far, features, unit, limit):
+
+
+def all_products(near, far, features, limit):
     half_rows, block_c = near.shape
     width = features[0].shape[1]
+    count = len(features)
     away = jax.ShapeDtypeStruct((half_rows, width), BF16)
     kept = jax.ShapeDtypeStruct((half_rows, width), F32)
-    last = (2, half_rows // 2, width)
     outs = call(
-        functools.partial(products, unit),
-        [away] * 2 + [kept] * 3 + [jax.ShapeDtypeStruct(last, F32), jax.ShapeDtypeStruct(last, BF16)],
-        [VMEM] * 6,
+        products,
+        [away] * (count - 1) + [kept] * count,
+        [VMEM] * (2 + count),
         (near, far, *features),
-        [pltpu.VMEM((block_c, 4 * width), BF16)],
+        [pltpu.VMEM((block_c, count * width), BF16)],
         limit,
     )
-    return outs[:2], outs[2:5], outs[5], outs[6]
-
-
-def add_and_halve(unit, kept_ref, came_ref, keep_ref, send_ref):
-    rows = keep_ref.shape[-2]
-    first, second = pl.ds(0, rows), pl.ds(rows, rows)
-    if len(kept_ref.shape) == 2:
-        keep_ref[...] = kept_ref[first, :] + came_ref[first, :].astype(F32)
-        send_ref[...] = (kept_ref[second, :] + came_ref[second, :].astype(F32)).astype(send_ref.dtype)
-        return
-    for i in range(kept_ref.shape[0]):
-        for j in range(rows // unit):
-            here = pl.ds(j * unit, unit)
-            even, odd = pl.ds(2 * j * unit, unit), pl.ds((2 * j + 1) * unit, unit)
-            keep_ref[i, here, :] = kept_ref[i, even, :] + came_ref[i, even, :].astype(F32)
-            total = kept_ref[i, odd, :] + came_ref[i, odd, :].astype(F32)
-            send_ref[i, here, :] = total.astype(send_ref.dtype)
-
-
-def halved(kept, came, unit, before):
-    shape = kept.shape[:-2] + (kept.shape[-2] // 2, kept.shape[-1])
+    return outs[: count - 1], outs[count - 1 :]
+
+
+def both_products(near_ref, far_ref, chunk_ref, keep_ref, send_ref):
+    half_rows = near_ref.shape[0]
+    step = math.gcd(half_rows // 2, 256)
+    for block, ref in ((1, far_ref), (0, near_ref)):
+        for row in range(0, half_rows, step):
+            values = jnp.dot(ref[pl.ds(row, step), :], chunk_ref[...], preferred_element_type=F32)
+            if row < half_rows // 2:
+                keep_ref[block, pl.ds(row, step), :] = values
+            else:
+                rows = pl.ds(row - half_rows // 2, step)
+                send_ref[block, rows, :] = values.astype(send_ref.dtype)
+
+
+def last_products(near, far, chunk, limit, before):
+    shape = (2, near.shape[0] // 2, chunk.shape[1])
     return call(
-        functools.partial(add_and_halve, unit),
+        both_products,
+        (jax.ShapeDtypeStruct(shape, F32), jax.ShapeDtypeStruct(shape, BF16)),
+        [VMEM] * 3,
+        (near, far, chunk),
+        (),
+        limit,
+        before=before,
+    )
+
+
+def add_and_halve(kept_ref, came_ref, keep_ref, send_ref):
+    rows = keep_ref.shape[0]
+    keep_ref[...] = kept_ref[:rows, :] + came_ref[:rows, :].astype(F32)
+    send_ref[...] = (kept_ref[rows:, :] + came_ref[rows:, :].astype(F32)).astype(send_ref.dtype)
+
+
+def halved(kept, came, before, cost=0):
+    shape = (kept.shape[0] // 2, kept.shape[1])
+    return call(
+        add_and_halve,
         (jax.ShapeDtypeStruct(shape, F32), jax.ShapeDtypeStruct(shape, BF16)),
         [VMEM] * 2,
         (kept, came),
         before=before,
+        cost=cost,
     )
 
 
@@ -248,6 +253,23 @@
         before=before,
         cost=cost,
     )
+
+
+def join_and_part(first_ref, second_ref, *out_refs):
+    count = first_ref.shape[0]
+    at = 0
+    for out in out_refs:
+        rows = pl.ds(at, out.shape[1])
+        at += out.shape[1]
+        for k in range(count):
+            out[k] = first_ref[k, rows, :]
+            out[count + k] = second_ref[k, rows, :]
+
+
+def joined_parts(first, second, heights, before):
+    count, _, shard_rows = first.shape
+    shapes = [jax.ShapeDtypeStruct((2 * count, height, shard_rows), first.dtype) for height in heights]
+    return call(join_and_part, shapes, [VMEM] * 2, (first, second), before=before)
 
 
 def mark(out_ref):
@@ -321,8 +343,9 @@
             left_ref[:, cols] = rows_refs[0][k]
             right_ref[:, cols] = rows_refs[1][k]
         else:
-            left_ref[:, cols] = rows_refs[0][2 * k]
-            right_ref[:, cols] = rows_refs[0][2 * k + 1]
+            place = k // 2 * 4 + k % 2
+            left_ref[:, cols] = rows_refs[0][place]
+            right_ref[:, cols] = rows_refs[0][place + 2]
     block_c = near_ref.shape[1]
     step = math.gcd(block_c, 256)
     part = out_refs[0].shape[0]
@@ -462,41 +485,29 @@
     flat = [rel for rels in owners for rel in rels]
 
     features = []
-    for h, inner in chunks:
-        if inner == 0:
-            parts = [swap(node_features, "row", 2 * k) if k else node_features for k in halves[h]]
-            features.append(jnp.concatenate(parts, axis=1) if len(parts) > 1 else parts[0])
-        else:
-            features.append(None)
-    features[1] = swap(features[0], "row", 1)
+    for rels in owners:
+        parts = [swap(node_features, "row", rel) if rel else node_features for rel in rels]
+        features.append(jnp.concatenate(parts, axis=1) if len(parts) > 1 else parts[0])
     near, far, own_features, first_away = dense_blocks(
         tile_values[0, 0],
         pltpu.with_memory_space_constraint(tile_coords[0, 0].T, pltpu.HBM),
         tile_count.reshape(-1),
         my_col,
+        my_row,
         pltpu.with_memory_space_constraint(features[0], pltpu.HBM),
         co,
         shard_rows,
         max(limit, 48),
     )
-    held = call(
-        copy_whole,
-        jax.ShapeDtypeStruct(features[2].shape, BF16),
-        [VMEM],
-        (features[2],),
-        before=(first_away,),
-    )
-    features[3] = swap(held, "row", 1)
     features[0] = own_features
-    away, kept, last_keep, last_send = all_products(near, far, features, shard_rows, limit)
-
+    away, kept = all_products(near, far, features[:3], limit)
+    last_keep, last_send = last_products(near, far, features[3], limit, (kept[0],))
+
+    keeps = [*kept, last_keep]
+    cames = [swap(v, "col", 1) for v in (first_away, *away)] + [swap(last_send, "col", 2)]
     stages = co.bit_length() - 1
-    reversed_bits = [sum(((p >> i) & 1) << (stages - 1 - i) for i in range(stages)) for p in range(co)]
-    keeps = [*kept, last_keep]
-    cames = [swap(v, "col", 1) for v in (first_away, *away)] + [swap(last_send, "col", n_col // 2)]
-    totals = [None] * 4
-    done = [0, 0, 0, 1]
-    turns = [0, 1, 0, 3, 2, 1, 3] if stages == 2 else ([0, 1, 3] * stages + [2])
+    done = [0] * 4
+    turns = [0, 1, 3, 0, 2, 1, 3, 2] if stages == 2 else [0, 1, 2, 3] * stages
     weight_rows = call(
         functools.partial(order_rows, owners),
         jax.ShapeDtypeStruct(layer_weight.shape, BF16),
@@ -507,33 +518,31 @@
     last = weight_rows
     for i in turns:
         before = [last]
-        if stages == 2 and i == 3 and done[3] == 1:
+        if stages == 2 and done[i] == 1 and i == 3:
             before.append(cames[0])
-        if i == 2:
-            own, sends = parted(keeps[2], cames[2], co, before)
-            last = sends[0]
-            totals[2] = [own] + [
-                swap(send, "col", 2 * reversed_bits[p + 1]) for p, send in enumerate(sends)
-            ]
-        elif i == 3 and done[3] == stages:
+        if stages == 2 and done[i] == 1 and i == 2:
+            before.append(cames[1])
+        if i == 3 and done[3] == 0:
             shape = keeps[3].shape[1:]
-            own, last = call(
+            keeps[3], last = call(
                 add_pair,
                 (jax.ShapeDtypeStruct(shape, F32), jax.ShapeDtypeStruct(shape, BF16)),
                 [VMEM] * 2,
                 (keeps[3], cames[3]),
                 before=before,
             )
-            totals[3] = [own, swap(last, "col", 1)]
+            bit = 1
         else:
-            keeps[i], last = halved(keeps[i], cames[i], shard_rows, before)
-            done[i] += 1
-            cames[i] = swap(last, "col", 1 << done[i] if i < 3 else n_col >> done[i])
-            totals[i] = [keeps[i], cames[i]]
-
-    out_groups = ((3,), (2,), (1, 0))
+            cost = COST_F if i in (1, 2) and done[i] == 0 else 0
+            keeps[i], last = halved(keeps[i], cames[i], before, cost)
+            bit = 2 << done[i]
+        done[i] += 1
+        cames[i] = swap(last, "col", bit)
+    totals = [[keep, came] for keep, came in zip(keeps, cames)]
+
+    out_groups = ((3,), (2, 1, 0))
     hidden, agg, grad_pre, grads = layer(
-        totals, out_groups, weight_rows, cotangent, (marked(last, cames[1]),)
+        totals, out_groups, weight_rows, cotangent, (last,)
     )
 
     places = [[flat.index(2 * k + inner) for k in range(ro)] for inner in range(2)]
@@ -596,18 +605,29 @@
         state["last"] = total
         state["w"] = [total, swap(total, axis, 1)]
 
-    rows = {"C": grads[0], "A": grads[1], "M": grads[2]}
-    bits = {"C": n_col // 2, "A": 1, "M": n_col // 2}
-    came_rows = {name: swap(rows[name], "col", bits[name]) for name in rows}
+    top = n_col // 2
+    rows = {"C": grads[0], "AM": grads[1]}
+    came_rows = {name: swap(rows[name], "col", top) for name in rows}
+    bits = {"C": top, "A": 2 * top, "M": top}
     backs = {}
 
+    def part():
+        height = grads[0].shape[1]
+        heights = (height, 2 * height)
+        outs = joined_parts(rows["AM"], came_rows["AM"], heights, order())
+        state["last"] = outs[0]
+        rows["A"], rows["M"] = outs
+        came_rows["A"] = swap(rows["A"], "col", 1)
+        came_rows["M"] = swap(rows["M"], "col", top // 2)
+        bits["M"] = top // 2
+
     def join(name, cost=0):
-        first, second = rows[name], came_rows[name]
-        bit = n_col // 2 if name == "A" and bits[name] == 1 else bits[name] // 2
-        bits[name] = bit
-        rows[name] = state["last"] = joined(first, second, order(), cost)
-        if not (name == "A" and bit == 1):
-            came_rows[name] = swap(rows[name], "col", bit)
+        rows[name] = state["last"] = joined(rows[name], came_rows[name], order(), cost)
+        bits[name] //= 2
+        if name == "A" and bits[name] == top:
+            bits[name] //= 2
+        if not (name == "A" and bits[name] == 1):
+            came_rows[name] = swap(rows[name], "col", bits[name])
 
     def back(members, pair, cost=0, more=()):
         dtypes = [BF16 if chunk[1] else F32 for chunk in members]
@@ -626,18 +646,17 @@
             arrived.extend(swap(v, "row", 2 * halves[h][p]) for p, v in zip(sent, parts))
 
     weight_core()
-    join("A")
     join("C")
     weight_side()
-    join("M")
     for _ in range(stages - 1):
         join("C")
+    part()
     weight_line()
-    for _ in range(stages - 1):
-        join("A", COST)
     back([(1, 1)], (rows["C"], came_rows["C"]))
     for _ in range(stages - 1):
         join("M")
+    for _ in range(stages - 1):
+        join("A")
     weight_sum()
     weight_stack("col")
     join("A", COST_S)

time: 101 us -> 99.6 us (0.986)
  waiting for transfers between devices: 36.1 us -> 42.8 us
  local copies, waits for them, and re-layouts: 6.14 us -> 0.01 us
  Pallas kernels: 16.4 us -> 13.6 us
    ppermute x37 -> x35, waiting for transfers between devices: 36.1 us -> 42.8 us  [swap(): return lax.ppermute(v, axis, [(i, i ^ bit) for i in range(size)])]
    unnamed x24 -> x4, local copies, waits for them, and re-layouts: 6.14 us -> 0.01 us
    pallas_call x34 -> x33, Pallas kernels: 16.4 us -> 13.6 us  [call(): pl.pallas_call(run, out_shape=tuple(out_shape) if many else out_shape, in...]
    ppermute x37 -> x35, starting transfers between devices: 40.3 us -> 41.2 us  [swap(): return lax.ppermute(v, axis, [(i, i ^ bit) for i in range(size)])]
  transfers between devices with their start and end apart: 37 -> 35, of which waited for: 15 -> 19; matrix products, arithmetic and copies ran while one was open for 0% -> 0% of each run, Pallas kernels for 14% -> 11%
where the time goes in v2:
time: 99.6 us; the launch traced here: 99.2 us
  waiting for transfers between devices  42.8 us (43%)
  starting transfers between devices  41.2 us (41%)
  Pallas kernels  13.6 us (14%)
  between operations  1.58 us (2%)
    ppermute x35, waiting for transfers between devices, swap(): return lax.ppermute(v, axis, [(i, i ^ bit) for i in range(size)])  42.8 us
    ppermute x35, starting transfers between devices, swap(): return lax.ppermute(v, axis, [(i, i ^ bit) for i in range(size)])  41.2 us
    pallas_call x33, Pallas kernels, call(): pl.pallas_call(run, out_shape=tuple(out_shape) if many else out_shape, in...  13.6 us
  transfers between devices with their start and end apart: 35, of which 19 were waited for; matrix products, arithmetic and copies ran while one was open for 0% of the time, Pallas kernels for 11%

profile of v2, /device:TPU:0, one launch (start us, length us, event | category | flops | bytes accessed | tf_op | source)
XLA Modules:
  0.0 99.2 jit_solution(17649730391416700411)
XLA Ops:
  1.1 2.6 %collective-permute-start.1 = (bf16[1024,128]{1,0:T(8,128)(2,1)}, bf16[1024,128]{1,0:T(8,128)(2,1)S(1)}, u32[]{:S(2)}, u32[]{:S(2)}) collective-permute-start(bf16[1024,128]{1,0:T(8,128)(2,1)} %refs_5_.1), channel_id=1, source_target_pairs={{0,16},{8,24},{16,0},{24,8},{1,17},{9,25},{17,1},{25,9},{2,18},{10... | collective-permute-start | bytes 786440 | tf_op jit(solution)/shard_map/ppermute | solution.py:480
  4.5 3.6 %shard_map.85 = (bf16[1024,1024]{1,0:T(8,128)(2,1)S(1)}, bf16[1024,1024]{1,0:T(8,128)(2,1)S(1)}, bf16[1024,128]{1,0:T(8,128)(2,1)S(1)}, bf16[1024,128]{1,0:T(8,128)(2,1)S(1)}) custom-call(s32[1]{0:T(128)} %bitcast.7.refs_0_, s32[1]{0:T(128)} %bitcast.1.refs_1_.refs_0_, s32[1]{0:T(128)} %bitcast.2.refs_2_.refs_0_, s32[2,96]{1,0:T(2,128)} %bitcast.9, ...), custom_call_target="tpu_custom_call" | custom-call | tf_op jit(solution)/shard_map/pallas_call | solution.py:28
  9.0 2.1 %collective-permute-done.1.refs_4_ = bf16[1024,128]{1,0:T(8,128)(2,1)S(1)} collective-permute-done((bf16[1024,128]{1,0:T(8,128)(2,1)}, bf16[1024,128]{1,0:T(8,128)(2,1)S(1)}, u32[]{:S(2)}, u32[]{:S(2)}) %collective-permute-start.1) | collective-permute-done | bytes 262176 | tf_op jit(solution)/shard_map/ppermute | solution.py:480
  11.1 1.9 %shard_map.86 = (bf16[1024,128]{1,0:T(8,128)(2,1)S(1)}, bf16[1024,128]{1,0:T(8,128)(2,1)S(1)}, f32[1024,128]{1,0:T(8,128)S(1)}, f32[1024,128]{1,0:T(8,128)S(1)}, f32[1024,128]{1,0:T(8,128)S(1)}) custom-call(bf16[1024,1024]{1,0:T(8,128)(2,1)S(1)} %get-tuple-element.45.refs_0_, bf16[1024,1024]{1,0:T(8,128)(2,1)S(1)} %get-tuple-element.46.refs_1_, ...), custom_call_target="tpu_custom_call" | custom-call | tf_op jit(solution)/shard_map/pallas_call | solution.py:28
  13.0 2.0 %collective-permute-start.6 = (bf16[1024,128]{1,0:T(8,128)(2,1)S(1)}, bf16[1024,128]{1,0:T(8,128)(2,1)S(1)}, u32[]{:S(2)}, u32[]{:S(2)}) collective-permute-start(bf16[1024,128]{1,0:T(8,128)(2,1)S(1)} %get-tuple-element.55), channel_id=1, source_target_pairs={{0,1},{1,0},{2,3},{3,2},{4,5},{5,4},{6,7},{7,6},{8,9},{9,8},{10,11... | collective-permute-start | bytes 786440 | tf_op jit(solution)/shard_map/ppermute | solution.py:480
  17.5 1.7 %collective-permute-start.5 = (bf16[2,512,128]{2,1,0:T(8,128)(2,1)S(1)}, bf16[2,512,128]{2,1,0:T(8,128)(2,1)S(1)}, u32[]{:S(2)}, u32[]{:S(2)}) collective-permute-start(bf16[2,512,128]{2,1,0:T(8,128)(2,1)S(1)} %get-tuple-element.53), channel_id=1, source_target_pairs={{0,2},{1,3},{2,0},{3,1},{4,6},{5,7},{6,4},{7,5},{8,10},{9,11},{10,... | collective-permute-start | bytes 786440 | tf_op jit(solution)/shard_map/ppermute | solution.py:480
  21.8 2.5 %collective-permute-start.8 = (bf16[512,128]{1,0:T(8,128)(2,1)S(1)}, bf16[512,128]{1,0:T(8,128)(2,1)S(1)}, u32[]{:S(2)}, u32[]{:S(2)}) collective-permute-start(bf16[512,128]{1,0:T(8,128)(2,1)S(1)} %get-tuple-element.56.refs_2_), channel_id=1, source_target_pairs={{0,2},{1,3},{2,0},{3,1},{4,6},{5,7},{6,4},{7,5},{8,10},{9,11},{10,... | collective-permute-start | bytes 393224 | tf_op jit(solution)/shard_map/ppermute | solution.py:480
  24.3 2.4 %collective-permute-done.5.refs_1_ = bf16[2,512,128]{2,1,0:T(8,128)(2,1)S(1)} collective-permute-done((bf16[2,512,128]{2,1,0:T(8,128)(2,1)S(1)}, bf16[2,512,128]{2,1,0:T(8,128)(2,1)S(1)}, u32[]{:S(2)}, u32[]{:S(2)}) %collective-permute-start.5) | collective-permute-done | bytes 262176 | tf_op jit(solution)/shard_map/ppermute | solution.py:480
  26.7 1.6 %collective-permute-start.12 = (bf16[512,128]{1,0:T(8,128)(2,1)S(1)}, bf16[512,128]{1,0:T(8,128)(2,1)S(1)}, u32[]{:S(2)}, u32[]{:S(2)}) collective-permute-start(bf16[512,128]{1,0:T(8,128)(2,1)S(1)} %get-tuple-element.57.refs_2_), channel_id=1, source_target_pairs={{0,1},{1,0},{2,3},{3,2},{4,5},{5,4},{6,7},{7,6},{8,9},{9,8},{10,11... | collective-permute-start | bytes 393224 | tf_op jit(solution)/shard_map/ppermute | solution.py:480
  29.6 1.7 %collective-permute-start.11 = (bf16[512,128]{1,0:T(8,128)(2,1)S(1)}, bf16[512,128]{1,0:T(8,128)(2,1)S(1)}, u32[]{:S(2)}, u32[]{:S(2)}) collective-permute-start(bf16[512,128]{1,0:T(8,128)(2,1)S(1)} %get-tuple-element.63.refs_2_), channel_id=1, source_target_pairs={{0,2},{1,3},{2,0},{3,1},{4,6},{5,7},{6,4},{7,5},{8,10},{9,11},{10,... | collective-permute-start | bytes 393224 | tf_op jit(solution)/shard_map/ppermute | solution.py:480
  31.2 2.6 %collective-permute-start.7 = (bf16[256,128]{1,0:T(8,128)(2,1)S(1)}, bf16[256,128]{1,0:T(8,128)(2,1)S(1)}, u32[]{:S(2)}, u32[]{:S(2)}) collective-permute-start(bf16[256,128]{1,0:T(8,128)(2,1)S(1)} %get-tuple-element.59.refs_2_), channel_id=1, source_target_pairs={{0,4},{1,5},{2,6},{3,7},{4,0},{5,1},{6,2},{7,3},{8,12},{9,13},{10,... | collective-permute-start | bytes 196616 | tf_op jit(solution)/shard_map/ppermute | solution.py:480
  34.8 3.0 %collective-permute-done.7.refs_3_.refs_1_ = bf16[256,128]{1,0:T(8,128)(2,1)S(1)} collective-permute-done((bf16[256,128]{1,0:T(8,128)(2,1)S(1)}, bf16[256,128]{1,0:T(8,128)(2,1)S(1)}, u32[]{:S(2)}, u32[]{:S(2)}) %collective-permute-start.7) | collective-permute-done | bytes 65568 | tf_op jit(solution)/shard_map/ppermute | solution.py:480
  37.9 1.7 %collective-permute-start.14 = (bf16[256,128]{1,0:T(8,128)(2,1)S(1)}, bf16[256,128]{1,0:T(8,128)(2,1)S(1)}, u32[]{:S(2)}, u32[]{:S(2)}) collective-permute-start(bf16[256,128]{1,0:T(8,128)(2,1)S(1)} %get-tuple-element.68.refs_2_), channel_id=1, source_target_pairs={{0,4},{1,5},{2,6},{3,7},{4,0},{5,1},{6,2},{7,3},{8,12},{9,13},{10,... | collective-permute-start | bytes 196616 | tf_op jit(solution)/shard_map/ppermute | solution.py:480
  39.6 2.3 %collective-permute-done.10.refs_3_ = bf16[256,128]{1,0:T(8,128)(2,1)S(1)} collective-permute-done((bf16[256,128]{1,0:T(8,128)(2,1)S(1)}, bf16[256,128]{1,0:T(8,128)(2,1)S(1)}, u32[]{:S(2)}, u32[]{:S(2)}) %collective-permute-start.10) | collective-permute-done | bytes 65568 | tf_op jit(solution)/shard_map/ppermute | solution.py:480
  43.1 4.5 %collective-permute-done.13.refs_5_ = bf16[256,128]{1,0:T(8,128)(2,1)S(1)} collective-permute-done((bf16[256,128]{1,0:T(8,128)(2,1)S(1)}, bf16[256,128]{1,0:T(8,128)(2,1)S(1)}, u32[]{:S(2)}, u32[]{:S(2)}) %collective-permute-start.13) | collective-permute-done | bytes 65568 | tf_op jit(solution)/shard_map/ppermute | solution.py:480
  49.2 2.9 %collective-permute-start.19 = (bf16[1,384,256]{2,1,0:T(8,128)(2,1)S(1)}, bf16[1,384,256]{2,1,0:T(8,128)(2,1)S(1)}, u32[]{:S(2)}, u32[]{:S(2)}) collective-permute-start(bf16[1,384,256]{2,1,0:T(8,128)(2,1)S(1)} %get-tuple-element.82.refs_0_), channel_id=1, source_target_pairs={{0,4},{1,5},{2,6},{3,7},{4,0},{5,1},{6,2},{7,3},{8,12},{9,13},{10,... | collective-permute-start | bytes 589832 | tf_op jit(solution)/shard_map/ppermute | solution.py:480
  53.8 5.8 %collective-permute-done.17.refs_1_ = bf16[1,128,256]{2,1,0:T(8,128)(2,1)S(1)} collective-permute-done((bf16[1,128,256]{2,1,0:T(8,128)(2,1)S(1)}, bf16[1,128,256]{2,1,0:T(8,128)(2,1)S(1)}, u32[]{:S(2)}, u32[]{:S(2)}) %collective-permute-start.17) | collective-permute-done | bytes 65568 | tf_op jit(solution)/shard_map/ppermute | solution.py:480
  59.7 6.8 %collective-permute-done.20.refs_1_ = bf16[2,128,256]{2,1,0:T(8,128)(2,1)S(1)} collective-permute-done((bf16[2,128,256]{2,1,0:T(8,128)(2,1)S(1)}, bf16[2,128,256]{2,1,0:T(8,128)(2,1)S(1)}, u32[]{:S(2)}, u32[]{:S(2)}) %collective-permute-start.20) | collective-permute-done | bytes 131104 | tf_op jit(solution)/shard_map/ppermute | solution.py:480
  70.4 2.7 %collective-permute-done.18.refs_1_ = bf16[64,512]{1,0:T(8,128)(2,1)S(1)} collective-permute-done((bf16[64,512]{1,0:T(8,128)(2,1)S(1)}, bf16[64,512]{1,0:T(8,128)(2,1)S(1)}, u32[]{:S(2)}, u32[]{:S(2)}) %collective-permute-start.18) | collective-permute-done | bytes 65568 | tf_op jit(solution)/shard_map/ppermute | solution.py:480
  73.1 1.9 %collective-permute-start.23 = (bf16[64,512]{1,0:T(8,128)(2,1)S(1)}, bf16[64,512]{1,0:T(8,128)(2,1)S(1)}, u32[]{:S(2)}, u32[]{:S(2)}) collective-permute-start(bf16[64,512]{1,0:T(8,128)(2,1)S(1)} %shard_map.104.refs_4_.refs_0_), channel_id=1, source_target_pairs={{0,6},{1,7},{2,4},{3,5},{4,2},{5,3},{6,0},{7,1},{8,14},{9,15},{10,... | collective-permute-start | bytes 196616 | tf_op jit(solution)/shard_map/ppermute | solution.py:480
  75.0 1.6 %collective-permute-start.22 = (bf16[64,512]{1,0:T(8,128)(2,1)S(1)}, bf16[64,512]{1,0:T(8,128)(2,1)S(1)}, u32[]{:S(2)}, u32[]{:S(2)}) collective-permute-start(bf16[64,512]{1,0:T(8,128)(2,1)S(1)} %shard_map.104.refs_4_.refs_0_), channel_id=1, source_target_pairs={{0,4},{1,5},{2,6},{3,7},{4,0},{5,1},{6,2},{7,3},{8,12},{9,13},{10,... | collective-permute-start | bytes 196616 | tf_op jit(solution)/shard_map/ppermute | solution.py:480
  81.3 1.6 %collective-permute-start.27 = (bf16[64,512]{1,0:T(8,128)(2,1)S(1)}, bf16[64,512]{1,0:T(8,128)(2,1)S(1)}, u32[]{:S(2)}, u32[]{:S(2)}) collective-permute-start(bf16[64,512]{1,0:T(8,128)(2,1)S(1)} %shard_map.108.refs_0_.refs_2_), channel_id=1, source_target_pairs={{0,16},{8,24},{16,0},{24,8},{1,17},{9,25},{17,1},{25,9},{2,18},{10... | collective-permute-start | bytes 196616 | tf_op jit(solution)/shard_map/ppermute | solution.py:480
  82.9 2.8 %collective-permute-done.27.refs_1_ = bf16[64,512]{1,0:T(8,128)(2,1)S(1)} collective-permute-done((bf16[64,512]{1,0:T(8,128)(2,1)S(1)}, bf16[64,512]{1,0:T(8,128)(2,1)S(1)}, u32[]{:S(2)}, u32[]{:S(2)}) %collective-permute-start.27) | collective-permute-done | bytes 65568 | tf_op jit(solution)/shard_map/ppermute | solution.py:480
  91.0 2.3 %collective-permute-done.29.refs_3_ = bf16[4,256,256]{2,1,0:T(8,128)(2,1)S(1)} collective-permute-done((bf16[4,256,256]{2,1,0:T(8,128)(2,1)S(1)}, bf16[4,256,256]{2,1,0:T(8,128)(2,1)S(1)}, u32[]{:S(2)}, u32[]{:S(2)}) %collective-permute-start.29) | collective-permute-done | bytes 524320 | tf_op jit(solution)/shard_map/ppermute | solution.py:480
  (83 shorter events, 33.2 us)
Async XLA Ops:
  0.6 8.3 %collective-permute-start = (bf16[1024,128]{1,0:T(8,128)(2,1)}, bf16[1024,128]{1,0:T(8,128)(2,1)S(1)}, u32[]{:S(2)}, u32[]{:S(2)}) collective-permute-start(bf16[1024,128]{1,0:T(8,128)(2,1)} %refs_5_.1), channel_id=1, source_target_pairs={{0,8},{8,0},{16,24},{24,16},{1,9},{9,1},{17,25},{25,17},{2,10},{10... | collective-permute-start | bytes 786440 | tf_op jit(solution)/shard_map/ppermute | solution.py:480
  1.1 10.0 %collective-permute-start.1 = (bf16[1024,128]{1,0:T(8,128)(2,1)}, bf16[1024,128]{1,0:T(8,128)(2,1)S(1)}, u32[]{:S(2)}, u32[]{:S(2)}) collective-permute-start(bf16[1024,128]{1,0:T(8,128)(2,1)} %refs_5_.1), channel_id=1, source_target_pairs={{0,16},{8,24},{16,0},{24,8},{1,17},{9,25},{17,1},{25,9},{2,18},{10... | collective-permute-start | bytes 786440 | tf_op jit(solution)/shard_map/ppermute | solution.py:480
  3.7 12.5 %collective-permute-start.3 = (bf16[1024,128]{1,0:T(8,128)(2,1)}, bf16[1024,128]{1,0:T(8,128)(2,1)S(1)}, u32[]{:S(2)}, u32[]{:S(2)}) collective-permute-start(bf16[1024,128]{1,0:T(8,128)(2,1)} %refs_5_.1), channel_id=1, source_target_pairs={{0,24},{8,16},{16,8},{24,0},{1,25},{9,17},{17,9},{25,1},{2,26},{10... | collective-permute-start | bytes 786440 | tf_op jit(solution)/shard_map/ppermute | solution.py:480
  8.1 12.6 %collective-permute-start.2 = (bf16[1024,128]{1,0:T(8,128)(2,1)S(1)}, bf16[1024,128]{1,0:T(8,128)(2,1)S(1)}, u32[]{:S(2)}, u32[]{:S(2)}) collective-permute-start(bf16[1024,128]{1,0:T(8,128)(2,1)S(1)} %get-tuple-element.49), channel_id=1, source_target_pairs={{0,1},{1,0},{2,3},{3,2},{4,5},{5,4},{6,7},{7,6},{8,9},{9,8},{10,11... | collective-permute-start | bytes 786440 | tf_op jit(solution)/shard_map/ppermute | solution.py:480
  13.0 8.7 %collective-permute-start.6 = (bf16[1024,128]{1,0:T(8,128)(2,1)S(1)}, bf16[1024,128]{1,0:T(8,128)(2,1)S(1)}, u32[]{:S(2)}, u32[]{:S(2)}) collective-permute-start(bf16[1024,128]{1,0:T(8,128)(2,1)S(1)} %get-tuple-element.55), channel_id=1, source_target_pairs={{0,1},{1,0},{2,3},{3,2},{4,5},{5,4},{6,7},{7,6},{8,9},{9,8},{10,11... | collective-permute-start | bytes 786440 | tf_op jit(solution)/shard_map/ppermute | solution.py:480
  17.5 9.2 %collective-permute-start.5 = (bf16[2,512,128]{2,1,0:T(8,128)(2,1)S(1)}, bf16[2,512,128]{2,1,0:T(8,128)(2,1)S(1)}, u32[]{:S(2)}, u32[]{:S(2)}) collective-permute-start(bf16[2,512,128]{2,1,0:T(8,128)(2,1)S(1)} %get-tuple-element.53), channel_id=1, source_target_pairs={{0,2},{1,3},{2,0},{3,1},{4,6},{5,7},{6,4},{7,5},{8,10},{9,11},{10,... | collective-permute-start | bytes 786440 | tf_op jit(solution)/shard_map/ppermute | solution.py:480
  19.2 10.3 %collective-permute-start.9 = (bf16[1024,128]{1,0:T(8,128)(2,1)S(1)}, bf16[1024,128]{1,0:T(8,128)(2,1)S(1)}, u32[]{:S(2)}, u32[]{:S(2)}) collective-permute-start(bf16[1024,128]{1,0:T(8,128)(2,1)S(1)} %get-tuple-element.62), channel_id=1, source_target_pairs={{0,1},{1,0},{2,3},{3,2},{4,5},{5,4},{6,7},{7,6},{8,9},{9,8},{10,11... | collective-permute-start | bytes 786440 | tf_op jit(solution)/shard_map/ppermute | solution.py:480
  20.8 8.7 %collective-permute-start.4 = (bf16[512,128]{1,0:T(8,128)(2,1)S(1)}, bf16[512,128]{1,0:T(8,128)(2,1)S(1)}, u32[]{:S(2)}, u32[]{:S(2)}) collective-permute-start(bf16[512,128]{1,0:T(8,128)(2,1)S(1)} %get-tuple-element.52.refs_2_), channel_id=1, source_target_pairs={{0,2},{1,3},{2,0},{3,1},{4,6},{5,7},{6,4},{7,5},{8,10},{9,11},{10,... | collective-permute-start | bytes 393224 | tf_op jit(solution)/shard_map/ppermute | solution.py:480
  21.8 12.1 %collective-permute-start.8 = (bf16[512,128]{1,0:T(8,128)(2,1)S(1)}, bf16[512,128]{1,0:T(8,128)(2,1)S(1)}, u32[]{:S(2)}, u32[]{:S(2)}) collective-permute-start(bf16[512,128]{1,0:T(8,128)(2,1)S(1)} %get-tuple-element.56.refs_2_), channel_id=1, source_target_pairs={{0,2},{1,3},{2,0},{3,1},{4,6},{5,7},{6,4},{7,5},{8,10},{9,11},{10,... | collective-permute-start | bytes 393224 | tf_op jit(solution)/shard_map/ppermute | solution.py:480
  26.7 11.1 %collective-permute-start.12 = (bf16[512,128]{1,0:T(8,128)(2,1)S(1)}, bf16[512,128]{1,0:T(8,128)(2,1)S(1)}, u32[]{:S(2)}, u32[]{:S(2)}) collective-permute-start(bf16[512,128]{1,0:T(8,128)(2,1)S(1)} %get-tuple-element.57.refs_2_), channel_id=1, source_target_pairs={{0,1},{1,0},{2,3},{3,2},{4,5},{5,4},{6,7},{7,6},{8,9},{9,8},{10,11... | collective-permute-start | bytes 393224 | tf_op jit(solution)/shard_map/ppermute | solution.py:480
  29.6 10.0 %collective-permute-start.11 = (bf16[512,128]{1,0:T(8,128)(2,1)S(1)}, bf16[512,128]{1,0:T(8,128)(2,1)S(1)}, u32[]{:S(2)}, u32[]{:S(2)}) collective-permute-start(bf16[512,128]{1,0:T(8,128)(2,1)S(1)} %get-tuple-element.63.refs_2_), channel_id=1, source_target_pairs={{0,2},{1,3},{2,0},{3,1},{4,6},{5,7},{6,4},{7,5},{8,10},{9,11},{10,... | collective-permute-start | bytes 393224 | tf_op jit(solution)/shard_map/ppermute | solution.py:480
  33.9 8.0 %collective-permute-start.10 = (bf16[256,128]{1,0:T(8,128)(2,1)S(1)}, bf16[256,128]{1,0:T(8,128)(2,1)S(1)}, u32[]{:S(2)}, u32[]{:S(2)}) collective-permute-start(bf16[256,128]{1,0:T(8,128)(2,1)S(1)} %get-tuple-element.65.refs_2_), channel_id=1, source_target_pairs={{0,4},{1,5},{2,6},{3,7},{4,0},{5,1},{6,2},{7,3},{8,12},{9,13},{10,... | collective-permute-start | bytes 196616 | tf_op jit(solution)/shard_map/ppermute | solution.py:480
  49.2 10.4 %collective-permute-start.17 = (bf16[1,128,256]{2,1,0:T(8,128)(2,1)S(1)}, bf16[1,128,256]{2,1,0:T(8,128)(2,1)S(1)}, u32[]{:S(2)}, u32[]{:S(2)}) collective-permute-start(bf16[1,128,256]{2,1,0:T(8,128)(2,1)S(1)} %get-tuple-element.79.refs_0_), channel_id=1, source_target_pairs={{0,4},{1,5},{2,6},{3,7},{4,0},{5,1},{6,2},{7,3},{8,12},{9,13},{10,... | collective-permute-start | bytes 196616 | tf_op jit(solution)/shard_map/ppermute | solution.py:480
  49.2 18.9 %collective-permute-start.19 = (bf16[1,384,256]{2,1,0:T(8,128)(2,1)S(1)}, bf16[1,384,256]{2,1,0:T(8,128)(2,1)S(1)}, u32[]{:S(2)}, u32[]{:S(2)}) collective-permute-start(bf16[1,384,256]{2,1,0:T(8,128)(2,1)S(1)} %get-tuple-element.82.refs_0_), channel_id=1, source_target_pairs={{0,4},{1,5},{2,6},{3,7},{4,0},{5,1},{6,2},{7,3},{8,12},{9,13},{10,... | collective-permute-start | bytes 589832 | tf_op jit(solution)/shard_map/ppermute | solution.py:480
  52.2 7.4 %collective-permute-start.16 = (bf16[2,64,512]{2,1,0:T(8,128)(2,1)S(1)}, bf16[2,64,512]{2,1,0:T(8,128)(2,1)S(1)}, u32[]{:S(2)}, u32[]{:S(2)}) collective-permute-start(bf16[2,64,512]{2,1,0:T(8,128)(2,1)S(1)} %get-tuple-element.78.refs_2_), channel_id=1, source_target_pairs={{0,1},{1,0},{2,3},{3,2},{4,5},{5,4},{6,7},{7,6},{8,9},{9,8},{10,11... | collective-permute-start | bytes 393224 | tf_op jit(solution)/shard_map/ppermute | solution.py:480
  59.6 7.0 %collective-permute-start.20 = (bf16[2,128,256]{2,1,0:T(8,128)(2,1)S(1)}, bf16[2,128,256]{2,1,0:T(8,128)(2,1)S(1)}, u32[]{:S(2)}, u32[]{:S(2)}) collective-permute-start(bf16[2,128,256]{2,1,0:T(8,128)(2,1)S(1)} %shard_map.100.refs_2_.refs_0_), channel_id=1, source_target_pairs={{0,2},{1,3},{2,0},{3,1},{4,6},{5,7},{6,4},{7,5},{8,10},{9,11},{10,... | collective-permute-start | bytes 393224 | tf_op jit(solution)/shard_map/ppermute | solution.py:480
  66.6 10.0 %collective-permute-start.26 = (bf16[4,128,256]{2,1,0:T(8,128)(2,1)S(1)}, bf16[4,128,256]{2,1,0:T(8,128)(2,1)S(1)}, u32[]{:S(2)}, u32[]{:S(2)}) collective-permute-start(bf16[4,128,256]{2,1,0:T(8,128)(2,1)S(1)} %shard_map.102.refs_2_), channel_id=1, source_target_pairs={{0,1},{1,0},{2,3},{3,2},{4,5},{5,4},{6,7},{7,6},{8,9},{9,8},{10,11... | collective-permute-start | bytes 786440 | tf_op jit(solution)/shard_map/ppermute | solution.py:480
  68.2 10.2 %collective-permute-start.25 = (bf16[2,256,256]{2,1,0:T(8,128)(2,1)S(1)}, bf16[2,256,256]{2,1,0:T(8,128)(2,1)S(1)}, u32[]{:S(2)}, u32[]{:S(2)}) collective-permute-start(bf16[2,256,256]{2,1,0:T(8,128)(2,1)S(1)} %get-tuple-element.84.refs_0_), channel_id=1, source_target_pairs={{0,2},{1,3},{2,0},{3,1},{4,6},{5,7},{6,4},{7,5},{8,10},{9,11},{10,... | collective-permute-start | bytes 786440 | tf_op jit(solution)/shard_map/ppermute | solution.py:480
  68.3 10.2 %collective-permute-start.24 = (bf16[2,128,256]{2,1,0:T(8,128)(2,1)S(1)}, bf16[2,128,256]{2,1,0:T(8,128)(2,1)S(1)}, u32[]{:S(2)}, u32[]{:S(2)}) collective-permute-start(bf16[2,128,256]{2,1,0:T(8,128)(2,1)S(1)} %get-tuple-element.83.refs_2_.refs_0_), channel_id=1, source_target_pairs={{0,1},{1,0},{2,3},{3,2},{4,5},{5,4},{6,7},{7,6},{8,9},{9,8},{10,11... | collective-permute-start | bytes 393224 | tf_op jit(solution)/shard_map/ppermute | solution.py:480
  78.4 11.0 %collective-permute-start.31 = (bf16[128,1024]{1,0:T(8,128)(2,1)S(1)}, bf16[128,1024]{1,0:T(8,128)(2,1)S(1)}, u32[]{:S(2)}, u32[]{:S(2)}) collective-permute-start(bf16[128,1024]{1,0:T(8,128)(2,1)S(1)} %shard_map.105.refs_2_), channel_id=1, source_target_pairs={{0,8},{8,0},{16,24},{24,16},{1,9},{9,1},{17,25},{25,17},{2,10},{10... | collective-permute-start | bytes 786440 | tf_op jit(solution)/shard_map/ppermute | solution.py:480
  78.5 14.8 %collective-permute-start.29 = (bf16[4,256,256]{2,1,0:T(8,128)(2,1)S(1)}, bf16[4,256,256]{2,1,0:T(8,128)(2,1)S(1)}, u32[]{:S(2)}, u32[]{:S(2)}) collective-permute-start(bf16[4,256,256]{2,1,0:T(8,128)(2,1)S(1)} %shard_map.106.refs_2_), channel_id=1, source_target_pairs={{0,1},{1,0},{2,3},{3,2},{4,5},{5,4},{6,7},{7,6},{8,9},{9,8},{10,11... | collective-permute-start | bytes 1572872 | tf_op jit(solution)/shard_map/ppermute | solution.py:480
  80.1 8.5 %collective-permute-start.30 = (bf16[4,128,256]{2,1,0:T(8,128)(2,1)S(1)}, bf16[4,128,256]{2,1,0:T(8,128)(2,1)S(1)}, u32[]{:S(2)}, u32[]{:S(2)}) collective-permute-start(bf16[4,128,256]{2,1,0:T(8,128)(2,1)S(1)} %shard_map.107.refs_4_.refs_0_), channel_id=1, source_target_pairs={{0,2},{1,3},{2,0},{3,1},{4,6},{5,7},{6,4},{7,5},{8,10},{9,11},{10,... | collective-permute-start | bytes 786440 | tf_op jit(solution)/shard_map/ppermute | solution.py:480
  85.7 10.0 %collective-permute-start.28 = (bf16[2,64,512]{2,1,0:T(8,128)(2,1)S(1)}, bf16[2,64,512]{2,1,0:T(8,128)(2,1)S(1)}, u32[]{:S(2)}, u32[]{:S(2)}) collective-permute-start(bf16[2,64,512]{2,1,0:T(8,128)(2,1)S(1)} %shard_map.109.refs_2_.refs_0_), channel_id=1, source_target_pairs={{0,1},{1,0},{2,3},{3,2},{4,5},{5,4},{6,7},{7,6},{8,9},{9,8},{10,11... | collective-permute-start | bytes 393224 | tf_op jit(solution)/shard_map/ppermute | solution.py:480
  89.4 7.7 %collective-permute-start.34 = (bf16[128,1024]{1,0:T(8,128)(2,1)S(1)}, bf16[128,1024]{1,0:T(8,128)(2,1)S(1)}, u32[]{:S(2)}, u32[]{:S(2)}) collective-permute-start(bf16[128,1024]{1,0:T(8,128)(2,1)S(1)} %shard_map.112.refs_4_), channel_id=1, source_target_pairs={{0,16},{8,24},{16,0},{24,8},{1,17},{9,25},{17,1},{25,9},{2,18},{10... | collective-permute-start | bytes 786440 | tf_op jit(solution)/shard_map/ppermute | solution.py:480
  (13 other events, 75.0 us)

commit v3 on v2

--- a/solution.py
+++ b/solution.py
@@ -169,24 +169,21 @@
     return outs[: count - 1], outs[count - 1 :]
 
 
-def both_products(near_ref, far_ref, chunk_ref, keep_ref, send_ref):
+def one_product(near_ref, far_ref, chunk_ref, away_ref, kept_ref):
     half_rows = near_ref.shape[0]
-    step = math.gcd(half_rows // 2, 256)
-    for block, ref in ((1, far_ref), (0, near_ref)):
+    step = math.gcd(half_rows, 256)
+    for ref, out in ((far_ref, away_ref), (near_ref, kept_ref)):
         for row in range(0, half_rows, step):
-            values = jnp.dot(ref[pl.ds(row, step), :], chunk_ref[...], preferred_element_type=F32)
-            if row < half_rows // 2:
-                keep_ref[block, pl.ds(row, step), :] = values
-            else:
-                rows = pl.ds(row - half_rows // 2, step)
-                send_ref[block, rows, :] = values.astype(send_ref.dtype)
+            rows = pl.ds(row, step)
+            values = jnp.dot(ref[rows, :], chunk_ref[...], preferred_element_type=F32)
+            out[rows, :] = values.astype(out.dtype)
 
 
 def last_products(near, far, chunk, limit, before):
-    shape = (2, near.shape[0] // 2, chunk.shape[1])
+    shape = (near.shape[0], chunk.shape[1])
     return call(
-        both_products,
-        (jax.ShapeDtypeStruct(shape, F32), jax.ShapeDtypeStruct(shape, BF16)),
+        one_product,
+        (jax.ShapeDtypeStruct(shape, BF16), jax.ShapeDtypeStruct(shape, F32)),
         [VMEM] * 3,
         (near, far, chunk),
         (),
@@ -231,11 +228,6 @@
         before=before,
     )
     return outs[0], outs[1:]
-
-
-def add_pair(kept_ref, came_ref, keep_ref, send_ref):
-    keep_ref[...] = kept_ref[0] + came_ref[0].astype(F32)
-    send_ref[...] = (kept_ref[1] + came_ref[1].astype(F32)).astype(send_ref.dtype)
 
 
 def join_two(first_ref, second_ref, out_ref):
@@ -343,9 +335,8 @@
             left_ref[:, cols] = rows_refs[0][k]
             right_ref[:, cols] = rows_refs[1][k]
         else:
-            place = k // 2 * 4 + k % 2
-            left_ref[:, cols] = rows_refs[0][place]
-            right_ref[:, cols] = rows_refs[0][place + 2]
+            left_ref[:, cols] = rows_refs[0][2 * k]
+            right_ref[:, cols] = rows_refs[0][2 * k + 1]
     block_c = near_ref.shape[1]
     step = math.gcd(block_c, 256)
     part = out_refs[0].shape[0]
@@ -501,46 +492,36 @@
     )
     features[0] = own_features
     away, kept = all_products(near, far, features[:3], limit)
-    last_keep, last_send = last_products(near, far, features[3], limit, (kept[0],))
-
-    keeps = [*kept, last_keep]
-    cames = [swap(v, "col", 1) for v in (first_away, *away)] + [swap(last_send, "col", 2)]
+    keeps = [*kept, None]
+    cames = [swap(v, "col", 1) for v in (first_away, *away)] + [None]
     stages = co.bit_length() - 1
     done = [0] * 4
-    turns = [0, 1, 3, 0, 2, 1, 3, 2] if stages == 2 else [0, 1, 2, 3] * stages
+    turns = [0, 1, 0, 2, 1, 3, 2, 3] if stages == 2 else [0, 1, 2, 3] * stages
     weight_rows = call(
         functools.partial(order_rows, owners),
         jax.ShapeDtypeStruct(layer_weight.shape, BF16),
         [SMEM, VMEM],
         (my_row, layer_weight),
-        before=(last_keep,),
+        before=(kept[0],),
     )
     last = weight_rows
-    for i in turns:
+    for turn, i in enumerate(turns):
         before = [last]
-        if stages == 2 and done[i] == 1 and i == 3:
+        if stages == 2 and turn == 5:
             before.append(cames[0])
-        if stages == 2 and done[i] == 1 and i == 2:
+        if stages == 2 and turn == 7:
             before.append(cames[1])
-        if i == 3 and done[3] == 0:
-            shape = keeps[3].shape[1:]
-            keeps[3], last = call(
-                add_pair,
-                (jax.ShapeDtypeStruct(shape, F32), jax.ShapeDtypeStruct(shape, BF16)),
-                [VMEM] * 2,
-                (keeps[3], cames[3]),
-                before=before,
-            )
-            bit = 1
-        else:
-            cost = COST_F if i in (1, 2) and done[i] == 0 else 0
-            keeps[i], last = halved(keeps[i], cames[i], before, cost)
-            bit = 2 << done[i]
+        cost = COST_F if i in (1, 2) and done[i] == 0 else 0
+        keeps[i], last = halved(keeps[i], cames[i], before, cost)
+        cames[i] = swap(last, "col", 2 << done[i])
         done[i] += 1
-        cames[i] = swap(last, "col", bit)
+        if turn == 0:
+            last_away, keeps[3] = last_products(near, far, features[3], limit, (last,))
+            cames[3] = swap(last_away, "col", 1)
+            last = keeps[3]
     totals = [[keep, came] for keep, came in zip(keeps, cames)]
 
-    out_groups = ((3,), (2, 1, 0))
+    out_groups = ((3,), (2,), (1, 0))
     hidden, agg, grad_pre, grads = layer(
         totals, out_groups, weight_rows, cotangent, (last,)
     )
@@ -583,11 +564,14 @@
         )
         state["last"] = outs[0]
         state["w"] = [outs[0]] + [swap(v, "row", 2 * (k + 1)) for k, v in enumerate(outs[1:])]
+        state["bit"] = n_col // 2
 
     def weight_line():
-        total = sum_of(state["w"], BF16, order())
+        bit = state["bit"]
+        total = sum_of(state["w"], BF16 if bit > 2 else F32, order())
         state["last"] = total
-        state["w"] = [total] + [swap(total, "col", 2 * k) for k in range(1, co)]
+        state["w"] = [total, swap(total, "col", bit)]
+        state["bit"] = bit // 2
 
     def weight_sum():
         total = sum_of(state["w"], BF16, order(), COST_W)
@@ -605,29 +589,18 @@
         state["last"] = total
         state["w"] = [total, swap(total, axis, 1)]
 
-    top = n_col // 2
-    rows = {"C": grads[0], "AM": grads[1]}
-    came_rows = {name: swap(rows[name], "col", top) for name in rows}
-    bits = {"C": top, "A": 2 * top, "M": top}
+    rows = {"C": grads[0], "A": grads[1], "M": grads[2]}
+    bits = {"C": n_col // 2, "A": 1, "M": n_col // 2}
+    came_rows = {name: swap(rows[name], "col", bits[name]) for name in rows}
     backs = {}
 
-    def part():
-        height = grads[0].shape[1]
-        heights = (height, 2 * height)
-        outs = joined_parts(rows["AM"], came_rows["AM"], heights, order())
-        state["last"] = outs[0]
-        rows["A"], rows["M"] = outs
-        came_rows["A"] = swap(rows["A"], "col", 1)
-        came_rows["M"] = swap(rows["M"], "col", top // 2)
-        bits["M"] = top // 2
-
     def join(name, cost=0):
-        rows[name] = state["last"] = joined(rows[name], came_rows[name], order(), cost)
-        bits[name] //= 2
-        if name == "A" and bits[name] == top:
-            bits[name] //= 2
-        if not (name == "A" and bits[name] == 1):
-            came_rows[name] = swap(rows[name], "col", bits[name])
+        first, second = rows[name], came_rows[name]
+        bit = n_col // 2 if name == "A" and bits[name] == 1 else bits[name] // 2
+        bits[name] = bit
+        rows[name] = state["last"] = joined(first, second, order(), cost)
+        if not (name == "A" and bit == 1):
+            came_rows[name] = swap(rows[name], "col", bit)
 
     def back(members, pair, cost=0, more=()):
         dtypes = [BF16 if chunk[1] else F32 for chunk in members]
@@ -646,17 +619,20 @@
             arrived.extend(swap(v, "row", 2 * halves[h][p]) for p, v in zip(sent, parts))
 
     weight_core()
+    join("A")
     join("C")
     weight_side()
+    join("M")
     for _ in range(stages - 1):
         join("C")
-    part()
     weight_line()
+    for _ in range(stages - 1):
+        join("A", COST)
+    for _ in range(stages - 1):
+        weight_line()
     back([(1, 1)], (rows["C"], came_rows["C"]))
     for _ in range(stages - 1):
         join("M")
-    for _ in range(stages - 1):
-        join("A")
     weight_sum()
     weight_stack("col")
     join("A", COST_S)

time: 99.6 us -> 97.4 us (0.978)
  waiting for transfers between devices: 42.8 us -> 36.2 us
  starting transfers between devices: 41.2 us -> 46.1 us
    ppermute x35, waiting for transfers between devices: 42.8 us -> 36.2 us  [swap(): return lax.ppermute(v, axis, [(i, i ^ bit) for i in range(size)])]
    ppermute x35, starting transfers between devices: 41.2 us -> 46.1 us  [swap(): return lax.ppermute(v, axis, [(i, i ^ bit) for i in range(size)])]
    pallas_call x33 -> x35, Pallas kernels: 13.6 us -> 13.9 us  [call(): pl.pallas_call(run, out_shape=tuple(out_shape) if many else out_shape, in...]
  transfers between devices with their start and end apart: 35 -> 35, of which waited for: 19 -> 18; matrix products, arithmetic and copies ran while one was open for 0% -> 0% of each run, Pallas kernels for 11% -> 12%
where the time goes in v3:
time: 97.4 us; the launch traced here: 97.7 us
  starting transfers between devices  46.1 us (47%)
  waiting for transfers between devices  36.2 us (37%)
  Pallas kernels  13.9 us (14%)
  between operations  1.56 us (2%)
    ppermute x35, starting transfers between devices, swap(): return lax.ppermute(v, axis, [(i, i ^ bit) for i in range(size)])  46.1 us
    ppermute x35, waiting for transfers between devices, swap(): return lax.ppermute(v, axis, [(i, i ^ bit) for i in range(size)])  36.2 us
    pallas_call x35, Pallas kernels, call(): pl.pallas_call(run, out_shape=tuple(out_shape) if many else out_shape, in...  13.9 us
  transfers between devices with their start and end apart: 35, of which 18 were waited for; matrix products, arithmetic and copies ran while one was open for 0% of the time, Pallas kernels for 12%

profile of v3, /device:TPU:0, one launch (start us, length us, event | category | flops | bytes accessed | tf_op | source)
XLA Modules:
  0.0 97.7 jit_solution(685096227716533277)
XLA Ops:
  1.2 2.6 %collective-permute-start.1 = (bf16[1024,128]{1,0:T(8,128)(2,1)}, bf16[1024,128]{1,0:T(8,128)(2,1)S(1)}, u32[]{:S(2)}, u32[]{:S(2)}) collective-permute-start(bf16[1024,128]{1,0:T(8,128)(2,1)} %refs_5_.1), channel_id=1, source_target_pairs={{0,16},{8,24},{16,0},{24,8},{1,17},{9,25},{17,1},{25,9},{2,18},{10... | collective-permute-start | bytes 786440 | tf_op jit(solution)/shard_map/ppermute | solution.py:471
  4.4 3.6 %shard_map.85 = (bf16[1024,1024]{1,0:T(8,128)(2,1)S(1)}, bf16[1024,1024]{1,0:T(8,128)(2,1)S(1)}, bf16[1024,128]{1,0:T(8,128)(2,1)S(1)}, bf16[1024,128]{1,0:T(8,128)(2,1)S(1)}) custom-call(s32[1]{0:T(128)} %bitcast.7.refs_0_, s32[1]{0:T(128)} %bitcast.1.refs_1_.refs_0_, s32[1]{0:T(128)} %bitcast.2.refs_2_.refs_0_, s32[2,96]{1,0:T(2,128)} %bitcast.9, ...), custom_call_target="tpu_custom_call" | custom-call | tf_op jit(solution)/shard_map/pallas_call | solution.py:28
  9.0 1.9 %collective-permute-done.1.refs_4_ = bf16[1024,128]{1,0:T(8,128)(2,1)S(1)} collective-permute-done((bf16[1024,128]{1,0:T(8,128)(2,1)}, bf16[1024,128]{1,0:T(8,128)(2,1)S(1)}, u32[]{:S(2)}, u32[]{:S(2)}) %collective-permute-start.1) | collective-permute-done | bytes 262176 | tf_op jit(solution)/shard_map/ppermute | solution.py:471
  10.9 1.9 %shard_map.86 = (bf16[1024,128]{1,0:T(8,128)(2,1)S(1)}, bf16[1024,128]{1,0:T(8,128)(2,1)S(1)}, f32[1024,128]{1,0:T(8,128)S(1)}, f32[1024,128]{1,0:T(8,128)S(1)}, f32[1024,128]{1,0:T(8,128)S(1)}) custom-call(bf16[1024,1024]{1,0:T(8,128)(2,1)S(1)} %get-tuple-element.44.refs_0_, bf16[1024,1024]{1,0:T(8,128)(2,1)S(1)} %get-tuple-element.45.refs_1_, ...), custom_call_target="tpu_custom_call" | custom-call | tf_op jit(solution)/shard_map/pallas_call | solution.py:28
  12.7 1.8 %collective-permute-start.4 = (bf16[1024,128]{1,0:T(8,128)(2,1)S(1)}, bf16[1024,128]{1,0:T(8,128)(2,1)S(1)}, u32[]{:S(2)}, u32[]{:S(2)}) collective-permute-start(bf16[1024,128]{1,0:T(8,128)(2,1)S(1)} %get-tuple-element.52), channel_id=1, source_target_pairs={{0,1},{1,0},{2,3},{3,2},{4,5},{5,4},{6,7},{7,6},{8,9},{9,8},{10,11... | collective-permute-start | bytes 786440 | tf_op jit(solution)/shard_map/ppermute | solution.py:471
  19.6 1.9 %collective-permute-start.3 = (bf16[512,128]{1,0:T(8,128)(2,1)S(1)}, bf16[512,128]{1,0:T(8,128)(2,1)S(1)}, u32[]{:S(2)}, u32[]{:S(2)}) collective-permute-start(bf16[512,128]{1,0:T(8,128)(2,1)S(1)} %get-tuple-element.50.refs_3_), channel_id=1, source_target_pairs={{0,2},{1,3},{2,0},{3,1},{4,6},{5,7},{6,4},{7,5},{8,10},{9,11},{10,... | collective-permute-start | bytes 393224 | tf_op jit(solution)/shard_map/ppermute | solution.py:471
  22.1 2.2 %collective-permute-start.7 = (bf16[512,128]{1,0:T(8,128)(2,1)S(1)}, bf16[512,128]{1,0:T(8,128)(2,1)S(1)}, u32[]{:S(2)}, u32[]{:S(2)}) collective-permute-start(bf16[512,128]{1,0:T(8,128)(2,1)S(1)} %get-tuple-element.54.refs_2_), channel_id=1, source_target_pairs={{0,2},{1,3},{2,0},{3,1},{4,6},{5,7},{6,4},{7,5},{8,10},{9,11},{10,... | collective-permute-start | bytes 393224 | tf_op jit(solution)/shard_map/ppermute | solution.py:471
  25.6 3.4 %collective-permute-start.6 = (bf16[256,128]{1,0:T(8,128)(2,1)S(1)}, bf16[256,128]{1,0:T(8,128)(2,1)S(1)}, u32[]{:S(2)}, u32[]{:S(2)}) collective-permute-start(bf16[256,128]{1,0:T(8,128)(2,1)S(1)} %get-tuple-element.56.refs_2_), channel_id=1, source_target_pairs={{0,4},{1,5},{2,6},{3,7},{4,0},{5,1},{6,2},{7,3},{8,12},{9,13},{10,... | collective-permute-start | bytes 196616 | tf_op jit(solution)/shard_map/ppermute | solution.py:471
  29.1 1.7 %collective-permute-start.10 = (bf16[512,128]{1,0:T(8,128)(2,1)S(1)}, bf16[512,128]{1,0:T(8,128)(2,1)S(1)}, u32[]{:S(2)}, u32[]{:S(2)}) collective-permute-start(bf16[512,128]{1,0:T(8,128)(2,1)S(1)} %get-tuple-element.60.refs_2_), channel_id=1, source_target_pairs={{0,2},{1,3},{2,0},{3,1},{4,6},{5,7},{6,4},{7,5},{8,10},{9,11},{10,... | collective-permute-start | bytes 393224 | tf_op jit(solution)/shard_map/ppermute | solution.py:471
  30.8 1.9 %collective-permute-done.11.refs_1_ = bf16[1024,128]{1,0:T(8,128)(2,1)S(1)} collective-permute-done((bf16[1024,128]{1,0:T(8,128)(2,1)S(1)}, bf16[1024,128]{1,0:T(8,128)(2,1)S(1)}, u32[]{:S(2)}, u32[]{:S(2)}) %collective-permute-start.11) | collective-permute-done | bytes 262176 | tf_op jit(solution)/shard_map/ppermute | solution.py:471
  32.7 2.2 %collective-permute-start.13 = (bf16[512,128]{1,0:T(8,128)(2,1)S(1)}, bf16[512,128]{1,0:T(8,128)(2,1)S(1)}, u32[]{:S(2)}, u32[]{:S(2)}) collective-permute-start(bf16[512,128]{1,0:T(8,128)(2,1)S(1)} %get-tuple-element.65.refs_2_), channel_id=1, source_target_pairs={{0,2},{1,3},{2,0},{3,1},{4,6},{5,7},{6,4},{7,5},{8,10},{9,11},{10,... | collective-permute-start | bytes 393224 | tf_op jit(solution)/shard_map/ppermute | solution.py:471
  34.9 2.3 %collective-permute-start.9 = (bf16[256,128]{1,0:T(8,128)(2,1)S(1)}, bf16[256,128]{1,0:T(8,128)(2,1)S(1)}, u32[]{:S(2)}, u32[]{:S(2)}) collective-permute-start(bf16[256,128]{1,0:T(8,128)(2,1)S(1)} %get-tuple-element.62.refs_2_), channel_id=1, source_target_pairs={{0,4},{1,5},{2,6},{3,7},{4,0},{5,1},{6,2},{7,3},{8,12},{9,13},{10,... | collective-permute-start | bytes 196616 | tf_op jit(solution)/shard_map/ppermute | solution.py:471
  37.9 3.7 %collective-permute-done.9.refs_3_ = bf16[256,128]{1,0:T(8,128)(2,1)S(1)} collective-permute-done((bf16[256,128]{1,0:T(8,128)(2,1)S(1)}, bf16[256,128]{1,0:T(8,128)(2,1)S(1)}, u32[]{:S(2)}, u32[]{:S(2)}) %collective-permute-start.9) | collective-permute-done | bytes 65568 | tf_op jit(solution)/shard_map/ppermute | solution.py:471
  43.0 2.3 %collective-permute-done.12.refs_5_ = bf16[256,128]{1,0:T(8,128)(2,1)S(1)} collective-permute-done((bf16[256,128]{1,0:T(8,128)(2,1)S(1)}, bf16[256,128]{1,0:T(8,128)(2,1)S(1)}, u32[]{:S(2)}, u32[]{:S(2)}) %collective-permute-start.12) | collective-permute-done | bytes 65568 | tf_op jit(solution)/shard_map/ppermute | solution.py:471
  52.2 1.7 %collective-permute-start.21 = (bf16[1,256,256]{2,1,0:T(8,128)(2,1)S(1)}, bf16[1,256,256]{2,1,0:T(8,128)(2,1)S(1)}, u32[]{:S(2)}, u32[]{:S(2)}) collective-permute-start(bf16[1,256,256]{2,1,0:T(8,128)(2,1)S(1)} %get-tuple-element.82.refs_0_), channel_id=1, source_target_pairs={{0,4},{1,5},{2,6},{3,7},{4,0},{5,1},{6,2},{7,3},{8,12},{9,13},{10,... | collective-permute-start | bytes 393224 | tf_op jit(solution)/shard_map/ppermute | solution.py:471
  55.5 2.1 %collective-permute-start.20 = (bf16[2,128,256]{2,1,0:T(8,128)(2,1)S(1)}, bf16[2,128,256]{2,1,0:T(8,128)(2,1)S(1)}, u32[]{:S(2)}, u32[]{:S(2)}) collective-permute-start(bf16[2,128,256]{2,1,0:T(8,128)(2,1)S(1)} %shard_map.101.refs_2_.refs_0_), channel_id=1, source_target_pairs={{0,2},{1,3},{2,0},{3,1},{4,6},{5,7},{6,4},{7,5},{8,10},{9,11},{10,... | collective-permute-start | bytes 393224 | tf_op jit(solution)/shard_map/ppermute | solution.py:471
  58.7 1.8 %collective-permute-done.21.refs_1_ = bf16[1,256,256]{2,1,0:T(8,128)(2,1)S(1)} collective-permute-done((bf16[1,256,256]{2,1,0:T(8,128)(2,1)S(1)}, bf16[1,256,256]{2,1,0:T(8,128)(2,1)S(1)}, u32[]{:S(2)}, u32[]{:S(2)}) %collective-permute-start.21) | collective-permute-done | bytes 131104 | tf_op jit(solution)/shard_map/ppermute | solution.py:471
  60.5 2.3 %collective-permute-start.25 = (bf16[2,256,256]{2,1,0:T(8,128)(2,1)S(1)}, bf16[2,256,256]{2,1,0:T(8,128)(2,1)S(1)}, u32[]{:S(2)}, u32[]{:S(2)}) collective-permute-start(bf16[2,256,256]{2,1,0:T(8,128)(2,1)S(1)} %shard_map.103.refs_2_.refs_0_), channel_id=1, source_target_pairs={{0,2},{1,3},{2,0},{3,1},{4,6},{5,7},{6,4},{7,5},{8,10},{9,11},{10,... | collective-permute-start | bytes 786440 | tf_op jit(solution)/shard_map/ppermute | solution.py:471
  64.4 6.1 %collective-permute-start.22 = (bf16[64,512]{1,0:T(8,128)(2,1)S(1)}, bf16[64,512]{1,0:T(8,128)(2,1)S(1)}, u32[]{:S(2)}, u32[]{:S(2)}) collective-permute-start(bf16[64,512]{1,0:T(8,128)(2,1)S(1)} %shard_map.105.refs_2_.refs_0_), channel_id=1, source_target_pairs={{0,4},{1,5},{2,6},{3,7},{4,0},{5,1},{6,2},{7,3},{8,12},{9,13},{10,... | collective-permute-start | bytes 196616 | tf_op jit(solution)/shard_map/ppermute | solution.py:471
  70.5 2.7 %collective-permute-done.22.refs_1_ = bf16[64,512]{1,0:T(8,128)(2,1)S(1)} collective-permute-done((bf16[64,512]{1,0:T(8,128)(2,1)S(1)}, bf16[64,512]{1,0:T(8,128)(2,1)S(1)}, u32[]{:S(2)}, u32[]{:S(2)}) %collective-permute-start.22) | collective-permute-done | bytes 65568 | tf_op jit(solution)/shard_map/ppermute | solution.py:471
  73.2 2.8 %collective-permute-start.24 = (f32[64,512]{1,0:T(8,128)S(1)}, f32[64,512]{1,0:T(8,128)S(1)}, u32[]{:S(2)}, u32[]{:S(2)}) collective-permute-start(f32[64,512]{1,0:T(8,128)S(1)} %shard_map.107.refs_4_.refs_0_), channel_id=1, source_target_pairs={{0,2},{1,3},{2,0},{3,1},{4,6},{5,7},{6,4},{7,5},{8,10},{9,11},{10,... | collective-permute-start | bytes 393224 | tf_op jit(solution)/shard_map/ppermute | solution.py:471
  77.1 2.6 %collective-permute-done.24.refs_1_ = f32[64,512]{1,0:T(8,128)S(1)} collective-permute-done((f32[64,512]{1,0:T(8,128)S(1)}, f32[64,512]{1,0:T(8,128)S(1)}, u32[]{:S(2)}, u32[]{:S(2)}) %collective-permute-start.24) | collective-permute-done | bytes 131104 | tf_op jit(solution)/shard_map/ppermute | solution.py:471
  79.8 4.3 %collective-permute-done.27.refs_1_ = bf16[64,512]{1,0:T(8,128)(2,1)S(1)} collective-permute-done((bf16[64,512]{1,0:T(8,128)(2,1)S(1)}, bf16[64,512]{1,0:T(8,128)(2,1)S(1)}, u32[]{:S(2)}, u32[]{:S(2)}) %collective-permute-start.27) | collective-permute-done | bytes 65568 | tf_op jit(solution)/shard_map/ppermute | solution.py:471
  86.4 5.4 %collective-permute-done.29.refs_3_ = bf16[4,256,256]{2,1,0:T(8,128)(2,1)S(1)} collective-permute-done((bf16[4,256,256]{2,1,0:T(8,128)(2,1)S(1)}, bf16[4,256,256]{2,1,0:T(8,128)(2,1)S(1)}, u32[]{:S(2)}, u32[]{:S(2)}) %collective-permute-start.29) | collective-permute-done | bytes 524320 | tf_op jit(solution)/shard_map/ppermute | solution.py:471
  (87 shorter events, 31.2 us)
Async XLA Ops:
  0.6 8.3 %collective-permute-start = (bf16[1024,128]{1,0:T(8,128)(2,1)}, bf16[1024,128]{1,0:T(8,128)(2,1)S(1)}, u32[]{:S(2)}, u32[]{:S(2)}) collective-permute-start(bf16[1024,128]{1,0:T(8,128)(2,1)} %refs_5_.1), channel_id=1, source_target_pairs={{0,8},{8,0},{16,24},{24,16},{1,9},{9,1},{17,25},{25,17},{2,10},{10... | collective-permute-start | bytes 786440 | tf_op jit(solution)/shard_map/ppermute | solution.py:471
  1.2 9.7 %collective-permute-start.1 = (bf16[1024,128]{1,0:T(8,128)(2,1)}, bf16[1024,128]{1,0:T(8,128)(2,1)S(1)}, u32[]{:S(2)}, u32[]{:S(2)}) collective-permute-start(bf16[1024,128]{1,0:T(8,128)(2,1)} %refs_5_.1), channel_id=1, source_target_pairs={{0,16},{8,24},{16,0},{24,8},{1,17},{9,25},{17,1},{25,9},{2,18},{10... | collective-permute-start | bytes 786440 | tf_op jit(solution)/shard_map/ppermute | solution.py:471
  8.0 8.3 %collective-permute-start.2 = (bf16[1024,128]{1,0:T(8,128)(2,1)S(1)}, bf16[1024,128]{1,0:T(8,128)(2,1)S(1)}, u32[]{:S(2)}, u32[]{:S(2)}) collective-permute-start(bf16[1024,128]{1,0:T(8,128)(2,1)S(1)} %get-tuple-element.48), channel_id=1, source_target_pairs={{0,1},{1,0},{2,3},{3,2},{4,5},{5,4},{6,7},{7,6},{8,9},{9,8},{10,11... | collective-permute-start | bytes 786440 | tf_op jit(solution)/shard_map/ppermute | solution.py:471
  8.7 8.1 %collective-permute-start.5 = (bf16[1024,128]{1,0:T(8,128)(2,1)S(1)}, bf16[1024,128]{1,0:T(8,128)(2,1)S(1)}, u32[]{:S(2)}, u32[]{:S(2)}) collective-permute-start(bf16[1024,128]{1,0:T(8,128)(2,1)S(1)} %copy-done.2), channel_id=1, source_target_pairs={{0,24},{8,16},{16,8},{24,0},{1,25},{9,17},{17,9},{25,1},{2,26},{10... | collective-permute-start | bytes 786440 | tf_op jit(solution)/shard_map/ppermute | solution.py:471
  12.7 9.3 %collective-permute-start.4 = (bf16[1024,128]{1,0:T(8,128)(2,1)S(1)}, bf16[1024,128]{1,0:T(8,128)(2,1)S(1)}, u32[]{:S(2)}, u32[]{:S(2)}) collective-permute-start(bf16[1024,128]{1,0:T(8,128)(2,1)S(1)} %get-tuple-element.52), channel_id=1, source_target_pairs={{0,1},{1,0},{2,3},{3,2},{4,5},{5,4},{6,7},{7,6},{8,9},{9,8},{10,11... | collective-permute-start | bytes 786440 | tf_op jit(solution)/shard_map/ppermute | solution.py:471
  14.5 14.5 %collective-permute-start.8 = (bf16[1024,128]{1,0:T(8,128)(2,1)S(1)}, bf16[1024,128]{1,0:T(8,128)(2,1)S(1)}, u32[]{:S(2)}, u32[]{:S(2)}) collective-permute-start(bf16[1024,128]{1,0:T(8,128)(2,1)S(1)} %get-tuple-element.59), channel_id=1, source_target_pairs={{0,1},{1,0},{2,3},{3,2},{4,5},{5,4},{6,7},{7,6},{8,9},{9,8},{10,11... | collective-permute-start | bytes 786440 | tf_op jit(solution)/shard_map/ppermute | solution.py:471
  18.1 14.6 %collective-permute-start.11 = (bf16[1024,128]{1,0:T(8,128)(2,1)S(1)}, bf16[1024,128]{1,0:T(8,128)(2,1)S(1)}, u32[]{:S(2)}, u32[]{:S(2)}) collective-permute-start(bf16[1024,128]{1,0:T(8,128)(2,1)S(1)} %get-tuple-element.64), channel_id=1, source_target_pairs={{0,1},{1,0},{2,3},{3,2},{4,5},{5,4},{6,7},{7,6},{8,9},{9,8},{10,11... | collective-permute-start | bytes 786440 | tf_op jit(solution)/shard_map/ppermute | solution.py:471
  22.1 8.7 %collective-permute-start.7 = (bf16[512,128]{1,0:T(8,128)(2,1)S(1)}, bf16[512,128]{1,0:T(8,128)(2,1)S(1)}, u32[]{:S(2)}, u32[]{:S(2)}) collective-permute-start(bf16[512,128]{1,0:T(8,128)(2,1)S(1)} %get-tuple-element.54.refs_2_), channel_id=1, source_target_pairs={{0,2},{1,3},{2,0},{3,1},{4,6},{5,7},{6,4},{7,5},{8,10},{9,11},{10,... | collective-permute-start | bytes 393224 | tf_op jit(solution)/shard_map/ppermute | solution.py:471
  25.6 7.1 %collective-permute-start.6 = (bf16[256,128]{1,0:T(8,128)(2,1)S(1)}, bf16[256,128]{1,0:T(8,128)(2,1)S(1)}, u32[]{:S(2)}, u32[]{:S(2)}) collective-permute-start(bf16[256,128]{1,0:T(8,128)(2,1)S(1)} %get-tuple-element.56.refs_2_), channel_id=1, source_target_pairs={{0,4},{1,5},{2,6},{3,7},{4,0},{5,1},{6,2},{7,3},{8,12},{9,13},{10,... | collective-permute-start | bytes 196616 | tf_op jit(solution)/shard_map/ppermute | solution.py:471
  29.1 8.1 %collective-permute-start.10 = (bf16[512,128]{1,0:T(8,128)(2,1)S(1)}, bf16[512,128]{1,0:T(8,128)(2,1)S(1)}, u32[]{:S(2)}, u32[]{:S(2)}) collective-permute-start(bf16[512,128]{1,0:T(8,128)(2,1)S(1)} %get-tuple-element.60.refs_2_), channel_id=1, source_target_pairs={{0,2},{1,3},{2,0},{3,1},{4,6},{5,7},{6,4},{7,5},{8,10},{9,11},{10,... | collective-permute-start | bytes 393224 | tf_op jit(solution)/shard_map/ppermute | solution.py:471
  32.7 8.9 %collective-permute-start.13 = (bf16[512,128]{1,0:T(8,128)(2,1)S(1)}, bf16[512,128]{1,0:T(8,128)(2,1)S(1)}, u32[]{:S(2)}, u32[]{:S(2)}) collective-permute-start(bf16[512,128]{1,0:T(8,128)(2,1)S(1)} %get-tuple-element.65.refs_2_), channel_id=1, source_target_pairs={{0,2},{1,3},{2,0},{3,1},{4,6},{5,7},{6,4},{7,5},{8,10},{9,11},{10,... | collective-permute-start | bytes 393224 | tf_op jit(solution)/shard_map/ppermute | solution.py:471
  37.2 8.1 %collective-permute-start.12 = (bf16[256,128]{1,0:T(8,128)(2,1)S(1)}, bf16[256,128]{1,0:T(8,128)(2,1)S(1)}, u32[]{:S(2)}, u32[]{:S(2)}) collective-permute-start(bf16[256,128]{1,0:T(8,128)(2,1)S(1)} %get-tuple-element.67.refs_2_), channel_id=1, source_target_pairs={{0,4},{1,5},{2,6},{3,7},{4,0},{5,1},{6,2},{7,3},{8,12},{9,13},{10,... | collective-permute-start | bytes 196616 | tf_op jit(solution)/shard_map/ppermute | solution.py:471
  51.4 7.2 %collective-permute-start.16 = (bf16[2,64,512]{2,1,0:T(8,128)(2,1)S(1)}, bf16[2,64,512]{2,1,0:T(8,128)(2,1)S(1)}, u32[]{:S(2)}, u32[]{:S(2)}) collective-permute-start(bf16[2,64,512]{2,1,0:T(8,128)(2,1)S(1)} %get-tuple-element.77.refs_2_), channel_id=1, source_target_pairs={{0,1},{1,0},{2,3},{3,2},{4,5},{5,4},{6,7},{7,6},{8,9},{9,8},{10,11... | collective-permute-start | bytes 393224 | tf_op jit(solution)/shard_map/ppermute | solution.py:471
  52.2 8.3 %collective-permute-start.21 = (bf16[1,256,256]{2,1,0:T(8,128)(2,1)S(1)}, bf16[1,256,256]{2,1,0:T(8,128)(2,1)S(1)}, u32[]{:S(2)}, u32[]{:S(2)}) collective-permute-start(bf16[1,256,256]{2,1,0:T(8,128)(2,1)S(1)} %get-tuple-element.82.refs_0_), channel_id=1, source_target_pairs={{0,4},{1,5},{2,6},{3,7},{4,0},{5,1},{6,2},{7,3},{8,12},{9,13},{10,... | collective-permute-start | bytes 393224 | tf_op jit(solution)/shard_map/ppermute | solution.py:471
  55.5 7.2 %collective-permute-start.20 = (bf16[2,128,256]{2,1,0:T(8,128)(2,1)S(1)}, bf16[2,128,256]{2,1,0:T(8,128)(2,1)S(1)}, u32[]{:S(2)}, u32[]{:S(2)}) collective-permute-start(bf16[2,128,256]{2,1,0:T(8,128)(2,1)S(1)} %shard_map.101.refs_2_.refs_0_), channel_id=1, source_target_pairs={{0,2},{1,3},{2,0},{3,1},{4,6},{5,7},{6,4},{7,5},{8,10},{9,11},{10,... | collective-permute-start | bytes 393224 | tf_op jit(solution)/shard_map/ppermute | solution.py:471
  57.6 12.9 %collective-permute-start.23 = (bf16[2,128,256]{2,1,0:T(8,128)(2,1)S(1)}, bf16[2,128,256]{2,1,0:T(8,128)(2,1)S(1)}, u32[]{:S(2)}, u32[]{:S(2)}) collective-permute-start(bf16[2,128,256]{2,1,0:T(8,128)(2,1)S(1)} %shard_map.100.refs_2_.refs_0_), channel_id=1, source_target_pairs={{0,4},{1,5},{2,6},{3,7},{4,0},{5,1},{6,2},{7,3},{8,12},{9,13},{10,... | collective-permute-start | bytes 393224 | tf_op jit(solution)/shard_map/ppermute | solution.py:471
  60.5 16.5 %collective-permute-start.25 = (bf16[2,256,256]{2,1,0:T(8,128)(2,1)S(1)}, bf16[2,256,256]{2,1,0:T(8,128)(2,1)S(1)}, u32[]{:S(2)}, u32[]{:S(2)}) collective-permute-start(bf16[2,256,256]{2,1,0:T(8,128)(2,1)S(1)} %shard_map.103.refs_2_.refs_0_), channel_id=1, source_target_pairs={{0,2},{1,3},{2,0},{3,1},{4,6},{5,7},{6,4},{7,5},{8,10},{9,11},{10,... | collective-permute-start | bytes 786440 | tf_op jit(solution)/shard_map/ppermute | solution.py:471
  62.8 13.4 %collective-permute-start.26 = (bf16[4,128,256]{2,1,0:T(8,128)(2,1)S(1)}, bf16[4,128,256]{2,1,0:T(8,128)(2,1)S(1)}, u32[]{:S(2)}, u32[]{:S(2)}) collective-permute-start(bf16[4,128,256]{2,1,0:T(8,128)(2,1)S(1)} %shard_map.104.refs_2_), channel_id=1, source_target_pairs={{0,1},{1,0},{2,3},{3,2},{4,5},{5,4},{6,7},{7,6},{8,9},{9,8},{10,11... | collective-permute-start | bytes 786440 | tf_op jit(solution)/shard_map/ppermute | solution.py:471
  64.4 8.8 %collective-permute-start.22 = (bf16[64,512]{1,0:T(8,128)(2,1)S(1)}, bf16[64,512]{1,0:T(8,128)(2,1)S(1)}, u32[]{:S(2)}, u32[]{:S(2)}) collective-permute-start(bf16[64,512]{1,0:T(8,128)(2,1)S(1)} %shard_map.105.refs_2_.refs_0_), channel_id=1, source_target_pairs={{0,4},{1,5},{2,6},{3,7},{4,0},{5,1},{6,2},{7,3},{8,12},{9,13},{10,... | collective-permute-start | bytes 196616 | tf_op jit(solution)/shard_map/ppermute | solution.py:471
  76.1 8.4 %collective-permute-start.30 = (bf16[4,128,256]{2,1,0:T(8,128)(2,1)S(1)}, bf16[4,128,256]{2,1,0:T(8,128)(2,1)S(1)}, u32[]{:S(2)}, u32[]{:S(2)}) collective-permute-start(bf16[4,128,256]{2,1,0:T(8,128)(2,1)S(1)} %shard_map.106.refs_2_.refs_0_), channel_id=1, source_target_pairs={{0,2},{1,3},{2,0},{3,1},{4,6},{5,7},{6,4},{7,5},{8,10},{9,11},{10,... | collective-permute-start | bytes 786440 | tf_op jit(solution)/shard_map/ppermute | solution.py:471
  76.9 8.3 %collective-permute-start.31 = (bf16[128,1024]{1,0:T(8,128)(2,1)S(1)}, bf16[128,1024]{1,0:T(8,128)(2,1)S(1)}, u32[]{:S(2)}, u32[]{:S(2)}) collective-permute-start(bf16[128,1024]{1,0:T(8,128)(2,1)S(1)} %shard_map.108.refs_2_), channel_id=1, source_target_pairs={{0,8},{8,0},{16,24},{24,16},{1,9},{9,1},{17,25},{25,17},{2,10},{10... | collective-permute-start | bytes 786440 | tf_op jit(solution)/shard_map/ppermute | solution.py:471
  77.0 14.8 %collective-permute-start.29 = (bf16[4,256,256]{2,1,0:T(8,128)(2,1)S(1)}, bf16[4,256,256]{2,1,0:T(8,128)(2,1)S(1)}, u32[]{:S(2)}, u32[]{:S(2)}) collective-permute-start(bf16[4,256,256]{2,1,0:T(8,128)(2,1)S(1)} %shard_map.109.refs_2_), channel_id=1, source_target_pairs={{0,1},{1,0},{2,3},{3,2},{4,5},{5,4},{6,7},{7,6},{8,9},{9,8},{10,11... | collective-permute-start | bytes 1572872 | tf_op jit(solution)/shard_map/ppermute | solution.py:471
  84.1 10.1 %collective-permute-start.28 = (bf16[2,64,512]{2,1,0:T(8,128)(2,1)S(1)}, bf16[2,64,512]{2,1,0:T(8,128)(2,1)S(1)}, u32[]{:S(2)}, u32[]{:S(2)}) collective-permute-start(bf16[2,64,512]{2,1,0:T(8,128)(2,1)S(1)} %shard_map.111.refs_2_.refs_0_), channel_id=1, source_target_pairs={{0,1},{1,0},{2,3},{3,2},{4,5},{5,4},{6,7},{7,6},{8,9},{9,8},{10,11... | collective-permute-start | bytes 393224 | tf_op jit(solution)/shard_map/ppermute | solution.py:471
  85.3 9.0 %collective-permute-start.34 = (bf16[128,1024]{1,0:T(8,128)(2,1)S(1)}, bf16[128,1024]{1,0:T(8,128)(2,1)S(1)}, u32[]{:S(2)}, u32[]{:S(2)}) collective-permute-start(bf16[128,1024]{1,0:T(8,128)(2,1)S(1)} %shard_map.114.refs_4_), channel_id=1, source_target_pairs={{0,16},{8,24},{16,0},{24,8},{1,17},{9,25},{17,1},{25,9},{2,18},{10... | collective-permute-start | bytes 786440 | tf_op jit(solution)/shard_map/ppermute | solution.py:471
  (14 other events, 84.0 us)

commit v4 on v3

--- a/solution.py
+++ b/solution.py
@@ -12,7 +12,7 @@
 BF16 = jnp.bfloat16
 MIB = 1024 * 1024
 COST_F = 1_000_000_000
-COST, COST_S, COST_W, COST_M = 4_000_000_000, 1_000_000_000, 4_000_000_000, 4_000_000_000
+COST, COST_S, COST_W, COST_M = 4_000_000_000, 3_000_000_000, 0, 8_000_000_000
 SMEM = pl.BlockSpec(memory_space=pltpu.SMEM)
 VMEM = pl.BlockSpec(memory_space=pltpu.VMEM)
 ANYWHERE = pl.BlockSpec(memory_space=pl.ANY)
@@ -629,10 +629,10 @@
     for _ in range(stages - 1):
         join("A", COST)
     for _ in range(stages - 1):
+        join("M")
+    for _ in range(stages - 1):
         weight_line()
     back([(1, 1)], (rows["C"], came_rows["C"]))
-    for _ in range(stages - 1):
-        join("M")
     weight_sum()
     weight_stack("col")
     join("A", COST_S)

time: 97.4 us -> 96.6 us (level)
  waiting for transfers between devices: 36.2 us -> 31.7 us
  starting transfers between devices: 46.1 us -> 50.5 us
    ppermute x35, waiting for transfers between devices: 36.2 us -> 31.7 us  [swap(): return lax.ppermute(v, axis, [(i, i ^ bit) for i in range(size)])]
    ppermute x35, starting transfers between devices: 46.1 us -> 50.5 us  [swap(): return lax.ppermute(v, axis, [(i, i ^ bit) for i in range(size)])]
  transfers between devices with their start and end apart: 35 -> 35, of which waited for: 18 -> 14; matrix products, arithmetic and copies ran while one was open for 0% -> 0% of each run, Pallas kernels for 12% -> 12%
where the time goes in v4:
time: 96.6 us; the launch traced here: 97.7 us
  starting transfers between devices  50.5 us (52%)
  waiting for transfers between devices  31.7 us (33%)
  Pallas kernels  13.9 us (14%)
  between operations  1.56 us (2%)
    ppermute x35, starting transfers between devices, swap(): return lax.ppermute(v, axis, [(i, i ^ bit) for i in range(size)])  50.5 us
    ppermute x35, waiting for transfers between devices, swap(): return lax.ppermute(v, axis, [(i, i ^ bit) for i in range(size)])  31.7 us
    pallas_call x35, Pallas kernels, call(): pl.pallas_call(run, out_shape=tuple(out_shape) if many else out_shape, in...  13.9 us
  transfers between devices with their start and end apart: 35, of which 14 were waited for; matrix products, arithmetic and copies ran while one was open for 0% of the time, Pallas kernels for 12%

profile of v4, /device:TPU:0, one launch (start us, length us, event | category | flops | bytes accessed | tf_op | source)
XLA Modules:
  0.0 97.7 jit_solution(8550744672323754388)
XLA Ops:
  1.2 2.6 %collective-permute-start.1 = (bf16[1024,128]{1,0:T(8,128)(2,1)}, bf16[1024,128]{1,0:T(8,128)(2,1)S(1)}, u32[]{:S(2)}, u32[]{:S(2)}) collective-permute-start(bf16[1024,128]{1,0:T(8,128)(2,1)} %refs_5_.1), channel_id=1, source_target_pairs={{0,16},{8,24},{16,0},{24,8},{1,17},{9,25},{17,1},{25,9},{2,18},{10... | collective-permute-start | bytes 786440 | tf_op jit(solution)/shard_map/ppermute | solution.py:471
  4.4 3.6 %shard_map.85 = (bf16[1024,1024]{1,0:T(8,128)(2,1)S(1)}, bf16[1024,1024]{1,0:T(8,128)(2,1)S(1)}, bf16[1024,128]{1,0:T(8,128)(2,1)S(1)}, bf16[1024,128]{1,0:T(8,128)(2,1)S(1)}) custom-call(s32[1]{0:T(128)} %bitcast.7.refs_0_, s32[1]{0:T(128)} %bitcast.1.refs_1_.refs_0_, s32[1]{0:T(128)} %bitcast.2.refs_2_.refs_0_, s32[2,96]{1,0:T(2,128)} %bitcast.9, ...), custom_call_target="tpu_custom_call" | custom-call | tf_op jit(solution)/shard_map/pallas_call | solution.py:28
  8.7 2.1 %collective-permute-done.1.refs_4_ = bf16[1024,128]{1,0:T(8,128)(2,1)S(1)} collective-permute-done((bf16[1024,128]{1,0:T(8,128)(2,1)}, bf16[1024,128]{1,0:T(8,128)(2,1)S(1)}, u32[]{:S(2)}, u32[]{:S(2)}) %collective-permute-start.1) | collective-permute-done | bytes 262176 | tf_op jit(solution)/shard_map/ppermute | solution.py:471
  10.9 1.9 %shard_map.86 = (bf16[1024,128]{1,0:T(8,128)(2,1)S(1)}, bf16[1024,128]{1,0:T(8,128)(2,1)S(1)}, f32[1024,128]{1,0:T(8,128)S(1)}, f32[1024,128]{1,0:T(8,128)S(1)}, f32[1024,128]{1,0:T(8,128)S(1)}) custom-call(bf16[1024,1024]{1,0:T(8,128)(2,1)S(1)} %get-tuple-element.44.refs_0_, bf16[1024,1024]{1,0:T(8,128)(2,1)S(1)} %get-tuple-element.45.refs_1_, ...), custom_call_target="tpu_custom_call" | custom-call | tf_op jit(solution)/shard_map/pallas_call | solution.py:28
  14.9 2.4 %collective-permute-done.2.refs_1_ = bf16[1024,128]{1,0:T(8,128)(2,1)S(1)} collective-permute-done((bf16[1024,128]{1,0:T(8,128)(2,1)S(1)}, bf16[1024,128]{1,0:T(8,128)(2,1)S(1)}, u32[]{:S(2)}, u32[]{:S(2)}) %collective-permute-start.2) | collective-permute-done | bytes 262176 | tf_op jit(solution)/shard_map/ppermute | solution.py:471
  24.0 2.4 %collective-permute-done.3.refs_1_ = bf16[512,128]{1,0:T(8,128)(2,1)S(1)} collective-permute-done((bf16[512,128]{1,0:T(8,128)(2,1)S(1)}, bf16[512,128]{1,0:T(8,128)(2,1)S(1)}, u32[]{:S(2)}, u32[]{:S(2)}) %collective-permute-start.3) | collective-permute-done | bytes 131104 | tf_op jit(solution)/shard_map/ppermute | solution.py:471
  29.6 3.7 %collective-permute-done.11.refs_1_ = bf16[1024,128]{1,0:T(8,128)(2,1)S(1)} collective-permute-done((bf16[1024,128]{1,0:T(8,128)(2,1)S(1)}, bf16[1024,128]{1,0:T(8,128)(2,1)S(1)}, u32[]{:S(2)}, u32[]{:S(2)}) %collective-permute-start.11) | collective-permute-done | bytes 262176 | tf_op jit(solution)/shard_map/ppermute | solution.py:471
  34.3 3.2 %collective-permute-start.9 = (bf16[256,128]{1,0:T(8,128)(2,1)S(1)}, bf16[256,128]{1,0:T(8,128)(2,1)S(1)}, u32[]{:S(2)}, u32[]{:S(2)}) collective-permute-start(bf16[256,128]{1,0:T(8,128)(2,1)S(1)} %get-tuple-element.62.refs_2_), channel_id=1, source_target_pairs={{0,4},{1,5},{2,6},{3,7},{4,0},{5,1},{6,2},{7,3},{8,12},{9,13},{10,... | collective-permute-start | bytes 196616 | tf_op jit(solution)/shard_map/ppermute | solution.py:471
  37.7 2.5 %collective-permute-done.9.refs_3_ = bf16[256,128]{1,0:T(8,128)(2,1)S(1)} collective-permute-done((bf16[256,128]{1,0:T(8,128)(2,1)S(1)}, bf16[256,128]{1,0:T(8,128)(2,1)S(1)}, u32[]{:S(2)}, u32[]{:S(2)}) %collective-permute-start.9) | collective-permute-done | bytes 65568 | tf_op jit(solution)/shard_map/ppermute | solution.py:471
  40.2 2.6 %collective-permute-start.14 = (bf16[256,128]{1,0:T(8,128)(2,1)S(1)}, bf16[256,128]{1,0:T(8,128)(2,1)S(1)}, u32[]{:S(2)}, u32[]{:S(2)}) collective-permute-start(bf16[256,128]{1,0:T(8,128)(2,1)S(1)} %get-tuple-element.70.refs_10_), channel_id=1, source_target_pairs={{0,4},{1,5},{2,6},{3,7},{4,0},{5,1},{6,2},{7,3},{8,12},{9,13},{10,... | collective-permute-start | bytes 196616 | tf_op jit(solution)/shard_map/ppermute | solution.py:471
  42.8 2.7 %collective-permute-done.12.refs_5_ = bf16[256,128]{1,0:T(8,128)(2,1)S(1)} collective-permute-done((bf16[256,128]{1,0:T(8,128)(2,1)S(1)}, bf16[256,128]{1,0:T(8,128)(2,1)S(1)}, u32[]{:S(2)}, u32[]{:S(2)}) %collective-permute-start.12) | collective-permute-done | bytes 65568 | tf_op jit(solution)/shard_map/ppermute | solution.py:471
  48.0 1.9 %collective-permute-start.17 = (bf16[1,128,256]{2,1,0:T(8,128)(2,1)S(1)}, bf16[1,128,256]{2,1,0:T(8,128)(2,1)S(1)}, u32[]{:S(2)}, u32[]{:S(2)}) collective-permute-start(bf16[1,128,256]{2,1,0:T(8,128)(2,1)S(1)} %get-tuple-element.78.refs_0_), channel_id=1, source_target_pairs={{0,4},{1,5},{2,6},{3,7},{4,0},{5,1},{6,2},{7,3},{8,12},{9,13},{10,... | collective-permute-start | bytes 196616 | tf_op jit(solution)/shard_map/ppermute | solution.py:471
  54.7 3.4 %collective-permute-start.20 = (bf16[2,128,256]{2,1,0:T(8,128)(2,1)S(1)}, bf16[2,128,256]{2,1,0:T(8,128)(2,1)S(1)}, u32[]{:S(2)}, u32[]{:S(2)}) collective-permute-start(bf16[2,128,256]{2,1,0:T(8,128)(2,1)S(1)} %shard_map.101.refs_2_.refs_0_), channel_id=1, source_target_pairs={{0,2},{1,3},{2,0},{3,1},{4,6},{5,7},{6,4},{7,5},{8,10},{9,11},{10,... | collective-permute-start | bytes 393224 | tf_op jit(solution)/shard_map/ppermute | solution.py:471
  58.1 3.6 %collective-permute-start.24 = (bf16[2,128,256]{2,1,0:T(8,128)(2,1)S(1)}, bf16[2,128,256]{2,1,0:T(8,128)(2,1)S(1)}, u32[]{:S(2)}, u32[]{:S(2)}) collective-permute-start(bf16[2,128,256]{2,1,0:T(8,128)(2,1)S(1)} %shard_map.100.refs_2_.refs_0_), channel_id=1, source_target_pairs={{0,4},{1,5},{2,6},{3,7},{4,0},{5,1},{6,2},{7,3},{8,12},{9,13},{10,... | collective-permute-start | bytes 393224 | tf_op jit(solution)/shard_map/ppermute | solution.py:471
  64.0 2.1 %collective-permute-done.19.refs_1_ = bf16[64,512]{1,0:T(8,128)(2,1)S(1)} collective-permute-done((bf16[64,512]{1,0:T(8,128)(2,1)S(1)}, bf16[64,512]{1,0:T(8,128)(2,1)S(1)}, u32[]{:S(2)}, u32[]{:S(2)}) %collective-permute-start.19) | collective-permute-done | bytes 65568 | tf_op jit(solution)/shard_map/ppermute | solution.py:471
  66.1 3.6 %collective-permute-start.22 = (bf16[64,512]{1,0:T(8,128)(2,1)S(1)}, bf16[64,512]{1,0:T(8,128)(2,1)S(1)}, u32[]{:S(2)}, u32[]{:S(2)}) collective-permute-start(bf16[64,512]{1,0:T(8,128)(2,1)S(1)} %shard_map.105.refs_2_.refs_0_), channel_id=1, source_target_pairs={{0,4},{1,5},{2,6},{3,7},{4,0},{5,1},{6,2},{7,3},{8,12},{9,13},{10,... | collective-permute-start | bytes 196616 | tf_op jit(solution)/shard_map/ppermute | solution.py:471
  69.7 2.7 %collective-permute-start.30 = (bf16[4,128,256]{2,1,0:T(8,128)(2,1)S(1)}, bf16[4,128,256]{2,1,0:T(8,128)(2,1)S(1)}, u32[]{:S(2)}, u32[]{:S(2)}) collective-permute-start(bf16[4,128,256]{2,1,0:T(8,128)(2,1)S(1)} %shard_map.106.refs_2_.refs_0_), channel_id=1, source_target_pairs={{0,2},{1,3},{2,0},{3,1},{4,6},{5,7},{6,4},{7,5},{8,10},{9,11},{10,... | collective-permute-start | bytes 786440 | tf_op jit(solution)/shard_map/ppermute | solution.py:471
  72.5 2.4 %collective-permute-start.29 = (bf16[4,256,256]{2,1,0:T(8,128)(2,1)S(1)}, bf16[4,256,256]{2,1,0:T(8,128)(2,1)S(1)}, u32[]{:S(2)}, u32[]{:S(2)}) collective-permute-start(bf16[4,256,256]{2,1,0:T(8,128)(2,1)S(1)} %shard_map.107.refs_2_), channel_id=1, source_target_pairs={{0,1},{1,0},{2,3},{3,2},{4,5},{5,4},{6,7},{7,6},{8,9},{9,8},{10,11... | collective-permute-start | bytes 1572872 | tf_op jit(solution)/shard_map/ppermute | solution.py:471
  76.6 3.3 %collective-permute-done.25.refs_1_ = f32[64,512]{1,0:T(8,128)S(1)} collective-permute-done((f32[64,512]{1,0:T(8,128)S(1)}, f32[64,512]{1,0:T(8,128)S(1)}, u32[]{:S(2)}, u32[]{:S(2)}) %collective-permute-start.25) | collective-permute-done | bytes 131104 | tf_op jit(solution)/shard_map/ppermute | solution.py:471
  80.0 2.0 %collective-permute-start.27 = (bf16[64,512]{1,0:T(8,128)(2,1)S(1)}, bf16[64,512]{1,0:T(8,128)(2,1)S(1)}, u32[]{:S(2)}, u32[]{:S(2)}) collective-permute-start(bf16[64,512]{1,0:T(8,128)(2,1)S(1)} %shard_map.110.refs_0_.refs_2_), channel_id=1, source_target_pairs={{0,16},{8,24},{16,0},{24,8},{1,17},{9,25},{17,1},{25,9},{2,18},{10... | collective-permute-start | bytes 196616 | tf_op jit(solution)/shard_map/ppermute | solution.py:471
  82.0 2.3 %collective-permute-done.27.refs_1_ = bf16[64,512]{1,0:T(8,128)(2,1)S(1)} collective-permute-done((bf16[64,512]{1,0:T(8,128)(2,1)S(1)}, bf16[64,512]{1,0:T(8,128)(2,1)S(1)}, u32[]{:S(2)}, u32[]{:S(2)}) %collective-permute-start.27) | collective-permute-done | bytes 65568 | tf_op jit(solution)/shard_map/ppermute | solution.py:471
  84.3 3.1 %collective-permute-start.28 = (bf16[2,64,512]{2,1,0:T(8,128)(2,1)S(1)}, bf16[2,64,512]{2,1,0:T(8,128)(2,1)S(1)}, u32[]{:S(2)}, u32[]{:S(2)}) collective-permute-start(bf16[2,64,512]{2,1,0:T(8,128)(2,1)S(1)} %shard_map.111.refs_2_.refs_0_), channel_id=1, source_target_pairs={{0,1},{1,0},{2,3},{3,2},{4,5},{5,4},{6,7},{7,6},{8,9},{9,8},{10,11... | collective-permute-start | bytes 393224 | tf_op jit(solution)/shard_map/ppermute | solution.py:471
  88.3 2.1 %collective-permute-start.34 = (bf16[128,1024]{1,0:T(8,128)(2,1)S(1)}, bf16[128,1024]{1,0:T(8,128)(2,1)S(1)}, u32[]{:S(2)}, u32[]{:S(2)}) collective-permute-start(bf16[128,1024]{1,0:T(8,128)(2,1)S(1)} %shard_map.114.refs_4_), channel_id=1, source_target_pairs={{0,16},{8,24},{16,0},{24,8},{1,17},{9,25},{17,1},{25,9},{2,18},{10... | collective-permute-start | bytes 786440 | tf_op jit(solution)/shard_map/ppermute | solution.py:471
  92.3 3.5 %collective-permute-done.34.refs_1_.refs_2_ = bf16[128,1024]{1,0:T(8,128)(2,1)S(1)} collective-permute-done((bf16[128,1024]{1,0:T(8,128)(2,1)S(1)}, bf16[128,1024]{1,0:T(8,128)(2,1)S(1)}, u32[]{:S(2)}, u32[]{:S(2)}) %collective-permute-start.34) | collective-permute-done | bytes 262176 | tf_op jit(solution)/shard_map/ppermute | solution.py:471
  (87 shorter events, 30.4 us)
Async XLA Ops:
  0.6 8.1 %collective-permute-start = (bf16[1024,128]{1,0:T(8,128)(2,1)}, bf16[1024,128]{1,0:T(8,128)(2,1)S(1)}, u32[]{:S(2)}, u32[]{:S(2)}) collective-permute-start(bf16[1024,128]{1,0:T(8,128)(2,1)} %refs_5_.1), channel_id=1, source_target_pairs={{0,8},{8,0},{16,24},{24,16},{1,9},{9,1},{17,25},{25,17},{2,10},{10... | collective-permute-start | bytes 786440 | tf_op jit(solution)/shard_map/ppermute | solution.py:471
  1.2 9.7 %collective-permute-start.1 = (bf16[1024,128]{1,0:T(8,128)(2,1)}, bf16[1024,128]{1,0:T(8,128)(2,1)S(1)}, u32[]{:S(2)}, u32[]{:S(2)}) collective-permute-start(bf16[1024,128]{1,0:T(8,128)(2,1)} %refs_5_.1), channel_id=1, source_target_pairs={{0,16},{8,24},{16,0},{24,8},{1,17},{9,25},{17,1},{25,9},{2,18},{10... | collective-permute-start | bytes 786440 | tf_op jit(solution)/shard_map/ppermute | solution.py:471
  8.0 9.2 %collective-permute-start.2 = (bf16[1024,128]{1,0:T(8,128)(2,1)S(1)}, bf16[1024,128]{1,0:T(8,128)(2,1)S(1)}, u32[]{:S(2)}, u32[]{:S(2)}) collective-permute-start(bf16[1024,128]{1,0:T(8,128)(2,1)S(1)} %get-tuple-element.48), channel_id=1, source_target_pairs={{0,1},{1,0},{2,3},{3,2},{4,5},{5,4},{6,7},{7,6},{8,9},{9,8},{10,11... | collective-permute-start | bytes 786440 | tf_op jit(solution)/shard_map/ppermute | solution.py:471
  8.7 8.6 %collective-permute-start.5 = (bf16[1024,128]{1,0:T(8,128)(2,1)S(1)}, bf16[1024,128]{1,0:T(8,128)(2,1)S(1)}, u32[]{:S(2)}, u32[]{:S(2)}) collective-permute-start(bf16[1024,128]{1,0:T(8,128)(2,1)S(1)} %copy-done.2), channel_id=1, source_target_pairs={{0,24},{8,16},{16,8},{24,0},{1,25},{9,17},{17,9},{25,1},{2,26},{10... | collective-permute-start | bytes 786440 | tf_op jit(solution)/shard_map/ppermute | solution.py:471
  12.7 10.2 %collective-permute-start.4 = (bf16[1024,128]{1,0:T(8,128)(2,1)S(1)}, bf16[1024,128]{1,0:T(8,128)(2,1)S(1)}, u32[]{:S(2)}, u32[]{:S(2)}) collective-permute-start(bf16[1024,128]{1,0:T(8,128)(2,1)S(1)} %get-tuple-element.52), channel_id=1, source_target_pairs={{0,1},{1,0},{2,3},{3,2},{4,5},{5,4},{6,7},{7,6},{8,9},{9,8},{10,11... | collective-permute-start | bytes 786440 | tf_op jit(solution)/shard_map/ppermute | solution.py:471
  14.5 14.0 %collective-permute-start.8 = (bf16[1024,128]{1,0:T(8,128)(2,1)S(1)}, bf16[1024,128]{1,0:T(8,128)(2,1)S(1)}, u32[]{:S(2)}, u32[]{:S(2)}) collective-permute-start(bf16[1024,128]{1,0:T(8,128)(2,1)S(1)} %get-tuple-element.59), channel_id=1, source_target_pairs={{0,1},{1,0},{2,3},{3,2},{4,5},{5,4},{6,7},{7,6},{8,9},{9,8},{10,11... | collective-permute-start | bytes 786440 | tf_op jit(solution)/shard_map/ppermute | solution.py:471
  18.6 14.8 %collective-permute-start.11 = (bf16[1024,128]{1,0:T(8,128)(2,1)S(1)}, bf16[1024,128]{1,0:T(8,128)(2,1)S(1)}, u32[]{:S(2)}, u32[]{:S(2)}) collective-permute-start(bf16[1024,128]{1,0:T(8,128)(2,1)S(1)} %get-tuple-element.64), channel_id=1, source_target_pairs={{0,1},{1,0},{2,3},{3,2},{4,5},{5,4},{6,7},{7,6},{8,9},{9,8},{10,11... | collective-permute-start | bytes 786440 | tf_op jit(solution)/shard_map/ppermute | solution.py:471
  22.9 6.6 %collective-permute-start.7 = (bf16[512,128]{1,0:T(8,128)(2,1)S(1)}, bf16[512,128]{1,0:T(8,128)(2,1)S(1)}, u32[]{:S(2)}, u32[]{:S(2)}) collective-permute-start(bf16[512,128]{1,0:T(8,128)(2,1)S(1)} %get-tuple-element.54.refs_2_), channel_id=1, source_target_pairs={{0,2},{1,3},{2,0},{3,1},{4,6},{5,7},{6,4},{7,5},{8,10},{9,11},{10,... | collective-permute-start | bytes 393224 | tf_op jit(solution)/shard_map/ppermute | solution.py:471
  26.4 7.0 %collective-permute-start.6 = (bf16[256,128]{1,0:T(8,128)(2,1)S(1)}, bf16[256,128]{1,0:T(8,128)(2,1)S(1)}, u32[]{:S(2)}, u32[]{:S(2)}) collective-permute-start(bf16[256,128]{1,0:T(8,128)(2,1)S(1)} %get-tuple-element.56.refs_2_), channel_id=1, source_target_pairs={{0,4},{1,5},{2,6},{3,7},{4,0},{5,1},{6,2},{7,3},{8,12},{9,13},{10,... | collective-permute-start | bytes 196616 | tf_op jit(solution)/shard_map/ppermute | solution.py:471
  28.6 9.0 %collective-permute-start.10 = (bf16[512,128]{1,0:T(8,128)(2,1)S(1)}, bf16[512,128]{1,0:T(8,128)(2,1)S(1)}, u32[]{:S(2)}, u32[]{:S(2)}) collective-permute-start(bf16[512,128]{1,0:T(8,128)(2,1)S(1)} %get-tuple-element.60.refs_2_), channel_id=1, source_target_pairs={{0,2},{1,3},{2,0},{3,1},{4,6},{5,7},{6,4},{7,5},{8,10},{9,11},{10,... | collective-permute-start | bytes 393224 | tf_op jit(solution)/shard_map/ppermute | solution.py:471
  33.4 6.8 %collective-permute-start.13 = (bf16[512,128]{1,0:T(8,128)(2,1)S(1)}, bf16[512,128]{1,0:T(8,128)(2,1)S(1)}, u32[]{:S(2)}, u32[]{:S(2)}) collective-permute-start(bf16[512,128]{1,0:T(8,128)(2,1)S(1)} %get-tuple-element.65.refs_2_), channel_id=1, source_target_pairs={{0,2},{1,3},{2,0},{3,1},{4,6},{5,7},{6,4},{7,5},{8,10},{9,11},{10,... | collective-permute-start | bytes 393224 | tf_op jit(solution)/shard_map/ppermute | solution.py:471
  37.6 7.9 %collective-permute-start.12 = (bf16[256,128]{1,0:T(8,128)(2,1)S(1)}, bf16[256,128]{1,0:T(8,128)(2,1)S(1)}, u32[]{:S(2)}, u32[]{:S(2)}) collective-permute-start(bf16[256,128]{1,0:T(8,128)(2,1)S(1)} %get-tuple-element.67.refs_2_), channel_id=1, source_target_pairs={{0,4},{1,5},{2,6},{3,7},{4,0},{5,1},{6,2},{7,3},{8,12},{9,13},{10,... | collective-permute-start | bytes 196616 | tf_op jit(solution)/shard_map/ppermute | solution.py:471
  48.0 6.7 %collective-permute-start.17 = (bf16[1,128,256]{2,1,0:T(8,128)(2,1)S(1)}, bf16[1,128,256]{2,1,0:T(8,128)(2,1)S(1)}, u32[]{:S(2)}, u32[]{:S(2)}) collective-permute-start(bf16[1,128,256]{2,1,0:T(8,128)(2,1)S(1)} %get-tuple-element.78.refs_0_), channel_id=1, source_target_pairs={{0,4},{1,5},{2,6},{3,7},{4,0},{5,1},{6,2},{7,3},{8,12},{9,13},{10,... | collective-permute-start | bytes 196616 | tf_op jit(solution)/shard_map/ppermute | solution.py:471
  51.0 10.7 %collective-permute-start.16 = (bf16[2,64,512]{2,1,0:T(8,128)(2,1)S(1)}, bf16[2,64,512]{2,1,0:T(8,128)(2,1)S(1)}, u32[]{:S(2)}, u32[]{:S(2)}) collective-permute-start(bf16[2,64,512]{2,1,0:T(8,128)(2,1)S(1)} %get-tuple-element.77.refs_2_), channel_id=1, source_target_pairs={{0,1},{1,0},{2,3},{3,2},{4,5},{5,4},{6,7},{7,6},{8,9},{9,8},{10,11... | collective-permute-start | bytes 393224 | tf_op jit(solution)/shard_map/ppermute | solution.py:471
  52.1 9.8 %collective-permute-start.21 = (bf16[1,256,256]{2,1,0:T(8,128)(2,1)S(1)}, bf16[1,256,256]{2,1,0:T(8,128)(2,1)S(1)}, u32[]{:S(2)}, u32[]{:S(2)}) collective-permute-start(bf16[1,256,256]{2,1,0:T(8,128)(2,1)S(1)} %get-tuple-element.82.refs_0_), channel_id=1, source_target_pairs={{0,4},{1,5},{2,6},{3,7},{4,0},{5,1},{6,2},{7,3},{8,12},{9,13},{10,... | collective-permute-start | bytes 393224 | tf_op jit(solution)/shard_map/ppermute | solution.py:471
  54.7 7.8 %collective-permute-start.20 = (bf16[2,128,256]{2,1,0:T(8,128)(2,1)S(1)}, bf16[2,128,256]{2,1,0:T(8,128)(2,1)S(1)}, u32[]{:S(2)}, u32[]{:S(2)}) collective-permute-start(bf16[2,128,256]{2,1,0:T(8,128)(2,1)S(1)} %shard_map.101.refs_2_.refs_0_), channel_id=1, source_target_pairs={{0,2},{1,3},{2,0},{3,1},{4,6},{5,7},{6,4},{7,5},{8,10},{9,11},{10,... | collective-permute-start | bytes 393224 | tf_op jit(solution)/shard_map/ppermute | solution.py:471
  58.1 11.6 %collective-permute-start.24 = (bf16[2,128,256]{2,1,0:T(8,128)(2,1)S(1)}, bf16[2,128,256]{2,1,0:T(8,128)(2,1)S(1)}, u32[]{:S(2)}, u32[]{:S(2)}) collective-permute-start(bf16[2,128,256]{2,1,0:T(8,128)(2,1)S(1)} %shard_map.100.refs_2_.refs_0_), channel_id=1, source_target_pairs={{0,4},{1,5},{2,6},{3,7},{4,0},{5,1},{6,2},{7,3},{8,12},{9,13},{10,... | collective-permute-start | bytes 393224 | tf_op jit(solution)/shard_map/ppermute | solution.py:471
  61.8 10.6 %collective-permute-start.23 = (bf16[2,256,256]{2,1,0:T(8,128)(2,1)S(1)}, bf16[2,256,256]{2,1,0:T(8,128)(2,1)S(1)}, u32[]{:S(2)}, u32[]{:S(2)}) collective-permute-start(bf16[2,256,256]{2,1,0:T(8,128)(2,1)S(1)} %shard_map.103.refs_2_.refs_0_), channel_id=1, source_target_pairs={{0,2},{1,3},{2,0},{3,1},{4,6},{5,7},{6,4},{7,5},{8,10},{9,11},{10,... | collective-permute-start | bytes 786440 | tf_op jit(solution)/shard_map/ppermute | solution.py:471
  62.6 13.3 %collective-permute-start.26 = (bf16[4,128,256]{2,1,0:T(8,128)(2,1)S(1)}, bf16[4,128,256]{2,1,0:T(8,128)(2,1)S(1)}, u32[]{:S(2)}, u32[]{:S(2)}) collective-permute-start(bf16[4,128,256]{2,1,0:T(8,128)(2,1)S(1)} %shard_map.104.refs_2_), channel_id=1, source_target_pairs={{0,1},{1,0},{2,3},{3,2},{4,5},{5,4},{6,7},{7,6},{8,9},{9,8},{10,11... | collective-permute-start | bytes 786440 | tf_op jit(solution)/shard_map/ppermute | solution.py:471
  66.1 8.8 %collective-permute-start.22 = (bf16[64,512]{1,0:T(8,128)(2,1)S(1)}, bf16[64,512]{1,0:T(8,128)(2,1)S(1)}, u32[]{:S(2)}, u32[]{:S(2)}) collective-permute-start(bf16[64,512]{1,0:T(8,128)(2,1)S(1)} %shard_map.105.refs_2_.refs_0_), channel_id=1, source_target_pairs={{0,4},{1,5},{2,6},{3,7},{4,0},{5,1},{6,2},{7,3},{8,12},{9,13},{10,... | collective-permute-start | bytes 196616 | tf_op jit(solution)/shard_map/ppermute | solution.py:471
  69.7 17.7 %collective-permute-start.30 = (bf16[4,128,256]{2,1,0:T(8,128)(2,1)S(1)}, bf16[4,128,256]{2,1,0:T(8,128)(2,1)S(1)}, u32[]{:S(2)}, u32[]{:S(2)}) collective-permute-start(bf16[4,128,256]{2,1,0:T(8,128)(2,1)S(1)} %shard_map.106.refs_2_.refs_0_), channel_id=1, source_target_pairs={{0,2},{1,3},{2,0},{3,1},{4,6},{5,7},{6,4},{7,5},{8,10},{9,11},{10,... | collective-permute-start | bytes 786440 | tf_op jit(solution)/shard_map/ppermute | solution.py:471
  72.5 17.9 %collective-permute-start.29 = (bf16[4,256,256]{2,1,0:T(8,128)(2,1)S(1)}, bf16[4,256,256]{2,1,0:T(8,128)(2,1)S(1)}, u32[]{:S(2)}, u32[]{:S(2)}) collective-permute-start(bf16[4,256,256]{2,1,0:T(8,128)(2,1)S(1)} %shard_map.107.refs_2_), channel_id=1, source_target_pairs={{0,1},{1,0},{2,3},{3,2},{4,5},{5,4},{6,7},{7,6},{8,9},{9,8},{10,11... | collective-permute-start | bytes 1572872 | tf_op jit(solution)/shard_map/ppermute | solution.py:471
  84.3 7.4 %collective-permute-start.28 = (bf16[2,64,512]{2,1,0:T(8,128)(2,1)S(1)}, bf16[2,64,512]{2,1,0:T(8,128)(2,1)S(1)}, u32[]{:S(2)}, u32[]{:S(2)}) collective-permute-start(bf16[2,64,512]{2,1,0:T(8,128)(2,1)S(1)} %shard_map.111.refs_2_.refs_0_), channel_id=1, source_target_pairs={{0,1},{1,0},{2,3},{3,2},{4,5},{5,4},{6,7},{7,6},{8,9},{9,8},{10,11... | collective-permute-start | bytes 393224 | tf_op jit(solution)/shard_map/ppermute | solution.py:471
  88.3 7.5 %collective-permute-start.34 = (bf16[128,1024]{1,0:T(8,128)(2,1)S(1)}, bf16[128,1024]{1,0:T(8,128)(2,1)S(1)}, u32[]{:S(2)}, u32[]{:S(2)}) collective-permute-start(bf16[128,1024]{1,0:T(8,128)(2,1)S(1)} %shard_map.114.refs_4_), channel_id=1, source_target_pairs={{0,16},{8,24},{16,0},{24,8},{1,17},{9,25},{17,1},{25,9},{2,18},{10... | collective-permute-start | bytes 786440 | tf_op jit(solution)/shard_map/ppermute | solution.py:471
  (14 other events, 84.8 us)

commit v5 on v4

--- a/solution.py
+++ b/solution.py
@@ -11,8 +11,8 @@
 F32 = jnp.float32
 BF16 = jnp.bfloat16
 MIB = 1024 * 1024
-COST_F = 1_000_000_000
-COST, COST_S, COST_W, COST_M = 4_000_000_000, 3_000_000_000, 0, 8_000_000_000
+COST_F, COST_U = 1_000_000_000, 2_000_000_000
+COST, COST_S, COST_W, COST_M = 4_000_000_000, 2_000_000_000, 0, 2_000_000_000
 SMEM = pl.BlockSpec(memory_space=pltpu.SMEM)
 VMEM = pl.BlockSpec(memory_space=pltpu.VMEM)
 ANYWHERE = pl.BlockSpec(memory_space=pl.ANY)
@@ -507,11 +507,9 @@
     last = weight_rows
     for turn, i in enumerate(turns):
         before = [last]
-        if stages == 2 and turn == 5:
-            before.append(cames[0])
-        if stages == 2 and turn == 7:
-            before.append(cames[1])
-        cost = COST_F if i in (1, 2) and done[i] == 0 else 0
+        if stages == 2 and turn == 6:
+            before.extend(cames[:2])
+        cost = COST_F if i in (1, 2) and done[i] == 0 else COST_U if turn == 6 else 0
         keeps[i], last = halved(keeps[i], cames[i], before, cost)
         cames[i] = swap(last, "col", 2 << done[i])
         done[i] += 1
@@ -633,11 +631,11 @@
     for _ in range(stages - 1):
         weight_line()
     back([(1, 1)], (rows["C"], came_rows["C"]))
-    weight_sum()
-    weight_stack("col")
     join("A", COST_S)
     back([(1, 0)], (rows["A"],))
     send_parts(1)
+    weight_sum()
+    weight_stack("col")
     back([(0, 1), (0, 0)], (rows["M"], came_rows["M"]), COST_M)
     weight_stack("row")
     send_parts(0)

time: 96.6 us -> 103 us (1.066)
  waiting for transfers between devices: 31.7 us -> 46 us
  starting transfers between devices: 50.5 us -> 41.7 us
    ppermute x35, waiting for transfers between devices: 31.7 us -> 46 us  [swap(): return lax.ppermute(v, axis, [(i, i ^ bit) for i in range(size)])]
    ppermute x35, starting transfers between devices: 50.5 us -> 41.7 us  [swap(): return lax.ppermute(v, axis, [(i, i ^ bit) for i in range(size)])]
  transfers between devices with their start and end apart: 35 -> 35, of which waited for: 14 -> 19; matrix products, arithmetic and copies ran while one was open for 0% -> 0% of each run, Pallas kernels for 12% -> 11%
where the time goes in v5:
time: 103 us
  waiting for transfers between devices  46 us (45%)
  starting transfers between devices  41.7 us (40%)
  Pallas kernels  13.9 us (13%)
  between operations  1.55 us (2%)
    ppermute x35, waiting for transfers between devices, swap(): return lax.ppermute(v, axis, [(i, i ^ bit) for i in range(size)])  46 us
    ppermute x35, starting transfers between devices, swap(): return lax.ppermute(v, axis, [(i, i ^ bit) for i in range(size)])  41.7 us
    pallas_call x35, Pallas kernels, call(): pl.pallas_call(run, out_shape=tuple(out_shape) if many else out_shape, in...  13.9 us
  transfers between devices with their start and end apart: 35, of which 19 were waited for; matrix products, arithmetic and copies ran while one was open for 0% of the time, Pallas kernels for 11%

profile of v5, /device:TPU:0, one launch (start us, length us, event | category | flops | bytes accessed | tf_op | source)
XLA Modules:
  0.0 103.2 jit_solution(2671338839940683593)
XLA Ops:
  1.2 2.6 %collective-permute-start.1 = (bf16[1024,128]{1,0:T(8,128)(2,1)}, bf16[1024,128]{1,0:T(8,128)(2,1)S(1)}, u32[]{:S(2)}, u32[]{:S(2)}) collective-permute-start(bf16[1024,128]{1,0:T(8,128)(2,1)} %refs_5_.1), channel_id=1, source_target_pairs={{0,16},{8,24},{16,0},{24,8},{1,17},{9,25},{17,1},{25,9},{2,18},{10... | collective-permute-start | bytes 786440 | tf_op jit(solution)/shard_map/ppermute | solution.py:471
  4.4 3.6 %shard_map.85 = (bf16[1024,1024]{1,0:T(8,128)(2,1)S(1)}, bf16[1024,1024]{1,0:T(8,128)(2,1)S(1)}, bf16[1024,128]{1,0:T(8,128)(2,1)S(1)}, bf16[1024,128]{1,0:T(8,128)(2,1)S(1)}) custom-call(s32[1]{0:T(128)} %bitcast.7.refs_0_, s32[1]{0:T(128)} %bitcast.1.refs_1_.refs_0_, s32[1]{0:T(128)} %bitcast.2.refs_2_.refs_0_, s32[2,96]{1,0:T(2,128)} %bitcast.9, ...), custom_call_target="tpu_custom_call" | custom-call | tf_op jit(solution)/shard_map/pallas_call | solution.py:28
  9.0 1.8 %collective-permute-done.1.refs_4_ = bf16[1024,128]{1,0:T(8,128)(2,1)S(1)} collective-permute-done((bf16[1024,128]{1,0:T(8,128)(2,1)}, bf16[1024,128]{1,0:T(8,128)(2,1)S(1)}, u32[]{:S(2)}, u32[]{:S(2)}) %collective-permute-start.1) | collective-permute-done | bytes 262176 | tf_op jit(solution)/shard_map/ppermute | solution.py:471
  10.9 1.9 %shard_map.86 = (bf16[1024,128]{1,0:T(8,128)(2,1)S(1)}, bf16[1024,128]{1,0:T(8,128)(2,1)S(1)}, f32[1024,128]{1,0:T(8,128)S(1)}, f32[1024,128]{1,0:T(8,128)S(1)}, f32[1024,128]{1,0:T(8,128)S(1)}) custom-call(bf16[1024,1024]{1,0:T(8,128)(2,1)S(1)} %get-tuple-element.44.refs_0_, bf16[1024,1024]{1,0:T(8,128)(2,1)S(1)} %get-tuple-element.45.refs_1_, ...), custom_call_target="tpu_custom_call" | custom-call | tf_op jit(solution)/shard_map/pallas_call | solution.py:28
  12.7 1.8 %collective-permute-start.4 = (bf16[1024,128]{1,0:T(8,128)(2,1)S(1)}, bf16[1024,128]{1,0:T(8,128)(2,1)S(1)}, u32[]{:S(2)}, u32[]{:S(2)}) collective-permute-start(bf16[1024,128]{1,0:T(8,128)(2,1)S(1)} %get-tuple-element.52), channel_id=1, source_target_pairs={{0,1},{1,0},{2,3},{3,2},{4,5},{5,4},{6,7},{7,6},{8,9},{9,8},{10,11... | collective-permute-start | bytes 786440 | tf_op jit(solution)/shard_map/ppermute | solution.py:471
  14.9 2.1 %collective-permute-done.2.refs_1_ = bf16[1024,128]{1,0:T(8,128)(2,1)S(1)} collective-permute-done((bf16[1024,128]{1,0:T(8,128)(2,1)S(1)}, bf16[1024,128]{1,0:T(8,128)(2,1)S(1)}, u32[]{:S(2)}, u32[]{:S(2)}) %collective-permute-start.2) | collective-permute-done | bytes 262176 | tf_op jit(solution)/shard_map/ppermute | solution.py:471
  24.3 3.9 %collective-permute-done.8.refs_1_ = bf16[1024,128]{1,0:T(8,128)(2,1)S(1)} collective-permute-done((bf16[1024,128]{1,0:T(8,128)(2,1)S(1)}, bf16[1024,128]{1,0:T(8,128)(2,1)S(1)}, u32[]{:S(2)}, u32[]{:S(2)}) %collective-permute-start.8) | collective-permute-done | bytes 262176 | tf_op jit(solution)/shard_map/ppermute | solution.py:471
  29.9 2.3 %collective-permute-start.6 = (bf16[256,128]{1,0:T(8,128)(2,1)S(1)}, bf16[256,128]{1,0:T(8,128)(2,1)S(1)}, u32[]{:S(2)}, u32[]{:S(2)}) collective-permute-start(bf16[256,128]{1,0:T(8,128)(2,1)S(1)} %get-tuple-element.56.refs_2_), channel_id=1, source_target_pairs={{0,4},{1,5},{2,6},{3,7},{4,0},{5,1},{6,2},{7,3},{8,12},{9,13},{10,... | collective-permute-start | bytes 196616 | tf_op jit(solution)/shard_map/ppermute | solution.py:471
  33.0 1.8 %collective-permute-start.13 = (bf16[512,128]{1,0:T(8,128)(2,1)S(1)}, bf16[512,128]{1,0:T(8,128)(2,1)S(1)}, u32[]{:S(2)}, u32[]{:S(2)}) collective-permute-start(bf16[512,128]{1,0:T(8,128)(2,1)S(1)} %get-tuple-element.65.refs_2_), channel_id=1, source_target_pairs={{0,2},{1,3},{2,0},{3,1},{4,6},{5,7},{6,4},{7,5},{8,10},{9,11},{10,... | collective-permute-start | bytes 393224 | tf_op jit(solution)/shard_map/ppermute | solution.py:471
  35.8 2.3 %collective-permute-done.9.refs_4_.refs_3_ = bf16[256,128]{1,0:T(8,128)(2,1)S(1)} collective-permute-done((bf16[256,128]{1,0:T(8,128)(2,1)S(1)}, bf16[256,128]{1,0:T(8,128)(2,1)S(1)}, u32[]{:S(2)}, u32[]{:S(2)}) %collective-permute-start.9) | collective-permute-done | bytes 65568 | tf_op jit(solution)/shard_map/ppermute | solution.py:471
  39.4 2.1 %collective-permute-start.14 = (bf16[256,128]{1,0:T(8,128)(2,1)S(1)}, bf16[256,128]{1,0:T(8,128)(2,1)S(1)}, u32[]{:S(2)}, u32[]{:S(2)}) collective-permute-start(bf16[256,128]{1,0:T(8,128)(2,1)S(1)} %get-tuple-element.70.refs_10_), channel_id=1, source_target_pairs={{0,4},{1,5},{2,6},{3,7},{4,0},{5,1},{6,2},{7,3},{8,12},{9,13},{10,... | collective-permute-start | bytes 196616 | tf_op jit(solution)/shard_map/ppermute | solution.py:471
  41.5 4.1 %collective-permute-done.12.refs_5_ = bf16[256,128]{1,0:T(8,128)(2,1)S(1)} collective-permute-done((bf16[256,128]{1,0:T(8,128)(2,1)S(1)}, bf16[256,128]{1,0:T(8,128)(2,1)S(1)}, u32[]{:S(2)}, u32[]{:S(2)}) %collective-permute-start.12) | collective-permute-done | bytes 65568 | tf_op jit(solution)/shard_map/ppermute | solution.py:471
  48.6 1.8 %collective-permute-start.18 = (bf16[1,128,256]{2,1,0:T(8,128)(2,1)S(1)}, bf16[1,128,256]{2,1,0:T(8,128)(2,1)S(1)}, u32[]{:S(2)}, u32[]{:S(2)}) collective-permute-start(bf16[1,128,256]{2,1,0:T(8,128)(2,1)S(1)} %get-tuple-element.79.refs_0_), channel_id=1, source_target_pairs={{0,1},{1,0},{2,3},{3,2},{4,5},{5,4},{6,7},{7,6},{8,9},{9,8},{10,11... | collective-permute-start | bytes 196616 | tf_op jit(solution)/shard_map/ppermute | solution.py:471
  56.9 1.8 %collective-permute-start.19 = (bf16[64,512]{1,0:T(8,128)(2,1)S(1)}, bf16[64,512]{1,0:T(8,128)(2,1)S(1)}, u32[]{:S(2)}, u32[]{:S(2)}) collective-permute-start(bf16[64,512]{1,0:T(8,128)(2,1)S(1)} %get-tuple-element.81), channel_id=1, source_target_pairs={{0,16},{8,24},{16,0},{24,8},{1,17},{9,25},{17,1},{25,9},{2,18},{10... | collective-permute-start | bytes 196616 | tf_op jit(solution)/shard_map/ppermute | solution.py:471
  58.7 3.9 %collective-permute-done.21.refs_1_ = bf16[1,256,256]{2,1,0:T(8,128)(2,1)S(1)} collective-permute-done((bf16[1,256,256]{2,1,0:T(8,128)(2,1)S(1)}, bf16[1,256,256]{2,1,0:T(8,128)(2,1)S(1)}, u32[]{:S(2)}, u32[]{:S(2)}) %collective-permute-start.21) | collective-permute-done | bytes 131104 | tf_op jit(solution)/shard_map/ppermute | solution.py:471
  62.7 2.5 %collective-permute-start.27 = (bf16[4,128,256]{2,1,0:T(8,128)(2,1)S(1)}, bf16[4,128,256]{2,1,0:T(8,128)(2,1)S(1)}, u32[]{:S(2)}, u32[]{:S(2)}) collective-permute-start(bf16[4,128,256]{2,1,0:T(8,128)(2,1)S(1)} %shard_map.104.refs_2_), channel_id=1, source_target_pairs={{0,1},{1,0},{2,3},{3,2},{4,5},{5,4},{6,7},{7,6},{8,9},{9,8},{10,11... | collective-permute-start | bytes 786440 | tf_op jit(solution)/shard_map/ppermute | solution.py:471
  66.8 4.8 %collective-permute-done.23.refs_1_ = bf16[2,256,256]{2,1,0:T(8,128)(2,1)S(1)} collective-permute-done((bf16[2,256,256]{2,1,0:T(8,128)(2,1)S(1)}, bf16[2,256,256]{2,1,0:T(8,128)(2,1)S(1)}, u32[]{:S(2)}, u32[]{:S(2)}) %collective-permute-start.23) | collective-permute-done | bytes 262176 | tf_op jit(solution)/shard_map/ppermute | solution.py:471
  71.8 3.3 %collective-permute-start.22 = (bf16[64,512]{1,0:T(8,128)(2,1)S(1)}, bf16[64,512]{1,0:T(8,128)(2,1)S(1)}, u32[]{:S(2)}, u32[]{:S(2)}) collective-permute-start(bf16[64,512]{1,0:T(8,128)(2,1)S(1)} %shard_map.105.refs_2_.refs_0_), channel_id=1, source_target_pairs={{0,4},{1,5},{2,6},{3,7},{4,0},{5,1},{6,2},{7,3},{8,12},{9,13},{10,... | collective-permute-start | bytes 196616 | tf_op jit(solution)/shard_map/ppermute | solution.py:471
  75.1 3.3 %collective-permute-done.22.refs_1_ = bf16[64,512]{1,0:T(8,128)(2,1)S(1)} collective-permute-done((bf16[64,512]{1,0:T(8,128)(2,1)S(1)}, bf16[64,512]{1,0:T(8,128)(2,1)S(1)}, u32[]{:S(2)}, u32[]{:S(2)}) %collective-permute-start.22) | collective-permute-done | bytes 65568 | tf_op jit(solution)/shard_map/ppermute | solution.py:471
  79.3 4.6 %collective-permute-start.25 = (f32[64,512]{1,0:T(8,128)S(1)}, f32[64,512]{1,0:T(8,128)S(1)}, u32[]{:S(2)}, u32[]{:S(2)}) collective-permute-start(f32[64,512]{1,0:T(8,128)S(1)} %shard_map.108.refs_4_.refs_0_), channel_id=1, source_target_pairs={{0,2},{1,3},{2,0},{3,1},{4,6},{5,7},{6,4},{7,5},{8,10},{9,11},{10,... | collective-permute-start | bytes 393224 | tf_op jit(solution)/shard_map/ppermute | solution.py:471
  84.8 3.1 %collective-permute-done.25.refs_1_ = f32[64,512]{1,0:T(8,128)S(1)} collective-permute-done((f32[64,512]{1,0:T(8,128)S(1)}, f32[64,512]{1,0:T(8,128)S(1)}, u32[]{:S(2)}, u32[]{:S(2)}) %collective-permute-start.25) | collective-permute-done | bytes 131104 | tf_op jit(solution)/shard_map/ppermute | solution.py:471
  88.2 6.4 %collective-permute-done.29.refs_1_ = bf16[64,512]{1,0:T(8,128)(2,1)S(1)} collective-permute-done((bf16[64,512]{1,0:T(8,128)(2,1)S(1)}, bf16[64,512]{1,0:T(8,128)(2,1)S(1)}, u32[]{:S(2)}, u32[]{:S(2)}) %collective-permute-start.29) | collective-permute-done | bytes 65568 | tf_op jit(solution)/shard_map/ppermute | solution.py:471
  94.6 1.7 %collective-permute-start.30 = (bf16[2,64,512]{2,1,0:T(8,128)(2,1)S(1)}, bf16[2,64,512]{2,1,0:T(8,128)(2,1)S(1)}, u32[]{:S(2)}, u32[]{:S(2)}) collective-permute-start(bf16[2,64,512]{2,1,0:T(8,128)(2,1)S(1)} %shard_map.114.refs_4_.refs_0_), channel_id=1, source_target_pairs={{0,1},{1,0},{2,3},{3,2},{4,5},{5,4},{6,7},{7,6},{8,9},{9,8},{10,11... | collective-permute-start | bytes 393224 | tf_op jit(solution)/shard_map/ppermute | solution.py:471
  97.7 1.9 %collective-permute-done.30.refs_1_ = bf16[2,64,512]{2,1,0:T(8,128)(2,1)S(1)} collective-permute-done((bf16[2,64,512]{2,1,0:T(8,128)(2,1)S(1)}, bf16[2,64,512]{2,1,0:T(8,128)(2,1)S(1)}, u32[]{:S(2)}, u32[]{:S(2)}) %collective-permute-start.30) | collective-permute-done | bytes 131104 | tf_op jit(solution)/shard_map/ppermute | solution.py:471
  (87 shorter events, 32.3 us)
Async XLA Ops:
  0.6 8.4 %collective-permute-start = (bf16[1024,128]{1,0:T(8,128)(2,1)}, bf16[1024,128]{1,0:T(8,128)(2,1)S(1)}, u32[]{:S(2)}, u32[]{:S(2)}) collective-permute-start(bf16[1024,128]{1,0:T(8,128)(2,1)} %refs_5_.1), channel_id=1, source_target_pairs={{0,8},{8,0},{16,24},{24,16},{1,9},{9,1},{17,25},{25,17},{2,10},{10... | collective-permute-start | bytes 786440 | tf_op jit(solution)/shard_map/ppermute | solution.py:471
  1.2 9.7 %collective-permute-start.1 = (bf16[1024,128]{1,0:T(8,128)(2,1)}, bf16[1024,128]{1,0:T(8,128)(2,1)S(1)}, u32[]{:S(2)}, u32[]{:S(2)}) collective-permute-start(bf16[1024,128]{1,0:T(8,128)(2,1)} %refs_5_.1), channel_id=1, source_target_pairs={{0,16},{8,24},{16,0},{24,8},{1,17},{9,25},{17,1},{25,9},{2,18},{10... | collective-permute-start | bytes 786440 | tf_op jit(solution)/shard_map/ppermute | solution.py:471
  8.0 8.9 %collective-permute-start.2 = (bf16[1024,128]{1,0:T(8,128)(2,1)S(1)}, bf16[1024,128]{1,0:T(8,128)(2,1)S(1)}, u32[]{:S(2)}, u32[]{:S(2)}) collective-permute-start(bf16[1024,128]{1,0:T(8,128)(2,1)S(1)} %get-tuple-element.48), channel_id=1, source_target_pairs={{0,1},{1,0},{2,3},{3,2},{4,5},{5,4},{6,7},{7,6},{8,9},{9,8},{10,11... | collective-permute-start | bytes 786440 | tf_op jit(solution)/shard_map/ppermute | solution.py:471
  8.7 9.9 %collective-permute-start.5 = (bf16[1024,128]{1,0:T(8,128)(2,1)S(1)}, bf16[1024,128]{1,0:T(8,128)(2,1)S(1)}, u32[]{:S(2)}, u32[]{:S(2)}) collective-permute-start(bf16[1024,128]{1,0:T(8,128)(2,1)S(1)} %copy-done.2), channel_id=1, source_target_pairs={{0,24},{8,16},{16,8},{24,0},{1,25},{9,17},{17,9},{25,1},{2,26},{10... | collective-permute-start | bytes 786440 | tf_op jit(solution)/shard_map/ppermute | solution.py:471
  12.7 9.9 %collective-permute-start.4 = (bf16[1024,128]{1,0:T(8,128)(2,1)S(1)}, bf16[1024,128]{1,0:T(8,128)(2,1)S(1)}, u32[]{:S(2)}, u32[]{:S(2)}) collective-permute-start(bf16[1024,128]{1,0:T(8,128)(2,1)S(1)} %get-tuple-element.52), channel_id=1, source_target_pairs={{0,1},{1,0},{2,3},{3,2},{4,5},{5,4},{6,7},{7,6},{8,9},{9,8},{10,11... | collective-permute-start | bytes 786440 | tf_op jit(solution)/shard_map/ppermute | solution.py:471
  14.5 13.7 %collective-permute-start.8 = (bf16[1024,128]{1,0:T(8,128)(2,1)S(1)}, bf16[1024,128]{1,0:T(8,128)(2,1)S(1)}, u32[]{:S(2)}, u32[]{:S(2)}) collective-permute-start(bf16[1024,128]{1,0:T(8,128)(2,1)S(1)} %get-tuple-element.59), channel_id=1, source_target_pairs={{0,1},{1,0},{2,3},{3,2},{4,5},{5,4},{6,7},{7,6},{8,9},{9,8},{10,11... | collective-permute-start | bytes 786440 | tf_op jit(solution)/shard_map/ppermute | solution.py:471
  17.0 7.2 %collective-permute-start.3 = (bf16[512,128]{1,0:T(8,128)(2,1)S(1)}, bf16[512,128]{1,0:T(8,128)(2,1)S(1)}, u32[]{:S(2)}, u32[]{:S(2)}) collective-permute-start(bf16[512,128]{1,0:T(8,128)(2,1)S(1)} %get-tuple-element.50.refs_3_), channel_id=1, source_target_pairs={{0,2},{1,3},{2,0},{3,1},{4,6},{5,7},{6,4},{7,5},{8,10},{9,11},{10,... | collective-permute-start | bytes 393224 | tf_op jit(solution)/shard_map/ppermute | solution.py:471
  19.9 13.1 %collective-permute-start.11 = (bf16[1024,128]{1,0:T(8,128)(2,1)S(1)}, bf16[1024,128]{1,0:T(8,128)(2,1)S(1)}, u32[]{:S(2)}, u32[]{:S(2)}) collective-permute-start(bf16[1024,128]{1,0:T(8,128)(2,1)S(1)} %get-tuple-element.64), channel_id=1, source_target_pairs={{0,1},{1,0},{2,3},{3,2},{4,5},{5,4},{6,7},{7,6},{8,9},{9,8},{10,11... | collective-permute-start | bytes 786440 | tf_op jit(solution)/shard_map/ppermute | solution.py:471
  22.7 9.5 %collective-permute-start.7 = (bf16[512,128]{1,0:T(8,128)(2,1)S(1)}, bf16[512,128]{1,0:T(8,128)(2,1)S(1)}, u32[]{:S(2)}, u32[]{:S(2)}) collective-permute-start(bf16[512,128]{1,0:T(8,128)(2,1)S(1)} %get-tuple-element.54.refs_2_), channel_id=1, source_target_pairs={{0,2},{1,3},{2,0},{3,1},{4,6},{5,7},{6,4},{7,5},{8,10},{9,11},{10,... | collective-permute-start | bytes 393224 | tf_op jit(solution)/shard_map/ppermute | solution.py:471
  28.3 7.6 %collective-permute-start.10 = (bf16[512,128]{1,0:T(8,128)(2,1)S(1)}, bf16[512,128]{1,0:T(8,128)(2,1)S(1)}, u32[]{:S(2)}, u32[]{:S(2)}) collective-permute-start(bf16[512,128]{1,0:T(8,128)(2,1)S(1)} %get-tuple-element.60.refs_2_), channel_id=1, source_target_pairs={{0,2},{1,3},{2,0},{3,1},{4,6},{5,7},{6,4},{7,5},{8,10},{9,11},{10,... | collective-permute-start | bytes 393224 | tf_op jit(solution)/shard_map/ppermute | solution.py:471
  38.2 7.4 %collective-permute-start.12 = (bf16[256,128]{1,0:T(8,128)(2,1)S(1)}, bf16[256,128]{1,0:T(8,128)(2,1)S(1)}, u32[]{:S(2)}, u32[]{:S(2)}) collective-permute-start(bf16[256,128]{1,0:T(8,128)(2,1)S(1)} %get-tuple-element.67.refs_2_), channel_id=1, source_target_pairs={{0,4},{1,5},{2,6},{3,7},{4,0},{5,1},{6,2},{7,3},{8,12},{9,13},{10,... | collective-permute-start | bytes 196616 | tf_op jit(solution)/shard_map/ppermute | solution.py:471
  39.4 6.8 %collective-permute-start.14 = (bf16[256,128]{1,0:T(8,128)(2,1)S(1)}, bf16[256,128]{1,0:T(8,128)(2,1)S(1)}, u32[]{:S(2)}, u32[]{:S(2)}) collective-permute-start(bf16[256,128]{1,0:T(8,128)(2,1)S(1)} %get-tuple-element.70.refs_10_), channel_id=1, source_target_pairs={{0,4},{1,5},{2,6},{3,7},{4,0},{5,1},{6,2},{7,3},{8,12},{9,13},{10,... | collective-permute-start | bytes 196616 | tf_op jit(solution)/shard_map/ppermute | solution.py:471
  52.1 10.5 %collective-permute-start.21 = (bf16[1,256,256]{2,1,0:T(8,128)(2,1)S(1)}, bf16[1,256,256]{2,1,0:T(8,128)(2,1)S(1)}, u32[]{:S(2)}, u32[]{:S(2)}) collective-permute-start(bf16[1,256,256]{2,1,0:T(8,128)(2,1)S(1)} %get-tuple-element.82.refs_0_), channel_id=1, source_target_pairs={{0,4},{1,5},{2,6},{3,7},{4,0},{5,1},{6,2},{7,3},{8,12},{9,13},{10,... | collective-permute-start | bytes 393224 | tf_op jit(solution)/shard_map/ppermute | solution.py:471
  54.2 8.4 %collective-permute-start.20 = (bf16[2,128,256]{2,1,0:T(8,128)(2,1)S(1)}, bf16[2,128,256]{2,1,0:T(8,128)(2,1)S(1)}, u32[]{:S(2)}, u32[]{:S(2)}) collective-permute-start(bf16[2,128,256]{2,1,0:T(8,128)(2,1)S(1)} %shard_map.101.refs_2_.refs_0_), channel_id=1, source_target_pairs={{0,2},{1,3},{2,0},{3,1},{4,6},{5,7},{6,4},{7,5},{8,10},{9,11},{10,... | collective-permute-start | bytes 393224 | tf_op jit(solution)/shard_map/ppermute | solution.py:471
  55.2 11.5 %collective-permute-start.24 = (bf16[2,128,256]{2,1,0:T(8,128)(2,1)S(1)}, bf16[2,128,256]{2,1,0:T(8,128)(2,1)S(1)}, u32[]{:S(2)}, u32[]{:S(2)}) collective-permute-start(bf16[2,128,256]{2,1,0:T(8,128)(2,1)S(1)} %shard_map.100.refs_2_.refs_0_), channel_id=1, source_target_pairs={{0,4},{1,5},{2,6},{3,7},{4,0},{5,1},{6,2},{7,3},{8,12},{9,13},{10,... | collective-permute-start | bytes 393224 | tf_op jit(solution)/shard_map/ppermute | solution.py:471
  56.9 8.3 %collective-permute-start.19 = (bf16[64,512]{1,0:T(8,128)(2,1)S(1)}, bf16[64,512]{1,0:T(8,128)(2,1)S(1)}, u32[]{:S(2)}, u32[]{:S(2)}) collective-permute-start(bf16[64,512]{1,0:T(8,128)(2,1)S(1)} %get-tuple-element.81), channel_id=1, source_target_pairs={{0,16},{8,24},{16,0},{24,8},{1,17},{9,25},{17,1},{25,9},{2,18},{10... | collective-permute-start | bytes 196616 | tf_op jit(solution)/shard_map/ppermute | solution.py:471
  62.5 9.0 %collective-permute-start.23 = (bf16[2,256,256]{2,1,0:T(8,128)(2,1)S(1)}, bf16[2,256,256]{2,1,0:T(8,128)(2,1)S(1)}, u32[]{:S(2)}, u32[]{:S(2)}) collective-permute-start(bf16[2,256,256]{2,1,0:T(8,128)(2,1)S(1)} %shard_map.103.refs_2_.refs_0_), channel_id=1, source_target_pairs={{0,2},{1,3},{2,0},{3,1},{4,6},{5,7},{6,4},{7,5},{8,10},{9,11},{10,... | collective-permute-start | bytes 786440 | tf_op jit(solution)/shard_map/ppermute | solution.py:471
  62.7 15.7 %collective-permute-start.27 = (bf16[4,128,256]{2,1,0:T(8,128)(2,1)S(1)}, bf16[4,128,256]{2,1,0:T(8,128)(2,1)S(1)}, u32[]{:S(2)}, u32[]{:S(2)}) collective-permute-start(bf16[4,128,256]{2,1,0:T(8,128)(2,1)S(1)} %shard_map.104.refs_2_), channel_id=1, source_target_pairs={{0,1},{1,0},{2,3},{3,2},{4,5},{5,4},{6,7},{7,6},{8,9},{9,8},{10,11... | collective-permute-start | bytes 786440 | tf_op jit(solution)/shard_map/ppermute | solution.py:471
  71.6 24.8 %collective-permute-start.31 = (bf16[4,256,256]{2,1,0:T(8,128)(2,1)S(1)}, bf16[4,256,256]{2,1,0:T(8,128)(2,1)S(1)}, u32[]{:S(2)}, u32[]{:S(2)}) collective-permute-start(bf16[4,256,256]{2,1,0:T(8,128)(2,1)S(1)} %shard_map.107.refs_2_), channel_id=1, source_target_pairs={{0,1},{1,0},{2,3},{3,2},{4,5},{5,4},{6,7},{7,6},{8,9},{9,8},{10,11... | collective-permute-start | bytes 1572872 | tf_op jit(solution)/shard_map/ppermute | solution.py:471
  71.8 12.1 %collective-permute-start.26 = (bf16[4,128,256]{2,1,0:T(8,128)(2,1)S(1)}, bf16[4,128,256]{2,1,0:T(8,128)(2,1)S(1)}, u32[]{:S(2)}, u32[]{:S(2)}) collective-permute-start(bf16[4,128,256]{2,1,0:T(8,128)(2,1)S(1)} %shard_map.106.refs_2_.refs_0_), channel_id=1, source_target_pairs={{0,2},{1,3},{2,0},{3,1},{4,6},{5,7},{6,4},{7,5},{8,10},{9,11},{10,... | collective-permute-start | bytes 786440 | tf_op jit(solution)/shard_map/ppermute | solution.py:471
  71.8 6.6 %collective-permute-start.22 = (bf16[64,512]{1,0:T(8,128)(2,1)S(1)}, bf16[64,512]{1,0:T(8,128)(2,1)S(1)}, u32[]{:S(2)}, u32[]{:S(2)}) collective-permute-start(bf16[64,512]{1,0:T(8,128)(2,1)S(1)} %shard_map.105.refs_2_.refs_0_), channel_id=1, source_target_pairs={{0,4},{1,5},{2,6},{3,7},{4,0},{5,1},{6,2},{7,3},{8,12},{9,13},{10,... | collective-permute-start | bytes 196616 | tf_op jit(solution)/shard_map/ppermute | solution.py:471
  79.3 8.7 %collective-permute-start.25 = (f32[64,512]{1,0:T(8,128)S(1)}, f32[64,512]{1,0:T(8,128)S(1)}, u32[]{:S(2)}, u32[]{:S(2)}) collective-permute-start(f32[64,512]{1,0:T(8,128)S(1)} %shard_map.108.refs_4_.refs_0_), channel_id=1, source_target_pairs={{0,2},{1,3},{2,0},{3,1},{4,6},{5,7},{6,4},{7,5},{8,10},{9,11},{10,... | collective-permute-start | bytes 393224 | tf_op jit(solution)/shard_map/ppermute | solution.py:471
  84.8 15.0 %collective-permute-start.34 = (bf16[128,1024]{1,0:T(8,128)(2,1)S(1)}, bf16[128,1024]{1,0:T(8,128)(2,1)S(1)}, u32[]{:S(2)}, u32[]{:S(2)}) collective-permute-start(bf16[128,1024]{1,0:T(8,128)(2,1)S(1)} %shard_map.112.refs_2_), channel_id=1, source_target_pairs={{0,16},{8,24},{16,0},{24,8},{1,17},{9,25},{17,1},{25,9},{2,18},{10... | collective-permute-start | bytes 786440 | tf_op jit(solution)/shard_map/ppermute | solution.py:471
  88.0 6.6 %collective-permute-start.29 = (bf16[64,512]{1,0:T(8,128)(2,1)S(1)}, bf16[64,512]{1,0:T(8,128)(2,1)S(1)}, u32[]{:S(2)}, u32[]{:S(2)}) collective-permute-start(bf16[64,512]{1,0:T(8,128)(2,1)S(1)} %shard_map.113.refs_0_.refs_2_), channel_id=1, source_target_pairs={{0,16},{8,24},{16,0},{24,8},{1,17},{9,25},{17,1},{25,9},{2,18},{10... | collective-permute-start | bytes 196616 | tf_op jit(solution)/shard_map/ppermute | solution.py:471
  (14 other events, 74.9 us)

commit v6 on v5

--- a/solution.py
+++ b/solution.py
@@ -13,6 +13,7 @@
 MIB = 1024 * 1024
 COST_F, COST_U = 1_000_000_000, 2_000_000_000
 COST, COST_S, COST_W, COST_M = 4_000_000_000, 2_000_000_000, 0, 2_000_000_000
+COST_L, COST_K = 3_000_000_000, 2_000_000_000
 SMEM = pl.BlockSpec(memory_space=pltpu.SMEM)
 VMEM = pl.BlockSpec(memory_space=pltpu.VMEM)
 ANYWHERE = pl.BlockSpec(memory_space=pl.ANY)
@@ -564,9 +565,9 @@
         state["w"] = [outs[0]] + [swap(v, "row", 2 * (k + 1)) for k, v in enumerate(outs[1:])]
         state["bit"] = n_col // 2
 
-    def weight_line():
+    def weight_line(cost=0):
         bit = state["bit"]
-        total = sum_of(state["w"], BF16 if bit > 2 else F32, order())
+        total = sum_of(state["w"], BF16 if bit > 2 else F32, order(), cost)
         state["last"] = total
         state["w"] = [total, swap(total, "col", bit)]
         state["bit"] = bit // 2
@@ -576,13 +577,14 @@
         state["last"] = total
         state["w"] = [total] + [swap(total, "row", 2 * k) for k in range(1, ro)]
 
-    def weight_stack(axis):
+    def weight_stack(axis, cost=0):
         total = call(
             stack_all,
             jax.ShapeDtypeStruct((len(state["w"]),) + state["w"][0].shape, BF16),
             [VMEM] * len(state["w"]),
             tuple(state["w"]),
             before=order(),
+            cost=cost,
         )
         state["last"] = total
         state["w"] = [total, swap(total, axis, 1)]
@@ -629,13 +631,13 @@
     for _ in range(stages - 1):
         join("M")
     for _ in range(stages - 1):
-        weight_line()
+        weight_line(COST_L)
     back([(1, 1)], (rows["C"], came_rows["C"]))
+    weight_sum()
     join("A", COST_S)
     back([(1, 0)], (rows["A"],))
     send_parts(1)
-    weight_sum()
-    weight_stack("col")
+    weight_stack("col", COST_K)
     back([(0, 1), (0, 0)], (rows["M"], came_rows["M"]), COST_M)
     weight_stack("row")
     send_parts(0)

time: 103 us -> 94.1 us (0.914)
  waiting for transfers between devices: 46 us -> 39.6 us
  starting transfers between devices: 41.7 us -> 38.5 us
    ppermute x35, waiting for transfers between devices: 46 us -> 39.6 us  [swap(): return lax.ppermute(v, axis, [(i, i ^ bit) for i in range(size)])]
    ppermute x35, starting transfers between devices: 41.7 us -> 38.5 us  [swap(): return lax.ppermute(v, axis, [(i, i ^ bit) for i in range(size)])]
  transfers between devices with their start and end apart: 35 -> 35, of which waited for: 19 -> 19; matrix products, arithmetic and copies ran while one was open for 0% -> 0% of each run, Pallas kernels for 11% -> 12%
where the time goes in v6:
time: 94.1 us; the launch traced here: 93.6 us
  waiting for transfers between devices  39.6 us (42%)
  starting transfers between devices  38.5 us (41%)
  Pallas kernels  13.9 us (15%)
  between operations  1.54 us (2%)
    ppermute x35, waiting for transfers between devices, swap(): return lax.ppermute(v, axis, [(i, i ^ bit) for i in range(size)])  39.6 us
    ppermute x35, starting transfers between devices, swap(): return lax.ppermute(v, axis, [(i, i ^ bit) for i in range(size)])  38.5 us
    pallas_call x35, Pallas kernels, call(): pl.pallas_call(run, out_shape=tuple(out_shape) if many else out_shape, in...  13.9 us
  transfers between devices with their start and end apart: 35, of which 19 were waited for; matrix products, arithmetic and copies ran while one was open for 0% of the time, Pallas kernels for 12%

profile of v6, /device:TPU:0, one launch (start us, length us, event | category | flops | bytes accessed | tf_op | source)
XLA Modules:
  0.0 93.6 jit_solution(10426429503776371748)
XLA Ops:
  1.2 2.6 %collective-permute-start.1 = (bf16[1024,128]{1,0:T(8,128)(2,1)}, bf16[1024,128]{1,0:T(8,128)(2,1)S(1)}, u32[]{:S(2)}, u32[]{:S(2)}) collective-permute-start(bf16[1024,128]{1,0:T(8,128)(2,1)} %refs_5_.1), channel_id=1, source_target_pairs={{0,16},{8,24},{16,0},{24,8},{1,17},{9,25},{17,1},{25,9},{2,18},{10... | collective-permute-start | bytes 786440 | tf_op jit(solution)/shard_map/ppermute | solution.py:472
  4.4 3.6 %shard_map.85 = (bf16[1024,1024]{1,0:T(8,128)(2,1)S(1)}, bf16[1024,1024]{1,0:T(8,128)(2,1)S(1)}, bf16[1024,128]{1,0:T(8,128)(2,1)S(1)}, bf16[1024,128]{1,0:T(8,128)(2,1)S(1)}) custom-call(s32[1]{0:T(128)} %bitcast.7.refs_0_, s32[1]{0:T(128)} %bitcast.1.refs_1_.refs_0_, s32[1]{0:T(128)} %bitcast.2.refs_2_.refs_0_, s32[2,96]{1,0:T(2,128)} %bitcast.9, ...), custom_call_target="tpu_custom_call" | custom-call | tf_op jit(solution)/shard_map/pallas_call | solution.py:29
  9.0 1.9 %collective-permute-done.1.refs_4_ = bf16[1024,128]{1,0:T(8,128)(2,1)S(1)} collective-permute-done((bf16[1024,128]{1,0:T(8,128)(2,1)}, bf16[1024,128]{1,0:T(8,128)(2,1)S(1)}, u32[]{:S(2)}, u32[]{:S(2)}) %collective-permute-start.1) | collective-permute-done | bytes 262176 | tf_op jit(solution)/shard_map/ppermute | solution.py:472
  10.9 1.9 %shard_map.86 = (bf16[1024,128]{1,0:T(8,128)(2,1)S(1)}, bf16[1024,128]{1,0:T(8,128)(2,1)S(1)}, f32[1024,128]{1,0:T(8,128)S(1)}, f32[1024,128]{1,0:T(8,128)S(1)}, f32[1024,128]{1,0:T(8,128)S(1)}) custom-call(bf16[1024,1024]{1,0:T(8,128)(2,1)S(1)} %get-tuple-element.44.refs_0_, bf16[1024,1024]{1,0:T(8,128)(2,1)S(1)} %get-tuple-element.45.refs_1_, ...), custom_call_target="tpu_custom_call" | custom-call | tf_op jit(solution)/shard_map/pallas_call | solution.py:29
  12.7 1.8 %collective-permute-start.4 = (bf16[1024,128]{1,0:T(8,128)(2,1)S(1)}, bf16[1024,128]{1,0:T(8,128)(2,1)S(1)}, u32[]{:S(2)}, u32[]{:S(2)}) collective-permute-start(bf16[1024,128]{1,0:T(8,128)(2,1)S(1)} %get-tuple-element.52), channel_id=1, source_target_pairs={{0,1},{1,0},{2,3},{3,2},{4,5},{5,4},{6,7},{7,6},{8,9},{9,8},{10,11... | collective-permute-start | bytes 786440 | tf_op jit(solution)/shard_map/ppermute | solution.py:472
  14.9 1.7 %collective-permute-done.2.refs_1_ = bf16[1024,128]{1,0:T(8,128)(2,1)S(1)} collective-permute-done((bf16[1024,128]{1,0:T(8,128)(2,1)S(1)}, bf16[1024,128]{1,0:T(8,128)(2,1)S(1)}, u32[]{:S(2)}, u32[]{:S(2)}) %collective-permute-start.2) | collective-permute-done | bytes 262176 | tf_op jit(solution)/shard_map/ppermute | solution.py:472
  16.6 1.7 %collective-permute-start.3 = (bf16[512,128]{1,0:T(8,128)(2,1)S(1)}, bf16[512,128]{1,0:T(8,128)(2,1)S(1)}, u32[]{:S(2)}, u32[]{:S(2)}) collective-permute-start(bf16[512,128]{1,0:T(8,128)(2,1)S(1)} %get-tuple-element.50.refs_3_), channel_id=1, source_target_pairs={{0,2},{1,3},{2,0},{3,1},{4,6},{5,7},{6,4},{7,5},{8,10},{9,11},{10,... | collective-permute-start | bytes 393224 | tf_op jit(solution)/shard_map/ppermute | solution.py:472
  19.6 1.9 %collective-permute-start.11 = (bf16[1024,128]{1,0:T(8,128)(2,1)S(1)}, bf16[1024,128]{1,0:T(8,128)(2,1)S(1)}, u32[]{:S(2)}, u32[]{:S(2)}) collective-permute-start(bf16[1024,128]{1,0:T(8,128)(2,1)S(1)} %get-tuple-element.64), channel_id=1, source_target_pairs={{0,1},{1,0},{2,3},{3,2},{4,5},{5,4},{6,7},{7,6},{8,9},{9,8},{10,11... | collective-permute-start | bytes 786440 | tf_op jit(solution)/shard_map/ppermute | solution.py:472
  22.3 1.7 %collective-permute-start.7 = (bf16[512,128]{1,0:T(8,128)(2,1)S(1)}, bf16[512,128]{1,0:T(8,128)(2,1)S(1)}, u32[]{:S(2)}, u32[]{:S(2)}) collective-permute-start(bf16[512,128]{1,0:T(8,128)(2,1)S(1)} %get-tuple-element.54.refs_2_), channel_id=1, source_target_pairs={{0,2},{1,3},{2,0},{3,1},{4,6},{5,7},{6,4},{7,5},{8,10},{9,11},{10,... | collective-permute-start | bytes 393224 | tf_op jit(solution)/shard_map/ppermute | solution.py:472
  24.0 3.8 %collective-permute-done.8.refs_1_ = bf16[1024,128]{1,0:T(8,128)(2,1)S(1)} collective-permute-done((bf16[1024,128]{1,0:T(8,128)(2,1)S(1)}, bf16[1024,128]{1,0:T(8,128)(2,1)S(1)}, u32[]{:S(2)}, u32[]{:S(2)}) %collective-permute-start.8) | collective-permute-done | bytes 262176 | tf_op jit(solution)/shard_map/ppermute | solution.py:472
  27.9 1.7 %collective-permute-start.10 = (bf16[512,128]{1,0:T(8,128)(2,1)S(1)}, bf16[512,128]{1,0:T(8,128)(2,1)S(1)}, u32[]{:S(2)}, u32[]{:S(2)}) collective-permute-start(bf16[512,128]{1,0:T(8,128)(2,1)S(1)} %get-tuple-element.60.refs_2_), channel_id=1, source_target_pairs={{0,2},{1,3},{2,0},{3,1},{4,6},{5,7},{6,4},{7,5},{8,10},{9,11},{10,... | collective-permute-start | bytes 393224 | tf_op jit(solution)/shard_map/ppermute | solution.py:472
  29.6 2.6 %collective-permute-start.6 = (bf16[256,128]{1,0:T(8,128)(2,1)S(1)}, bf16[256,128]{1,0:T(8,128)(2,1)S(1)}, u32[]{:S(2)}, u32[]{:S(2)}) collective-permute-start(bf16[256,128]{1,0:T(8,128)(2,1)S(1)} %get-tuple-element.56.refs_2_), channel_id=1, source_target_pairs={{0,4},{1,5},{2,6},{3,7},{4,0},{5,1},{6,2},{7,3},{8,12},{9,13},{10,... | collective-permute-start | bytes 196616 | tf_op jit(solution)/shard_map/ppermute | solution.py:472
  32.8 1.7 %collective-permute-start.13 = (bf16[512,128]{1,0:T(8,128)(2,1)S(1)}, bf16[512,128]{1,0:T(8,128)(2,1)S(1)}, u32[]{:S(2)}, u32[]{:S(2)}) collective-permute-start(bf16[512,128]{1,0:T(8,128)(2,1)S(1)} %get-tuple-element.65.refs_2_), channel_id=1, source_target_pairs={{0,2},{1,3},{2,0},{3,1},{4,6},{5,7},{6,4},{7,5},{8,10},{9,11},{10,... | collective-permute-start | bytes 393224 | tf_op jit(solution)/shard_map/ppermute | solution.py:472
  34.6 1.6 %collective-permute-done.6.refs_3_.refs_1_ = bf16[256,128]{1,0:T(8,128)(2,1)S(1)} collective-permute-done((bf16[256,128]{1,0:T(8,128)(2,1)S(1)}, bf16[256,128]{1,0:T(8,128)(2,1)S(1)}, u32[]{:S(2)}, u32[]{:S(2)}) %collective-permute-start.6) | collective-permute-done | bytes 65568 | tf_op jit(solution)/shard_map/ppermute | solution.py:472
  36.2 2.1 %collective-permute-done.9.refs_4_.refs_3_ = bf16[256,128]{1,0:T(8,128)(2,1)S(1)} collective-permute-done((bf16[256,128]{1,0:T(8,128)(2,1)S(1)}, bf16[256,128]{1,0:T(8,128)(2,1)S(1)}, u32[]{:S(2)}, u32[]{:S(2)}) %collective-permute-start.9) | collective-permute-done | bytes 65568 | tf_op jit(solution)/shard_map/ppermute | solution.py:472
  39.5 2.3 %collective-permute-start.14 = (bf16[256,128]{1,0:T(8,128)(2,1)S(1)}, bf16[256,128]{1,0:T(8,128)(2,1)S(1)}, u32[]{:S(2)}, u32[]{:S(2)}) collective-permute-start(bf16[256,128]{1,0:T(8,128)(2,1)S(1)} %get-tuple-element.70.refs_10_), channel_id=1, source_target_pairs={{0,4},{1,5},{2,6},{3,7},{4,0},{5,1},{6,2},{7,3},{8,12},{9,13},{10,... | collective-permute-start | bytes 196616 | tf_op jit(solution)/shard_map/ppermute | solution.py:472
  41.8 3.5 %collective-permute-done.12.refs_5_ = bf16[256,128]{1,0:T(8,128)(2,1)S(1)} collective-permute-done((bf16[256,128]{1,0:T(8,128)(2,1)S(1)}, bf16[256,128]{1,0:T(8,128)(2,1)S(1)}, u32[]{:S(2)}, u32[]{:S(2)}) %collective-permute-start.12) | collective-permute-done | bytes 65568 | tf_op jit(solution)/shard_map/ppermute | solution.py:472
  51.5 2.2 %collective-permute-start.21 = (bf16[1,256,256]{2,1,0:T(8,128)(2,1)S(1)}, bf16[1,256,256]{2,1,0:T(8,128)(2,1)S(1)}, u32[]{:S(2)}, u32[]{:S(2)}) collective-permute-start(bf16[1,256,256]{2,1,0:T(8,128)(2,1)S(1)} %get-tuple-element.82.refs_0_), channel_id=1, source_target_pairs={{0,4},{1,5},{2,6},{3,7},{4,0},{5,1},{6,2},{7,3},{8,12},{9,13},{10,... | collective-permute-start | bytes 393224 | tf_op jit(solution)/shard_map/ppermute | solution.py:472
  58.7 5.3 %collective-permute-done.21.refs_1_ = bf16[1,256,256]{2,1,0:T(8,128)(2,1)S(1)} collective-permute-done((bf16[1,256,256]{2,1,0:T(8,128)(2,1)S(1)}, bf16[1,256,256]{2,1,0:T(8,128)(2,1)S(1)}, u32[]{:S(2)}, u32[]{:S(2)}) %collective-permute-start.21) | collective-permute-done | bytes 131104 | tf_op jit(solution)/shard_map/ppermute | solution.py:472
  67.6 6.5 %collective-permute-done.23.refs_1_ = bf16[2,256,256]{2,1,0:T(8,128)(2,1)S(1)} collective-permute-done((bf16[2,256,256]{2,1,0:T(8,128)(2,1)S(1)}, bf16[2,256,256]{2,1,0:T(8,128)(2,1)S(1)}, u32[]{:S(2)}, u32[]{:S(2)}) %collective-permute-start.23) | collective-permute-done | bytes 262176 | tf_op jit(solution)/shard_map/ppermute | solution.py:472
  75.7 4.5 %collective-permute-done.25.refs_1_ = f32[64,512]{1,0:T(8,128)S(1)} collective-permute-done((f32[64,512]{1,0:T(8,128)S(1)}, f32[64,512]{1,0:T(8,128)S(1)}, u32[]{:S(2)}, u32[]{:S(2)}) %collective-permute-start.25) | collective-permute-done | bytes 131104 | tf_op jit(solution)/shard_map/ppermute | solution.py:472
  80.2 2.4 %collective-permute-start.27 = (bf16[64,512]{1,0:T(8,128)(2,1)S(1)}, bf16[64,512]{1,0:T(8,128)(2,1)S(1)}, u32[]{:S(2)}, u32[]{:S(2)}) collective-permute-start(bf16[64,512]{1,0:T(8,128)(2,1)S(1)} %shard_map.110.refs_2_.refs_0_), channel_id=1, source_target_pairs={{0,16},{8,24},{16,0},{24,8},{1,17},{9,25},{17,1},{25,9},{2,18},{10... | collective-permute-start | bytes 196616 | tf_op jit(solution)/shard_map/ppermute | solution.py:472
  85.1 1.7 %collective-permute-start.30 = (bf16[2,64,512]{2,1,0:T(8,128)(2,1)S(1)}, bf16[2,64,512]{2,1,0:T(8,128)(2,1)S(1)}, u32[]{:S(2)}, u32[]{:S(2)}) collective-permute-start(bf16[2,64,512]{2,1,0:T(8,128)(2,1)S(1)} %shard_map.114.refs_4_.refs_0_), channel_id=1, source_target_pairs={{0,1},{1,0},{2,3},{3,2},{4,5},{5,4},{6,7},{7,6},{8,9},{9,8},{10,11... | collective-permute-start | bytes 393224 | tf_op jit(solution)/shard_map/ppermute | solution.py:472
  88.1 2.0 %collective-permute-done.30.refs_1_ = bf16[2,64,512]{2,1,0:T(8,128)(2,1)S(1)} collective-permute-done((bf16[2,64,512]{2,1,0:T(8,128)(2,1)S(1)}, bf16[2,64,512]{2,1,0:T(8,128)(2,1)S(1)}, u32[]{:S(2)}, u32[]{:S(2)}) %collective-permute-start.30) | collective-permute-done | bytes 131104 | tf_op jit(solution)/shard_map/ppermute | solution.py:472
  (87 shorter events, 29.4 us)
Async XLA Ops:
  0.6 8.4 %collective-permute-start = (bf16[1024,128]{1,0:T(8,128)(2,1)}, bf16[1024,128]{1,0:T(8,128)(2,1)S(1)}, u32[]{:S(2)}, u32[]{:S(2)}) collective-permute-start(bf16[1024,128]{1,0:T(8,128)(2,1)} %refs_5_.1), channel_id=1, source_target_pairs={{0,8},{8,0},{16,24},{24,16},{1,9},{9,1},{17,25},{25,17},{2,10},{10... | collective-permute-start | bytes 786440 | tf_op jit(solution)/shard_map/ppermute | solution.py:472
  1.2 9.7 %collective-permute-start.1 = (bf16[1024,128]{1,0:T(8,128)(2,1)}, bf16[1024,128]{1,0:T(8,128)(2,1)S(1)}, u32[]{:S(2)}, u32[]{:S(2)}) collective-permute-start(bf16[1024,128]{1,0:T(8,128)(2,1)} %refs_5_.1), channel_id=1, source_target_pairs={{0,16},{8,24},{16,0},{24,8},{1,17},{9,25},{17,1},{25,9},{2,18},{10... | collective-permute-start | bytes 786440 | tf_op jit(solution)/shard_map/ppermute | solution.py:472
  8.0 8.5 %collective-permute-start.2 = (bf16[1024,128]{1,0:T(8,128)(2,1)S(1)}, bf16[1024,128]{1,0:T(8,128)(2,1)S(1)}, u32[]{:S(2)}, u32[]{:S(2)}) collective-permute-start(bf16[1024,128]{1,0:T(8,128)(2,1)S(1)} %get-tuple-element.48), channel_id=1, source_target_pairs={{0,1},{1,0},{2,3},{3,2},{4,5},{5,4},{6,7},{7,6},{8,9},{9,8},{10,11... | collective-permute-start | bytes 786440 | tf_op jit(solution)/shard_map/ppermute | solution.py:472
  8.7 9.7 %collective-permute-start.5 = (bf16[1024,128]{1,0:T(8,128)(2,1)S(1)}, bf16[1024,128]{1,0:T(8,128)(2,1)S(1)}, u32[]{:S(2)}, u32[]{:S(2)}) collective-permute-start(bf16[1024,128]{1,0:T(8,128)(2,1)S(1)} %copy-done.2), channel_id=1, source_target_pairs={{0,24},{8,16},{16,8},{24,0},{1,25},{9,17},{17,9},{25,1},{2,26},{10... | collective-permute-start | bytes 786440 | tf_op jit(solution)/shard_map/ppermute | solution.py:472
  12.7 9.5 %collective-permute-start.4 = (bf16[1024,128]{1,0:T(8,128)(2,1)S(1)}, bf16[1024,128]{1,0:T(8,128)(2,1)S(1)}, u32[]{:S(2)}, u32[]{:S(2)}) collective-permute-start(bf16[1024,128]{1,0:T(8,128)(2,1)S(1)} %get-tuple-element.52), channel_id=1, source_target_pairs={{0,1},{1,0},{2,3},{3,2},{4,5},{5,4},{6,7},{7,6},{8,9},{9,8},{10,11... | collective-permute-start | bytes 786440 | tf_op jit(solution)/shard_map/ppermute | solution.py:472
  14.5 13.3 %collective-permute-start.8 = (bf16[1024,128]{1,0:T(8,128)(2,1)S(1)}, bf16[1024,128]{1,0:T(8,128)(2,1)S(1)}, u32[]{:S(2)}, u32[]{:S(2)}) collective-permute-start(bf16[1024,128]{1,0:T(8,128)(2,1)S(1)} %get-tuple-element.59), channel_id=1, source_target_pairs={{0,1},{1,0},{2,3},{3,2},{4,5},{5,4},{6,7},{7,6},{8,9},{9,8},{10,11... | collective-permute-start | bytes 786440 | tf_op jit(solution)/shard_map/ppermute | solution.py:472
  16.6 7.4 %collective-permute-start.3 = (bf16[512,128]{1,0:T(8,128)(2,1)S(1)}, bf16[512,128]{1,0:T(8,128)(2,1)S(1)}, u32[]{:S(2)}, u32[]{:S(2)}) collective-permute-start(bf16[512,128]{1,0:T(8,128)(2,1)S(1)} %get-tuple-element.50.refs_3_), channel_id=1, source_target_pairs={{0,2},{1,3},{2,0},{3,1},{4,6},{5,7},{6,4},{7,5},{8,10},{9,11},{10,... | collective-permute-start | bytes 393224 | tf_op jit(solution)/shard_map/ppermute | solution.py:472
  19.6 13.2 %collective-permute-start.11 = (bf16[1024,128]{1,0:T(8,128)(2,1)S(1)}, bf16[1024,128]{1,0:T(8,128)(2,1)S(1)}, u32[]{:S(2)}, u32[]{:S(2)}) collective-permute-start(bf16[1024,128]{1,0:T(8,128)(2,1)S(1)} %get-tuple-element.64), channel_id=1, source_target_pairs={{0,1},{1,0},{2,3},{3,2},{4,5},{5,4},{6,7},{7,6},{8,9},{9,8},{10,11... | collective-permute-start | bytes 786440 | tf_op jit(solution)/shard_map/ppermute | solution.py:472
  22.3 9.9 %collective-permute-start.7 = (bf16[512,128]{1,0:T(8,128)(2,1)S(1)}, bf16[512,128]{1,0:T(8,128)(2,1)S(1)}, u32[]{:S(2)}, u32[]{:S(2)}) collective-permute-start(bf16[512,128]{1,0:T(8,128)(2,1)S(1)} %get-tuple-element.54.refs_2_), channel_id=1, source_target_pairs={{0,2},{1,3},{2,0},{3,1},{4,6},{5,7},{6,4},{7,5},{8,10},{9,11},{10,... | collective-permute-start | bytes 393224 | tf_op jit(solution)/shard_map/ppermute | solution.py:472
  27.9 8.3 %collective-permute-start.10 = (bf16[512,128]{1,0:T(8,128)(2,1)S(1)}, bf16[512,128]{1,0:T(8,128)(2,1)S(1)}, u32[]{:S(2)}, u32[]{:S(2)}) collective-permute-start(bf16[512,128]{1,0:T(8,128)(2,1)S(1)} %get-tuple-element.60.refs_2_), channel_id=1, source_target_pairs={{0,2},{1,3},{2,0},{3,1},{4,6},{5,7},{6,4},{7,5},{8,10},{9,11},{10,... | collective-permute-start | bytes 393224 | tf_op jit(solution)/shard_map/ppermute | solution.py:472
  38.3 7.0 %collective-permute-start.12 = (bf16[256,128]{1,0:T(8,128)(2,1)S(1)}, bf16[256,128]{1,0:T(8,128)(2,1)S(1)}, u32[]{:S(2)}, u32[]{:S(2)}) collective-permute-start(bf16[256,128]{1,0:T(8,128)(2,1)S(1)} %get-tuple-element.67.refs_2_), channel_id=1, source_target_pairs={{0,4},{1,5},{2,6},{3,7},{4,0},{5,1},{6,2},{7,3},{8,12},{9,13},{10,... | collective-permute-start | bytes 196616 | tf_op jit(solution)/shard_map/ppermute | solution.py:472
  39.5 7.2 %collective-permute-start.14 = (bf16[256,128]{1,0:T(8,128)(2,1)S(1)}, bf16[256,128]{1,0:T(8,128)(2,1)S(1)}, u32[]{:S(2)}, u32[]{:S(2)}) collective-permute-start(bf16[256,128]{1,0:T(8,128)(2,1)S(1)} %get-tuple-element.70.refs_10_), channel_id=1, source_target_pairs={{0,4},{1,5},{2,6},{3,7},{4,0},{5,1},{6,2},{7,3},{8,12},{9,13},{10,... | collective-permute-start | bytes 196616 | tf_op jit(solution)/shard_map/ppermute | solution.py:472
  50.5 6.7 %collective-permute-start.16 = (bf16[2,64,512]{2,1,0:T(8,128)(2,1)S(1)}, bf16[2,64,512]{2,1,0:T(8,128)(2,1)S(1)}, u32[]{:S(2)}, u32[]{:S(2)}) collective-permute-start(bf16[2,64,512]{2,1,0:T(8,128)(2,1)S(1)} %get-tuple-element.77.refs_2_), channel_id=1, source_target_pairs={{0,1},{1,0},{2,3},{3,2},{4,5},{5,4},{6,7},{7,6},{8,9},{9,8},{10,11... | collective-permute-start | bytes 393224 | tf_op jit(solution)/shard_map/ppermute | solution.py:472
  51.5 12.4 %collective-permute-start.21 = (bf16[1,256,256]{2,1,0:T(8,128)(2,1)S(1)}, bf16[1,256,256]{2,1,0:T(8,128)(2,1)S(1)}, u32[]{:S(2)}, u32[]{:S(2)}) collective-permute-start(bf16[1,256,256]{2,1,0:T(8,128)(2,1)S(1)} %get-tuple-element.82.refs_0_), channel_id=1, source_target_pairs={{0,4},{1,5},{2,6},{3,7},{4,0},{5,1},{6,2},{7,3},{8,12},{9,13},{10,... | collective-permute-start | bytes 393224 | tf_op jit(solution)/shard_map/ppermute | solution.py:472
  54.7 9.3 %collective-permute-start.20 = (bf16[2,128,256]{2,1,0:T(8,128)(2,1)S(1)}, bf16[2,128,256]{2,1,0:T(8,128)(2,1)S(1)}, u32[]{:S(2)}, u32[]{:S(2)}) collective-permute-start(bf16[2,128,256]{2,1,0:T(8,128)(2,1)S(1)} %shard_map.101.refs_2_.refs_0_), channel_id=1, source_target_pairs={{0,2},{1,3},{2,0},{3,1},{4,6},{5,7},{6,4},{7,5},{8,10},{9,11},{10,... | collective-permute-start | bytes 393224 | tf_op jit(solution)/shard_map/ppermute | solution.py:472
  55.9 10.7 %collective-permute-start.24 = (bf16[2,128,256]{2,1,0:T(8,128)(2,1)S(1)}, bf16[2,128,256]{2,1,0:T(8,128)(2,1)S(1)}, u32[]{:S(2)}, u32[]{:S(2)}) collective-permute-start(bf16[2,128,256]{2,1,0:T(8,128)(2,1)S(1)} %shard_map.100.refs_2_.refs_0_), channel_id=1, source_target_pairs={{0,4},{1,5},{2,6},{3,7},{4,0},{5,1},{6,2},{7,3},{8,12},{9,13},{10,... | collective-permute-start | bytes 393224 | tf_op jit(solution)/shard_map/ppermute | solution.py:472
  57.2 8.2 %collective-permute-start.19 = (bf16[64,512]{1,0:T(8,128)(2,1)S(1)}, bf16[64,512]{1,0:T(8,128)(2,1)S(1)}, u32[]{:S(2)}, u32[]{:S(2)}) collective-permute-start(bf16[64,512]{1,0:T(8,128)(2,1)S(1)} %get-tuple-element.81), channel_id=1, source_target_pairs={{0,16},{8,24},{16,0},{24,8},{1,17},{9,25},{17,1},{25,9},{2,18},{10... | collective-permute-start | bytes 196616 | tf_op jit(solution)/shard_map/ppermute | solution.py:472
  63.9 10.2 %collective-permute-start.23 = (bf16[2,256,256]{2,1,0:T(8,128)(2,1)S(1)}, bf16[2,256,256]{2,1,0:T(8,128)(2,1)S(1)}, u32[]{:S(2)}, u32[]{:S(2)}) collective-permute-start(bf16[2,256,256]{2,1,0:T(8,128)(2,1)S(1)} %shard_map.103.refs_2_.refs_0_), channel_id=1, source_target_pairs={{0,2},{1,3},{2,0},{3,1},{4,6},{5,7},{6,4},{7,5},{8,10},{9,11},{10,... | collective-permute-start | bytes 786440 | tf_op jit(solution)/shard_map/ppermute | solution.py:472
  64.1 10.7 %collective-permute-start.26 = (bf16[4,128,256]{2,1,0:T(8,128)(2,1)S(1)}, bf16[4,128,256]{2,1,0:T(8,128)(2,1)S(1)}, u32[]{:S(2)}, u32[]{:S(2)}) collective-permute-start(bf16[4,128,256]{2,1,0:T(8,128)(2,1)S(1)} %shard_map.104.refs_2_), channel_id=1, source_target_pairs={{0,1},{1,0},{2,3},{3,2},{4,5},{5,4},{6,7},{7,6},{8,9},{9,8},{10,11... | collective-permute-start | bytes 786440 | tf_op jit(solution)/shard_map/ppermute | solution.py:472
  65.5 9.2 %collective-permute-start.22 = (bf16[64,512]{1,0:T(8,128)(2,1)S(1)}, bf16[64,512]{1,0:T(8,128)(2,1)S(1)}, u32[]{:S(2)}, u32[]{:S(2)}) collective-permute-start(bf16[64,512]{1,0:T(8,128)(2,1)S(1)} %shard_map.105.refs_2_.refs_0_), channel_id=1, source_target_pairs={{0,4},{1,5},{2,6},{3,7},{4,0},{5,1},{6,2},{7,3},{8,12},{9,13},{10,... | collective-permute-start | bytes 196616 | tf_op jit(solution)/shard_map/ppermute | solution.py:472
  66.7 16.0 %collective-permute-start.28 = (bf16[4,128,256]{2,1,0:T(8,128)(2,1)S(1)}, bf16[4,128,256]{2,1,0:T(8,128)(2,1)S(1)}, u32[]{:S(2)}, u32[]{:S(2)}) collective-permute-start(bf16[4,128,256]{2,1,0:T(8,128)(2,1)S(1)} %shard_map.106.refs_2_.refs_0_), channel_id=1, source_target_pairs={{0,2},{1,3},{2,0},{3,1},{4,6},{5,7},{6,4},{7,5},{8,10},{9,11},{10,... | collective-permute-start | bytes 786440 | tf_op jit(solution)/shard_map/ppermute | solution.py:472
  74.2 12.5 %collective-permute-start.31 = (bf16[4,256,256]{2,1,0:T(8,128)(2,1)S(1)}, bf16[4,256,256]{2,1,0:T(8,128)(2,1)S(1)}, u32[]{:S(2)}, u32[]{:S(2)}) collective-permute-start(bf16[4,256,256]{2,1,0:T(8,128)(2,1)S(1)} %shard_map.107.refs_2_), channel_id=1, source_target_pairs={{0,1},{1,0},{2,3},{3,2},{4,5},{5,4},{6,7},{7,6},{8,9},{9,8},{10,11... | collective-permute-start | bytes 1572872 | tf_op jit(solution)/shard_map/ppermute | solution.py:472
  75.6 7.8 %collective-permute-start.29 = (bf16[128,1024]{1,0:T(8,128)(2,1)S(1)}, bf16[128,1024]{1,0:T(8,128)(2,1)S(1)}, u32[]{:S(2)}, u32[]{:S(2)}) collective-permute-start(bf16[128,1024]{1,0:T(8,128)(2,1)S(1)} %shard_map.109.refs_2_), channel_id=1, source_target_pairs={{0,8},{8,0},{16,24},{24,16},{1,9},{9,1},{17,25},{25,17},{2,10},{10... | collective-permute-start | bytes 786440 | tf_op jit(solution)/shard_map/ppermute | solution.py:472
  83.5 7.4 %collective-permute-start.34 = (bf16[128,1024]{1,0:T(8,128)(2,1)S(1)}, bf16[128,1024]{1,0:T(8,128)(2,1)S(1)}, u32[]{:S(2)}, u32[]{:S(2)}) collective-permute-start(bf16[128,1024]{1,0:T(8,128)(2,1)S(1)} %shard_map.113.refs_2_), channel_id=1, source_target_pairs={{0,16},{8,24},{16,0},{24,8},{1,17},{9,25},{17,1},{25,9},{2,18},{10... | collective-permute-start | bytes 786440 | tf_op jit(solution)/shard_map/ppermute | solution.py:472
  (14 other events, 74.3 us)

commit v7 on v6

--- a/solution.py
+++ b/solution.py
@@ -476,10 +476,11 @@
     owners = [[2 * k + i for k in halves[h]] for h, i in chunks]
     flat = [rel for rels in owners for rel in rels]
 
-    features = []
-    for rels in owners:
-        parts = [swap(node_features, "row", rel) if rel else node_features for rel in rels]
-        features.append(jnp.concatenate(parts, axis=1) if len(parts) > 1 else parts[0])
+    def arriving(source, rels):
+        parts = [swap(source, "row", rel) if rel else source for rel in rels]
+        return jnp.concatenate(parts, axis=1) if len(parts) > 1 else parts[0]
+
+    features = [arriving(node_features, rels) for rels in owners[:2]]
     near, far, own_features, first_away = dense_blocks(
         tile_values[0, 0],
         pltpu.with_memory_space_constraint(tile_coords[0, 0].T, pltpu.HBM),
@@ -492,9 +493,11 @@
         max(limit, 48),
     )
     features[0] = own_features
-    away, kept = all_products(near, far, features[:3], limit)
-    keeps = [*kept, None]
-    cames = [swap(v, "col", 1) for v in (first_away, *away)] + [None]
+    features += [arriving(own_features if ro == 2 else node_features, rels) for rels in owners[2:]]
+    away, kept = all_products(near, far, features[:2], limit)
+
+    keeps = [*kept, None, None]
+    cames = [swap(v, "col", 1) for v in (first_away, *away)] + [None, None]
     stages = co.bit_length() - 1
     done = [0] * 4
     turns = [0, 1, 0, 2, 1, 3, 2, 3] if stages == 2 else [0, 1, 2, 3] * stages
@@ -514,10 +517,10 @@
         keeps[i], last = halved(keeps[i], cames[i], before, cost)
         cames[i] = swap(last, "col", 2 << done[i])
         done[i] += 1
-        if turn == 0:
-            last_away, keeps[3] = last_products(near, far, features[3], limit, (last,))
-            cames[3] = swap(last_away, "col", 1)
-            last = keeps[3]
+        if turn < 2:
+            next_away, keeps[turn + 2] = last_products(near, far, features[turn + 2], limit, (last,))
+            cames[turn + 2] = swap(next_away, "col", 1)
+            last = keeps[turn + 2]
     totals = [[keep, came] for keep, came in zip(keeps, cames)]
 
     out_groups = ((3,), (2,), (1, 0))

time: 94.1 us -> 93.2 us (level)
    pallas_call x35 -> x36, Pallas kernels: 13.9 us -> 14.6 us  [call(): pl.pallas_call(run, out_shape=tuple(out_shape) if many else out_shape, in...]
  transfers between devices with their start and end apart: 35 -> 35, of which waited for: 19 -> 16; matrix products, arithmetic and copies ran while one was open for 0% -> 0% of each run, Pallas kernels for 12% -> 13%
where the time goes in v7:
time: 93.2 us; the launch traced here: 93 us
  waiting for transfers between devices  39 us (42%)
  starting transfers between devices  37.8 us (41%)
  Pallas kernels  14.6 us (16%)
  between operations  1.59 us (2%)
    ppermute x35, waiting for transfers between devices, swap(): return lax.ppermute(v, axis, [(i, i ^ bit) for i in range(size)])  39 us
    ppermute x35, starting transfers between devices, swap(): return lax.ppermute(v, axis, [(i, i ^ bit) for i in range(size)])  37.8 us
    pallas_call x36, Pallas kernels, call(): pl.pallas_call(run, out_shape=tuple(out_shape) if many else out_shape, in...  14.6 us
  transfers between devices with their start and end apart: 35, of which 16 were waited for; matrix products, arithmetic and copies ran while one was open for 0% of the time, Pallas kernels for 13%

profile of v7, /device:TPU:0, one launch (start us, length us, event | category | flops | bytes accessed | tf_op | source)
XLA Modules:
  0.0 93.0 jit_solution(14192026181642234436)
XLA Ops:
  1.8 3.6 %shard_map.85 = (bf16[1024,1024]{1,0:T(8,128)(2,1)S(1)}, bf16[1024,1024]{1,0:T(8,128)(2,1)S(1)}, bf16[1024,128]{1,0:T(8,128)(2,1)S(1)}, bf16[1024,128]{1,0:T(8,128)(2,1)S(1)}) custom-call(s32[1]{0:T(128)} %bitcast.7.refs_0_, s32[1]{0:T(128)} %bitcast.1.refs_1_.refs_0_, s32[1]{0:T(128)} %bitcast.2.refs_2_.refs_0_, s32[2,96]{1,0:T(2,128)} %bitcast.9, ...), custom_call_target="tpu_custom_call" | custom-call | tf_op jit(solution)/shard_map/pallas_call | solution.py:29
  5.4 1.7 %collective-permute-start.1 = (bf16[1024,128]{1,0:T(8,128)(2,1)S(1)}, bf16[1024,128]{1,0:T(8,128)(2,1)S(1)}, u32[]{:S(2)}, u32[]{:S(2)}) collective-permute-start(bf16[1024,128]{1,0:T(8,128)(2,1)S(1)} %get-tuple-element.48), channel_id=1, source_target_pairs={{0,1},{1,0},{2,3},{3,2},{4,5},{5,4},{6,7},{7,6},{8,9},{9,8},{10,11... | collective-permute-start | bytes 786440 | tf_op jit(solution)/shard_map/ppermute | solution.py:472
  7.1 2.2 %collective-permute-start.5 = (bf16[1024,128]{1,0:T(8,128)(2,1)S(1)}, bf16[1024,128]{1,0:T(8,128)(2,1)S(1)}, u32[]{:S(2)}, u32[]{:S(2)}) collective-permute-start(bf16[1024,128]{1,0:T(8,128)(2,1)S(1)} %get-tuple-element.46.refs_2_), channel_id=1, source_target_pairs={{0,16},{8,24},{16,0},{24,8},{1,17},{9,25},{17,1},{25,9},{2,18},{10... | collective-permute-start | bytes 786440 | tf_op jit(solution)/shard_map/ppermute | solution.py:472
  10.9 3.8 %collective-permute-done.1.refs_1_ = bf16[1024,128]{1,0:T(8,128)(2,1)S(1)} collective-permute-done((bf16[1024,128]{1,0:T(8,128)(2,1)S(1)}, bf16[1024,128]{1,0:T(8,128)(2,1)S(1)}, u32[]{:S(2)}, u32[]{:S(2)}) %collective-permute-start.1) | collective-permute-done | bytes 262176 | tf_op jit(solution)/shard_map/ppermute | solution.py:472
  14.7 1.7 %collective-permute-done.5.refs_2_ = bf16[1024,128]{1,0:T(8,128)(2,1)S(1)} collective-permute-done((bf16[1024,128]{1,0:T(8,128)(2,1)S(1)}, bf16[1024,128]{1,0:T(8,128)(2,1)S(1)}, u32[]{:S(2)}, u32[]{:S(2)}) %collective-permute-start.5) | collective-permute-done | bytes 262176 | tf_op jit(solution)/shard_map/ppermute | solution.py:472
  18.0 2.1 %collective-permute-start.2 = (bf16[512,128]{1,0:T(8,128)(2,1)S(1)}, bf16[512,128]{1,0:T(8,128)(2,1)S(1)}, u32[]{:S(2)}, u32[]{:S(2)}) collective-permute-start(bf16[512,128]{1,0:T(8,128)(2,1)S(1)} %get-tuple-element.50.refs_3_), channel_id=1, source_target_pairs={{0,2},{1,3},{2,0},{3,1},{4,6},{5,7},{6,4},{7,5},{8,10},{9,11},{10,... | collective-permute-start | bytes 393224 | tf_op jit(solution)/shard_map/ppermute | solution.py:472
  23.2 1.9 %collective-permute-start.7 = (bf16[512,128]{1,0:T(8,128)(2,1)S(1)}, bf16[512,128]{1,0:T(8,128)(2,1)S(1)}, u32[]{:S(2)}, u32[]{:S(2)}) collective-permute-start(bf16[512,128]{1,0:T(8,128)(2,1)S(1)} %get-tuple-element.54.refs_3_), channel_id=1, source_target_pairs={{0,2},{1,3},{2,0},{3,1},{4,6},{5,7},{6,4},{7,5},{8,10},{9,11},{10,... | collective-permute-start | bytes 393224 | tf_op jit(solution)/shard_map/ppermute | solution.py:472
  25.4 2.3 %collective-permute-start.10 = (bf16[512,128]{1,0:T(8,128)(2,1)S(1)}, bf16[512,128]{1,0:T(8,128)(2,1)S(1)}, u32[]{:S(2)}, u32[]{:S(2)}) collective-permute-start(bf16[512,128]{1,0:T(8,128)(2,1)S(1)} %get-tuple-element.60.refs_2_), channel_id=1, source_target_pairs={{0,2},{1,3},{2,0},{3,1},{4,6},{5,7},{6,4},{7,5},{8,10},{9,11},{10,... | collective-permute-start | bytes 393224 | tf_op jit(solution)/shard_map/ppermute | solution.py:472
  27.8 3.2 %collective-permute-start.6 = (bf16[256,128]{1,0:T(8,128)(2,1)S(1)}, bf16[256,128]{1,0:T(8,128)(2,1)S(1)}, u32[]{:S(2)}, u32[]{:S(2)}) collective-permute-start(bf16[256,128]{1,0:T(8,128)(2,1)S(1)} %get-tuple-element.57.refs_2_), channel_id=1, source_target_pairs={{0,4},{1,5},{2,6},{3,7},{4,0},{5,1},{6,2},{7,3},{8,12},{9,13},{10,... | collective-permute-start | bytes 196616 | tf_op jit(solution)/shard_map/ppermute | solution.py:472
  32.5 2.2 %collective-permute-start.13 = (bf16[512,128]{1,0:T(8,128)(2,1)S(1)}, bf16[512,128]{1,0:T(8,128)(2,1)S(1)}, u32[]{:S(2)}, u32[]{:S(2)}) collective-permute-start(bf16[512,128]{1,0:T(8,128)(2,1)S(1)} %get-tuple-element.65.refs_2_), channel_id=1, source_target_pairs={{0,2},{1,3},{2,0},{3,1},{4,6},{5,7},{6,4},{7,5},{8,10},{9,11},{10,... | collective-permute-start | bytes 393224 | tf_op jit(solution)/shard_map/ppermute | solution.py:472
  34.9 2.6 %collective-permute-done.9.refs_4_.refs_3_ = bf16[256,128]{1,0:T(8,128)(2,1)S(1)} collective-permute-done((bf16[256,128]{1,0:T(8,128)(2,1)S(1)}, bf16[256,128]{1,0:T(8,128)(2,1)S(1)}, u32[]{:S(2)}, u32[]{:S(2)}) %collective-permute-start.9) | collective-permute-done | bytes 65568 | tf_op jit(solution)/shard_map/ppermute | solution.py:472
  38.5 2.2 %collective-permute-start.14 = (bf16[256,128]{1,0:T(8,128)(2,1)S(1)}, bf16[256,128]{1,0:T(8,128)(2,1)S(1)}, u32[]{:S(2)}, u32[]{:S(2)}) collective-permute-start(bf16[256,128]{1,0:T(8,128)(2,1)S(1)} %get-tuple-element.70.refs_10_), channel_id=1, source_target_pairs={{0,4},{1,5},{2,6},{3,7},{4,0},{5,1},{6,2},{7,3},{8,12},{9,13},{10,... | collective-permute-start | bytes 196616 | tf_op jit(solution)/shard_map/ppermute | solution.py:472
  40.6 3.1 %collective-permute-done.12.refs_5_ = bf16[256,128]{1,0:T(8,128)(2,1)S(1)} collective-permute-done((bf16[256,128]{1,0:T(8,128)(2,1)S(1)}, bf16[256,128]{1,0:T(8,128)(2,1)S(1)}, u32[]{:S(2)}, u32[]{:S(2)}) %collective-permute-start.12) | collective-permute-done | bytes 65568 | tf_op jit(solution)/shard_map/ppermute | solution.py:472
  49.3 1.7 %collective-permute-start.16 = (bf16[2,64,512]{2,1,0:T(8,128)(2,1)S(1)}, bf16[2,64,512]{2,1,0:T(8,128)(2,1)S(1)}, u32[]{:S(2)}, u32[]{:S(2)}) collective-permute-start(bf16[2,64,512]{2,1,0:T(8,128)(2,1)S(1)} %get-tuple-element.77.refs_2_), channel_id=1, source_target_pairs={{0,1},{1,0},{2,3},{3,2},{4,5},{5,4},{6,7},{7,6},{8,9},{9,8},{10,11... | collective-permute-start | bytes 393224 | tf_op jit(solution)/shard_map/ppermute | solution.py:472
  52.2 1.6 %collective-permute-done.17.refs_1_ = bf16[1,128,256]{2,1,0:T(8,128)(2,1)S(1)} collective-permute-done((bf16[1,128,256]{2,1,0:T(8,128)(2,1)S(1)}, bf16[1,128,256]{2,1,0:T(8,128)(2,1)S(1)}, u32[]{:S(2)}, u32[]{:S(2)}) %collective-permute-start.17) | collective-permute-done | bytes 65568 | tf_op jit(solution)/shard_map/ppermute | solution.py:472
  56.1 1.9 %collective-permute-start.19 = (bf16[64,512]{1,0:T(8,128)(2,1)S(1)}, bf16[64,512]{1,0:T(8,128)(2,1)S(1)}, u32[]{:S(2)}, u32[]{:S(2)}) collective-permute-start(bf16[64,512]{1,0:T(8,128)(2,1)S(1)} %get-tuple-element.81), channel_id=1, source_target_pairs={{0,16},{8,24},{16,0},{24,8},{1,17},{9,25},{17,1},{25,9},{2,18},{10... | collective-permute-start | bytes 196616 | tf_op jit(solution)/shard_map/ppermute | solution.py:472
  58.0 5.7 %collective-permute-done.21.refs_1_ = bf16[1,256,256]{2,1,0:T(8,128)(2,1)S(1)} collective-permute-done((bf16[1,256,256]{2,1,0:T(8,128)(2,1)S(1)}, bf16[1,256,256]{2,1,0:T(8,128)(2,1)S(1)}, u32[]{:S(2)}, u32[]{:S(2)}) %collective-permute-start.21) | collective-permute-done | bytes 131104 | tf_op jit(solution)/shard_map/ppermute | solution.py:472
  64.3 2.1 %collective-permute-start.22 = (bf16[64,512]{1,0:T(8,128)(2,1)S(1)}, bf16[64,512]{1,0:T(8,128)(2,1)S(1)}, u32[]{:S(2)}, u32[]{:S(2)}) collective-permute-start(bf16[64,512]{1,0:T(8,128)(2,1)S(1)} %shard_map.106.refs_2_.refs_0_), channel_id=1, source_target_pairs={{0,4},{1,5},{2,6},{3,7},{4,0},{5,1},{6,2},{7,3},{8,12},{9,13},{10,... | collective-permute-start | bytes 196616 | tf_op jit(solution)/shard_map/ppermute | solution.py:472
  66.6 7.1 %collective-permute-done.23.refs_1_ = bf16[2,256,256]{2,1,0:T(8,128)(2,1)S(1)} collective-permute-done((bf16[2,256,256]{2,1,0:T(8,128)(2,1)S(1)}, bf16[2,256,256]{2,1,0:T(8,128)(2,1)S(1)}, u32[]{:S(2)}, u32[]{:S(2)}) %collective-permute-start.23) | collective-permute-done | bytes 262176 | tf_op jit(solution)/shard_map/ppermute | solution.py:472
  74.7 4.6 %collective-permute-done.25.refs_1_ = f32[64,512]{1,0:T(8,128)S(1)} collective-permute-done((f32[64,512]{1,0:T(8,128)S(1)}, f32[64,512]{1,0:T(8,128)S(1)}, u32[]{:S(2)}, u32[]{:S(2)}) %collective-permute-start.25) | collective-permute-done | bytes 131104 | tf_op jit(solution)/shard_map/ppermute | solution.py:472
  79.4 1.7 %collective-permute-start.27 = (bf16[64,512]{1,0:T(8,128)(2,1)S(1)}, bf16[64,512]{1,0:T(8,128)(2,1)S(1)}, u32[]{:S(2)}, u32[]{:S(2)}) collective-permute-start(bf16[64,512]{1,0:T(8,128)(2,1)S(1)} %shard_map.111.refs_2_.refs_0_), channel_id=1, source_target_pairs={{0,16},{8,24},{16,0},{24,8},{1,17},{9,25},{17,1},{25,9},{2,18},{10... | collective-permute-start | bytes 196616 | tf_op jit(solution)/shard_map/ppermute | solution.py:472
  82.4 2.1 %collective-permute-done.27.refs_1_ = bf16[64,512]{1,0:T(8,128)(2,1)S(1)} collective-permute-done((bf16[64,512]{1,0:T(8,128)(2,1)S(1)}, bf16[64,512]{1,0:T(8,128)(2,1)S(1)}, u32[]{:S(2)}, u32[]{:S(2)}) %collective-permute-start.27) | collective-permute-done | bytes 65568 | tf_op jit(solution)/shard_map/ppermute | solution.py:472
  87.3 2.2 %collective-permute-done.30.refs_1_ = bf16[2,64,512]{2,1,0:T(8,128)(2,1)S(1)} collective-permute-done((bf16[2,64,512]{2,1,0:T(8,128)(2,1)S(1)}, bf16[2,64,512]{2,1,0:T(8,128)(2,1)S(1)}, u32[]{:S(2)}, u32[]{:S(2)}) %collective-permute-start.30) | collective-permute-done | bytes 131104 | tf_op jit(solution)/shard_map/ppermute | solution.py:472
  89.6 1.5 %collective-permute-done.32.refs_3_ = bf16[2,2,64,512]{3,2,1,0:T(8,128)(2,1)S(1)} collective-permute-done((bf16[2,2,64,512]{3,2,1,0:T(8,128)(2,1)S(1)}, bf16[2,2,64,512]{3,2,1,0:T(8,128)(2,1)S(1)}, u32[]{:S(2)}, u32[]{:S(2)}) %collective-permute-start.32) | collective-permute-done | bytes 262176 | tf_op jit(solution)/shard_map/ppermute | solution.py:472
  (86 shorter events, 26.7 us)
Async XLA Ops:
  0.6 8.7 %collective-permute-start = (bf16[1024,128]{1,0:T(8,128)(2,1)}, bf16[1024,128]{1,0:T(8,128)(2,1)S(1)}, u32[]{:S(2)}, u32[]{:S(2)}) collective-permute-start(bf16[1024,128]{1,0:T(8,128)(2,1)} %refs_5_.1), channel_id=1, source_target_pairs={{0,8},{8,0},{16,24},{24,16},{1,9},{9,1},{17,25},{25,17},{2,10},{10... | collective-permute-start | bytes 786440 | tf_op jit(solution)/shard_map/ppermute | solution.py:472
  5.4 9.2 %collective-permute-start.1 = (bf16[1024,128]{1,0:T(8,128)(2,1)S(1)}, bf16[1024,128]{1,0:T(8,128)(2,1)S(1)}, u32[]{:S(2)}, u32[]{:S(2)}) collective-permute-start(bf16[1024,128]{1,0:T(8,128)(2,1)S(1)} %get-tuple-element.48), channel_id=1, source_target_pairs={{0,1},{1,0},{2,3},{3,2},{4,5},{5,4},{6,7},{7,6},{8,9},{9,8},{10,11... | collective-permute-start | bytes 786440 | tf_op jit(solution)/shard_map/ppermute | solution.py:472
  7.1 9.3 %collective-permute-start.5 = (bf16[1024,128]{1,0:T(8,128)(2,1)S(1)}, bf16[1024,128]{1,0:T(8,128)(2,1)S(1)}, u32[]{:S(2)}, u32[]{:S(2)}) collective-permute-start(bf16[1024,128]{1,0:T(8,128)(2,1)S(1)} %get-tuple-element.46.refs_2_), channel_id=1, source_target_pairs={{0,16},{8,24},{16,0},{24,8},{1,17},{9,25},{17,1},{25,9},{2,18},{10... | collective-permute-start | bytes 786440 | tf_op jit(solution)/shard_map/ppermute | solution.py:472
  10.6 9.4 %collective-permute-start.4 = (bf16[1024,128]{1,0:T(8,128)(2,1)S(1)}, bf16[1024,128]{1,0:T(8,128)(2,1)S(1)}, u32[]{:S(2)}, u32[]{:S(2)}) collective-permute-start(bf16[1024,128]{1,0:T(8,128)(2,1)S(1)} %get-tuple-element.52), channel_id=1, source_target_pairs={{0,1},{1,0},{2,3},{3,2},{4,5},{5,4},{6,7},{7,6},{8,9},{9,8},{10,11... | collective-permute-start | bytes 786440 | tf_op jit(solution)/shard_map/ppermute | solution.py:472
  10.8 10.3 %collective-permute-start.3 = (bf16[1024,128]{1,0:T(8,128)(2,1)S(1)}, bf16[1024,128]{1,0:T(8,128)(2,1)S(1)}, u32[]{:S(2)}, u32[]{:S(2)}) collective-permute-start(bf16[1024,128]{1,0:T(8,128)(2,1)S(1)} %get-tuple-element.46.refs_2_), channel_id=1, source_target_pairs={{0,24},{8,16},{16,8},{24,0},{1,25},{9,17},{17,9},{25,1},{2,26},{10... | collective-permute-start | bytes 786440 | tf_op jit(solution)/shard_map/ppermute | solution.py:472
  17.7 7.7 %collective-permute-start.8 = (bf16[1024,128]{1,0:T(8,128)(2,1)S(1)}, bf16[1024,128]{1,0:T(8,128)(2,1)S(1)}, u32[]{:S(2)}, u32[]{:S(2)}) collective-permute-start(bf16[1024,128]{1,0:T(8,128)(2,1)S(1)} %get-tuple-element.59), channel_id=1, source_target_pairs={{0,1},{1,0},{2,3},{3,2},{4,5},{5,4},{6,7},{7,6},{8,9},{9,8},{10,11... | collective-permute-start | bytes 786440 | tf_op jit(solution)/shard_map/ppermute | solution.py:472
  18.0 7.1 %collective-permute-start.2 = (bf16[512,128]{1,0:T(8,128)(2,1)S(1)}, bf16[512,128]{1,0:T(8,128)(2,1)S(1)}, u32[]{:S(2)}, u32[]{:S(2)}) collective-permute-start(bf16[512,128]{1,0:T(8,128)(2,1)S(1)} %get-tuple-element.50.refs_3_), channel_id=1, source_target_pairs={{0,2},{1,3},{2,0},{3,1},{4,6},{5,7},{6,4},{7,5},{8,10},{9,11},{10,... | collective-permute-start | bytes 393224 | tf_op jit(solution)/shard_map/ppermute | solution.py:472
  22.4 10.1 %collective-permute-start.11 = (bf16[1024,128]{1,0:T(8,128)(2,1)S(1)}, bf16[1024,128]{1,0:T(8,128)(2,1)S(1)}, u32[]{:S(2)}, u32[]{:S(2)}) collective-permute-start(bf16[1024,128]{1,0:T(8,128)(2,1)S(1)} %get-tuple-element.64), channel_id=1, source_target_pairs={{0,1},{1,0},{2,3},{3,2},{4,5},{5,4},{6,7},{7,6},{8,9},{9,8},{10,11... | collective-permute-start | bytes 786440 | tf_op jit(solution)/shard_map/ppermute | solution.py:472
  23.2 7.8 %collective-permute-start.7 = (bf16[512,128]{1,0:T(8,128)(2,1)S(1)}, bf16[512,128]{1,0:T(8,128)(2,1)S(1)}, u32[]{:S(2)}, u32[]{:S(2)}) collective-permute-start(bf16[512,128]{1,0:T(8,128)(2,1)S(1)} %get-tuple-element.54.refs_3_), channel_id=1, source_target_pairs={{0,2},{1,3},{2,0},{3,1},{4,6},{5,7},{6,4},{7,5},{8,10},{9,11},{10,... | collective-permute-start | bytes 393224 | tf_op jit(solution)/shard_map/ppermute | solution.py:472
  25.4 9.4 %collective-permute-start.10 = (bf16[512,128]{1,0:T(8,128)(2,1)S(1)}, bf16[512,128]{1,0:T(8,128)(2,1)S(1)}, u32[]{:S(2)}, u32[]{:S(2)}) collective-permute-start(bf16[512,128]{1,0:T(8,128)(2,1)S(1)} %get-tuple-element.60.refs_2_), channel_id=1, source_target_pairs={{0,2},{1,3},{2,0},{3,1},{4,6},{5,7},{6,4},{7,5},{8,10},{9,11},{10,... | collective-permute-start | bytes 393224 | tf_op jit(solution)/shard_map/ppermute | solution.py:472
  27.8 7.1 %collective-permute-start.6 = (bf16[256,128]{1,0:T(8,128)(2,1)S(1)}, bf16[256,128]{1,0:T(8,128)(2,1)S(1)}, u32[]{:S(2)}, u32[]{:S(2)}) collective-permute-start(bf16[256,128]{1,0:T(8,128)(2,1)S(1)} %get-tuple-element.57.refs_2_), channel_id=1, source_target_pairs={{0,4},{1,5},{2,6},{3,7},{4,0},{5,1},{6,2},{7,3},{8,12},{9,13},{10,... | collective-permute-start | bytes 196616 | tf_op jit(solution)/shard_map/ppermute | solution.py:472
  46.9 6.8 %collective-permute-start.17 = (bf16[1,128,256]{2,1,0:T(8,128)(2,1)S(1)}, bf16[1,128,256]{2,1,0:T(8,128)(2,1)S(1)}, u32[]{:S(2)}, u32[]{:S(2)}) collective-permute-start(bf16[1,128,256]{2,1,0:T(8,128)(2,1)S(1)} %get-tuple-element.78.refs_0_), channel_id=1, source_target_pairs={{0,4},{1,5},{2,6},{3,7},{4,0},{5,1},{6,2},{7,3},{8,12},{9,13},{10,... | collective-permute-start | bytes 196616 | tf_op jit(solution)/shard_map/ppermute | solution.py:472
  49.3 6.8 %collective-permute-start.16 = (bf16[2,64,512]{2,1,0:T(8,128)(2,1)S(1)}, bf16[2,64,512]{2,1,0:T(8,128)(2,1)S(1)}, u32[]{:S(2)}, u32[]{:S(2)}) collective-permute-start(bf16[2,64,512]{2,1,0:T(8,128)(2,1)S(1)} %get-tuple-element.77.refs_2_), channel_id=1, source_target_pairs={{0,1},{1,0},{2,3},{3,2},{4,5},{5,4},{6,7},{7,6},{8,9},{9,8},{10,11... | collective-permute-start | bytes 393224 | tf_op jit(solution)/shard_map/ppermute | solution.py:472
  51.0 12.7 %collective-permute-start.21 = (bf16[1,256,256]{2,1,0:T(8,128)(2,1)S(1)}, bf16[1,256,256]{2,1,0:T(8,128)(2,1)S(1)}, u32[]{:S(2)}, u32[]{:S(2)}) collective-permute-start(bf16[1,256,256]{2,1,0:T(8,128)(2,1)S(1)} %get-tuple-element.82.refs_0_), channel_id=1, source_target_pairs={{0,4},{1,5},{2,6},{3,7},{4,0},{5,1},{6,2},{7,3},{8,12},{9,13},{10,... | collective-permute-start | bytes 393224 | tf_op jit(solution)/shard_map/ppermute | solution.py:472
  53.8 10.0 %collective-permute-start.20 = (bf16[2,128,256]{2,1,0:T(8,128)(2,1)S(1)}, bf16[2,128,256]{2,1,0:T(8,128)(2,1)S(1)}, u32[]{:S(2)}, u32[]{:S(2)}) collective-permute-start(bf16[2,128,256]{2,1,0:T(8,128)(2,1)S(1)} %shard_map.102.refs_2_.refs_0_), channel_id=1, source_target_pairs={{0,2},{1,3},{2,0},{3,1},{4,6},{5,7},{6,4},{7,5},{8,10},{9,11},{10,... | collective-permute-start | bytes 393224 | tf_op jit(solution)/shard_map/ppermute | solution.py:472
  54.7 11.8 %collective-permute-start.24 = (bf16[2,128,256]{2,1,0:T(8,128)(2,1)S(1)}, bf16[2,128,256]{2,1,0:T(8,128)(2,1)S(1)}, u32[]{:S(2)}, u32[]{:S(2)}) collective-permute-start(bf16[2,128,256]{2,1,0:T(8,128)(2,1)S(1)} %shard_map.101.refs_2_.refs_0_), channel_id=1, source_target_pairs={{0,4},{1,5},{2,6},{3,7},{4,0},{5,1},{6,2},{7,3},{8,12},{9,13},{10,... | collective-permute-start | bytes 393224 | tf_op jit(solution)/shard_map/ppermute | solution.py:472
  56.1 8.2 %collective-permute-start.19 = (bf16[64,512]{1,0:T(8,128)(2,1)S(1)}, bf16[64,512]{1,0:T(8,128)(2,1)S(1)}, u32[]{:S(2)}, u32[]{:S(2)}) collective-permute-start(bf16[64,512]{1,0:T(8,128)(2,1)S(1)} %get-tuple-element.81), channel_id=1, source_target_pairs={{0,16},{8,24},{16,0},{24,8},{1,17},{9,25},{17,1},{25,9},{2,18},{10... | collective-permute-start | bytes 196616 | tf_op jit(solution)/shard_map/ppermute | solution.py:472
  63.7 9.9 %collective-permute-start.23 = (bf16[2,256,256]{2,1,0:T(8,128)(2,1)S(1)}, bf16[2,256,256]{2,1,0:T(8,128)(2,1)S(1)}, u32[]{:S(2)}, u32[]{:S(2)}) collective-permute-start(bf16[2,256,256]{2,1,0:T(8,128)(2,1)S(1)} %shard_map.104.refs_2_.refs_0_), channel_id=1, source_target_pairs={{0,2},{1,3},{2,0},{3,1},{4,6},{5,7},{6,4},{7,5},{8,10},{9,11},{10,... | collective-permute-start | bytes 786440 | tf_op jit(solution)/shard_map/ppermute | solution.py:472
  63.8 10.0 %collective-permute-start.26 = (bf16[4,128,256]{2,1,0:T(8,128)(2,1)S(1)}, bf16[4,128,256]{2,1,0:T(8,128)(2,1)S(1)}, u32[]{:S(2)}, u32[]{:S(2)}) collective-permute-start(bf16[4,128,256]{2,1,0:T(8,128)(2,1)S(1)} %shard_map.105.refs_2_), channel_id=1, source_target_pairs={{0,1},{1,0},{2,3},{3,2},{4,5},{5,4},{6,7},{7,6},{8,9},{9,8},{10,11... | collective-permute-start | bytes 786440 | tf_op jit(solution)/shard_map/ppermute | solution.py:472
  64.3 9.4 %collective-permute-start.22 = (bf16[64,512]{1,0:T(8,128)(2,1)S(1)}, bf16[64,512]{1,0:T(8,128)(2,1)S(1)}, u32[]{:S(2)}, u32[]{:S(2)}) collective-permute-start(bf16[64,512]{1,0:T(8,128)(2,1)S(1)} %shard_map.106.refs_2_.refs_0_), channel_id=1, source_target_pairs={{0,4},{1,5},{2,6},{3,7},{4,0},{5,1},{6,2},{7,3},{8,12},{9,13},{10,... | collective-permute-start | bytes 196616 | tf_op jit(solution)/shard_map/ppermute | solution.py:472
  66.5 14.6 %collective-permute-start.28 = (bf16[4,128,256]{2,1,0:T(8,128)(2,1)S(1)}, bf16[4,128,256]{2,1,0:T(8,128)(2,1)S(1)}, u32[]{:S(2)}, u32[]{:S(2)}) collective-permute-start(bf16[4,128,256]{2,1,0:T(8,128)(2,1)S(1)} %shard_map.107.refs_2_.refs_0_), channel_id=1, source_target_pairs={{0,2},{1,3},{2,0},{3,1},{4,6},{5,7},{6,4},{7,5},{8,10},{9,11},{10,... | collective-permute-start | bytes 786440 | tf_op jit(solution)/shard_map/ppermute | solution.py:472
  73.7 12.2 %collective-permute-start.31 = (bf16[4,256,256]{2,1,0:T(8,128)(2,1)S(1)}, bf16[4,256,256]{2,1,0:T(8,128)(2,1)S(1)}, u32[]{:S(2)}, u32[]{:S(2)}) collective-permute-start(bf16[4,256,256]{2,1,0:T(8,128)(2,1)S(1)} %shard_map.108.refs_2_), channel_id=1, source_target_pairs={{0,1},{1,0},{2,3},{3,2},{4,5},{5,4},{6,7},{7,6},{8,9},{9,8},{10,11... | collective-permute-start | bytes 1572872 | tf_op jit(solution)/shard_map/ppermute | solution.py:472
  74.6 7.2 %collective-permute-start.29 = (bf16[128,1024]{1,0:T(8,128)(2,1)S(1)}, bf16[128,1024]{1,0:T(8,128)(2,1)S(1)}, u32[]{:S(2)}, u32[]{:S(2)}) collective-permute-start(bf16[128,1024]{1,0:T(8,128)(2,1)S(1)} %shard_map.110.refs_2_), channel_id=1, source_target_pairs={{0,8},{8,0},{16,24},{24,16},{1,9},{9,1},{17,25},{25,17},{2,10},{10... | collective-permute-start | bytes 786440 | tf_op jit(solution)/shard_map/ppermute | solution.py:472
  81.9 7.7 %collective-permute-start.34 = (bf16[128,1024]{1,0:T(8,128)(2,1)S(1)}, bf16[128,1024]{1,0:T(8,128)(2,1)S(1)}, u32[]{:S(2)}, u32[]{:S(2)}) collective-permute-start(bf16[128,1024]{1,0:T(8,128)(2,1)S(1)} %shard_map.114.refs_2_), channel_id=1, source_target_pairs={{0,16},{8,24},{16,0},{24,8},{1,17},{9,25},{17,1},{25,9},{2,18},{10... | collective-permute-start | bytes 786440 | tf_op jit(solution)/shard_map/ppermute | solution.py:472
  (13 other events, 63.4 us)

commit v8 on v7

--- a/solution.py
+++ b/solution.py
@@ -457,6 +457,11 @@
                 )
 
 
+def finish_both(me_ref, side_ref, own_ref, other_ref, *refs):
+    place_shares(me_ref, side_ref, own_ref, other_ref, refs[-2])
+    finish(*refs[:-2], refs[-1])
+
+
 def body(node_features, layer_weight, tile_values, tile_coords, tile_count, cotangent):
     n_row = lax.axis_size("row")
     n_col = lax.axis_size("col")
@@ -645,18 +650,15 @@
     weight_stack("row")
     send_parts(0)
     state["last"] = marked(state["last"], *arrived, cost=COST)
-    grad_features = call(
-        finish,
-        jax.ShapeDtypeStruct((block_c, piece), BF16),
-        [VMEM] * (2 + len(arrived)),
-        (backs[0, 0], backs[0, 1], *arrived),
+    grad_weight, grad_features = call(
+        finish_both,
+        (
+            jax.ShapeDtypeStruct((width, width), F32),
+            jax.ShapeDtypeStruct((block_c, piece), BF16),
+        ),
+        [SMEM, SMEM] + [VMEM] * (4 + len(arrived)),
+        (my_row, my_col, *state["w"], backs[0, 0], backs[0, 1], *arrived),
         before=order(),
-    )
-    grad_weight = call(
-        place_shares,
-        jax.ShapeDtypeStruct((width, width), F32),
-        [SMEM, SMEM, VMEM, VMEM],
-        (my_row, my_col, *state["w"]),
     )
     return (hidden, grad_weight, grad_features)
 

time: 93.2 us -> 93 us (level)
  waiting for transfers between devices: 39 us -> 40.6 us
  starting transfers between devices: 37.8 us -> 36.6 us
    ppermute x35, waiting for transfers between devices: 39 us -> 40.6 us  [swap(): return lax.ppermute(v, axis, [(i, i ^ bit) for i in range(size)])]
    ppermute x35, starting transfers between devices: 37.8 us -> 36.6 us  [swap(): return lax.ppermute(v, axis, [(i, i ^ bit) for i in range(size)])]
    pallas_call x36 -> x35, Pallas kernels: 14.6 us -> 13.9 us  [call(): pl.pallas_call(run, out_shape=tuple(out_shape) if many else out_shape, in...]
  transfers between devices with their start and end apart: 35 -> 35, of which waited for: 16 -> 18; matrix products, arithmetic and copies ran while one was open for 0% -> 0% of each run, Pallas kernels for 13% -> 12%
where the time goes in v8:
time: 93 us; the launch traced here: 92.7 us
  waiting for transfers between devices  40.6 us (44%)
  starting transfers between devices  36.6 us (39%)
  Pallas kernels  13.9 us (15%)
  between operations  1.57 us (2%)
    ppermute x35, waiting for transfers between devices, swap(): return lax.ppermute(v, axis, [(i, i ^ bit) for i in range(size)])  40.6 us
    ppermute x35, starting transfers between devices, swap(): return lax.ppermute(v, axis, [(i, i ^ bit) for i in range(size)])  36.6 us
    pallas_call x35, Pallas kernels, call(): pl.pallas_call(run, out_shape=tuple(out_shape) if many else out_shape, in...  13.9 us
  transfers between devices with their start and end apart: 35, of which 18 were waited for; matrix products, arithmetic and copies ran while one was open for 0% of the time, Pallas kernels for 12%

profile of v8, /device:TPU:0, one launch (start us, length us, event | category | flops | bytes accessed | tf_op | source)
XLA Modules:
  0.0 92.7 jit_solution(4913430704377805185)
XLA Ops:
  1.8 3.6 %shard_map.85 = (bf16[1024,1024]{1,0:T(8,128)(2,1)S(1)}, bf16[1024,1024]{1,0:T(8,128)(2,1)S(1)}, bf16[1024,128]{1,0:T(8,128)(2,1)S(1)}, bf16[1024,128]{1,0:T(8,128)(2,1)S(1)}) custom-call(s32[1]{0:T(128)} %bitcast.7.refs_0_, s32[1]{0:T(128)} %bitcast.1.refs_1_.refs_0_, s32[1]{0:T(128)} %bitcast.2.refs_2_.refs_0_, s32[2,96]{1,0:T(2,128)} %bitcast.9, ...), custom_call_target="tpu_custom_call" | custom-call | tf_op jit(solution)/shard_map/pallas_call | solution.py:29
  5.4 1.7 %collective-permute-start.1 = (bf16[1024,128]{1,0:T(8,128)(2,1)S(1)}, bf16[1024,128]{1,0:T(8,128)(2,1)S(1)}, u32[]{:S(2)}, u32[]{:S(2)}) collective-permute-start(bf16[1024,128]{1,0:T(8,128)(2,1)S(1)} %get-tuple-element.50), channel_id=1, source_target_pairs={{0,1},{1,0},{2,3},{3,2},{4,5},{5,4},{6,7},{7,6},{8,9},{9,8},{10,11... | collective-permute-start | bytes 786440 | tf_op jit(solution)/shard_map/ppermute | solution.py:477
  7.1 1.9 %collective-permute-start.5 = (bf16[1024,128]{1,0:T(8,128)(2,1)S(1)}, bf16[1024,128]{1,0:T(8,128)(2,1)S(1)}, u32[]{:S(2)}, u32[]{:S(2)}) collective-permute-start(bf16[1024,128]{1,0:T(8,128)(2,1)S(1)} %get-tuple-element.48.refs_2_), channel_id=1, source_target_pairs={{0,16},{8,24},{16,0},{24,8},{1,17},{9,25},{17,1},{25,9},{2,18},{10... | collective-permute-start | bytes 786440 | tf_op jit(solution)/shard_map/ppermute | solution.py:477
  10.9 3.8 %collective-permute-done.1.refs_1_ = bf16[1024,128]{1,0:T(8,128)(2,1)S(1)} collective-permute-done((bf16[1024,128]{1,0:T(8,128)(2,1)S(1)}, bf16[1024,128]{1,0:T(8,128)(2,1)S(1)}, u32[]{:S(2)}, u32[]{:S(2)}) %collective-permute-start.1) | collective-permute-done | bytes 262176 | tf_op jit(solution)/shard_map/ppermute | solution.py:477
  14.7 1.5 %collective-permute-done.5.refs_2_ = bf16[1024,128]{1,0:T(8,128)(2,1)S(1)} collective-permute-done((bf16[1024,128]{1,0:T(8,128)(2,1)S(1)}, bf16[1024,128]{1,0:T(8,128)(2,1)S(1)}, u32[]{:S(2)}, u32[]{:S(2)}) %collective-permute-start.5) | collective-permute-done | bytes 262176 | tf_op jit(solution)/shard_map/ppermute | solution.py:477
  18.0 1.9 %collective-permute-start.2 = (bf16[512,128]{1,0:T(8,128)(2,1)S(1)}, bf16[512,128]{1,0:T(8,128)(2,1)S(1)}, u32[]{:S(2)}, u32[]{:S(2)}) collective-permute-start(bf16[512,128]{1,0:T(8,128)(2,1)S(1)} %get-tuple-element.52.refs_3_), channel_id=1, source_target_pairs={{0,2},{1,3},{2,0},{3,1},{4,6},{5,7},{6,4},{7,5},{8,10},{9,11},{10,... | collective-permute-start | bytes 393224 | tf_op jit(solution)/shard_map/ppermute | solution.py:477
  23.3 2.1 %collective-permute-start.7 = (bf16[512,128]{1,0:T(8,128)(2,1)S(1)}, bf16[512,128]{1,0:T(8,128)(2,1)S(1)}, u32[]{:S(2)}, u32[]{:S(2)}) collective-permute-start(bf16[512,128]{1,0:T(8,128)(2,1)S(1)} %get-tuple-element.56.refs_3_), channel_id=1, source_target_pairs={{0,2},{1,3},{2,0},{3,1},{4,6},{5,7},{6,4},{7,5},{8,10},{9,11},{10,... | collective-permute-start | bytes 393224 | tf_op jit(solution)/shard_map/ppermute | solution.py:477
  26.0 2.7 %collective-permute-start.10 = (bf16[512,128]{1,0:T(8,128)(2,1)S(1)}, bf16[512,128]{1,0:T(8,128)(2,1)S(1)}, u32[]{:S(2)}, u32[]{:S(2)}) collective-permute-start(bf16[512,128]{1,0:T(8,128)(2,1)S(1)} %get-tuple-element.62.refs_2_), channel_id=1, source_target_pairs={{0,2},{1,3},{2,0},{3,1},{4,6},{5,7},{6,4},{7,5},{8,10},{9,11},{10,... | collective-permute-start | bytes 393224 | tf_op jit(solution)/shard_map/ppermute | solution.py:477
  28.7 1.7 %collective-permute-start.6 = (bf16[256,128]{1,0:T(8,128)(2,1)S(1)}, bf16[256,128]{1,0:T(8,128)(2,1)S(1)}, u32[]{:S(2)}, u32[]{:S(2)}) collective-permute-start(bf16[256,128]{1,0:T(8,128)(2,1)S(1)} %get-tuple-element.59.refs_2_), channel_id=1, source_target_pairs={{0,4},{1,5},{2,6},{3,7},{4,0},{5,1},{6,2},{7,3},{8,12},{9,13},{10,... | collective-permute-start | bytes 196616 | tf_op jit(solution)/shard_map/ppermute | solution.py:477
  30.5 2.0 %collective-permute-start.9 = (bf16[256,128]{1,0:T(8,128)(2,1)S(1)}, bf16[256,128]{1,0:T(8,128)(2,1)S(1)}, u32[]{:S(2)}, u32[]{:S(2)}) collective-permute-start(bf16[256,128]{1,0:T(8,128)(2,1)S(1)} %get-tuple-element.64.refs_2_), channel_id=1, source_target_pairs={{0,4},{1,5},{2,6},{3,7},{4,0},{5,1},{6,2},{7,3},{8,12},{9,13},{10,... | collective-permute-start | bytes 196616 | tf_op jit(solution)/shard_map/ppermute | solution.py:477
  32.6 2.1 %collective-permute-start.13 = (bf16[512,128]{1,0:T(8,128)(2,1)S(1)}, bf16[512,128]{1,0:T(8,128)(2,1)S(1)}, u32[]{:S(2)}, u32[]{:S(2)}) collective-permute-start(bf16[512,128]{1,0:T(8,128)(2,1)S(1)} %get-tuple-element.67.refs_2_), channel_id=1, source_target_pairs={{0,2},{1,3},{2,0},{3,1},{4,6},{5,7},{6,4},{7,5},{8,10},{9,11},{10,... | collective-permute-start | bytes 393224 | tf_op jit(solution)/shard_map/ppermute | solution.py:477
  34.7 2.3 %collective-permute-done.6.refs_3_.refs_1_ = bf16[256,128]{1,0:T(8,128)(2,1)S(1)} collective-permute-done((bf16[256,128]{1,0:T(8,128)(2,1)S(1)}, bf16[256,128]{1,0:T(8,128)(2,1)S(1)}, u32[]{:S(2)}, u32[]{:S(2)}) %collective-permute-start.6) | collective-permute-done | bytes 65568 | tf_op jit(solution)/shard_map/ppermute | solution.py:477
  38.7 2.2 %collective-permute-start.14 = (bf16[256,128]{1,0:T(8,128)(2,1)S(1)}, bf16[256,128]{1,0:T(8,128)(2,1)S(1)}, u32[]{:S(2)}, u32[]{:S(2)}) collective-permute-start(bf16[256,128]{1,0:T(8,128)(2,1)S(1)} %get-tuple-element.72.refs_10_), channel_id=1, source_target_pairs={{0,4},{1,5},{2,6},{3,7},{4,0},{5,1},{6,2},{7,3},{8,12},{9,13},{10,... | collective-permute-start | bytes 196616 | tf_op jit(solution)/shard_map/ppermute | solution.py:477
  40.9 3.0 %collective-permute-done.12.refs_5_ = bf16[256,128]{1,0:T(8,128)(2,1)S(1)} collective-permute-done((bf16[256,128]{1,0:T(8,128)(2,1)S(1)}, bf16[256,128]{1,0:T(8,128)(2,1)S(1)}, u32[]{:S(2)}, u32[]{:S(2)}) %collective-permute-start.12) | collective-permute-done | bytes 65568 | tf_op jit(solution)/shard_map/ppermute | solution.py:477
  43.9 1.4 %collective-permute-done.14.refs_7_ = bf16[256,128]{1,0:T(8,128)(2,1)S(1)} collective-permute-done((bf16[256,128]{1,0:T(8,128)(2,1)S(1)}, bf16[256,128]{1,0:T(8,128)(2,1)S(1)}, u32[]{:S(2)}, u32[]{:S(2)}) %collective-permute-start.14) | collective-permute-done | bytes 65568 | tf_op jit(solution)/shard_map/ppermute | solution.py:477
  49.5 1.6 %collective-permute-start.16 = (bf16[2,64,512]{2,1,0:T(8,128)(2,1)S(1)}, bf16[2,64,512]{2,1,0:T(8,128)(2,1)S(1)}, u32[]{:S(2)}, u32[]{:S(2)}) collective-permute-start(bf16[2,64,512]{2,1,0:T(8,128)(2,1)S(1)} %get-tuple-element.79.refs_2_), channel_id=1, source_target_pairs={{0,1},{1,0},{2,3},{3,2},{4,5},{5,4},{6,7},{7,6},{8,9},{9,8},{10,11... | collective-permute-start | bytes 393224 | tf_op jit(solution)/shard_map/ppermute | solution.py:477
  52.5 1.4 %collective-permute-done.17.refs_1_ = bf16[1,128,256]{2,1,0:T(8,128)(2,1)S(1)} collective-permute-done((bf16[1,128,256]{2,1,0:T(8,128)(2,1)S(1)}, bf16[1,128,256]{2,1,0:T(8,128)(2,1)S(1)}, u32[]{:S(2)}, u32[]{:S(2)}) %collective-permute-start.17) | collective-permute-done | bytes 65568 | tf_op jit(solution)/shard_map/ppermute | solution.py:477
  57.6 6.2 %collective-permute-done.21.refs_1_ = bf16[1,256,256]{2,1,0:T(8,128)(2,1)S(1)} collective-permute-done((bf16[1,256,256]{2,1,0:T(8,128)(2,1)S(1)}, bf16[1,256,256]{2,1,0:T(8,128)(2,1)S(1)}, u32[]{:S(2)}, u32[]{:S(2)}) %collective-permute-start.21) | collective-permute-done | bytes 131104 | tf_op jit(solution)/shard_map/ppermute | solution.py:477
  67.0 6.8 %collective-permute-done.23.refs_1_ = bf16[2,256,256]{2,1,0:T(8,128)(2,1)S(1)} collective-permute-done((bf16[2,256,256]{2,1,0:T(8,128)(2,1)S(1)}, bf16[2,256,256]{2,1,0:T(8,128)(2,1)S(1)}, u32[]{:S(2)}, u32[]{:S(2)}) %collective-permute-start.23) | collective-permute-done | bytes 262176 | tf_op jit(solution)/shard_map/ppermute | solution.py:477
  74.9 4.8 %collective-permute-done.25.refs_1_ = f32[64,512]{1,0:T(8,128)S(1)} collective-permute-done((f32[64,512]{1,0:T(8,128)S(1)}, f32[64,512]{1,0:T(8,128)S(1)}, u32[]{:S(2)}, u32[]{:S(2)}) %collective-permute-start.25) | collective-permute-done | bytes 131104 | tf_op jit(solution)/shard_map/ppermute | solution.py:477
  81.2 1.5 %collective-permute-start.34 = (bf16[128,1024]{1,0:T(8,128)(2,1)S(1)}, bf16[128,1024]{1,0:T(8,128)(2,1)S(1)}, u32[]{:S(2)}, u32[]{:S(2)}) collective-permute-start(bf16[128,1024]{1,0:T(8,128)(2,1)S(1)} %shard_map.114.refs_2_), channel_id=1, source_target_pairs={{0,16},{8,24},{16,0},{24,8},{1,17},{9,25},{17,1},{25,9},{2,18},{10... | collective-permute-start | bytes 786440 | tf_op jit(solution)/shard_map/ppermute | solution.py:477
  82.7 2.1 %collective-permute-done.27.refs_1_ = bf16[64,512]{1,0:T(8,128)(2,1)S(1)} collective-permute-done((bf16[64,512]{1,0:T(8,128)(2,1)S(1)}, bf16[64,512]{1,0:T(8,128)(2,1)S(1)}, u32[]{:S(2)}, u32[]{:S(2)}) %collective-permute-start.27) | collective-permute-done | bytes 65568 | tf_op jit(solution)/shard_map/ppermute | solution.py:477
  87.5 2.3 %collective-permute-done.30.refs_1_ = bf16[2,64,512]{2,1,0:T(8,128)(2,1)S(1)} collective-permute-done((bf16[2,64,512]{2,1,0:T(8,128)(2,1)S(1)}, bf16[2,64,512]{2,1,0:T(8,128)(2,1)S(1)}, u32[]{:S(2)}, u32[]{:S(2)}) %collective-permute-start.30) | collective-permute-done | bytes 131104 | tf_op jit(solution)/shard_map/ppermute | solution.py:477
  90.0 1.5 %collective-permute-done.32.refs_3_ = bf16[2,2,64,512]{3,2,1,0:T(8,128)(2,1)S(1)} collective-permute-done((bf16[2,2,64,512]{3,2,1,0:T(8,128)(2,1)S(1)}, bf16[2,2,64,512]{3,2,1,0:T(8,128)(2,1)S(1)}, u32[]{:S(2)}, u32[]{:S(2)}) %collective-permute-start.32) | collective-permute-done | bytes 262176 | tf_op jit(solution)/shard_map/ppermute | solution.py:477
  (85 shorter events, 28.8 us)
Async XLA Ops:
  0.6 8.4 %collective-permute-start = (bf16[1024,128]{1,0:T(8,128)(2,1)}, bf16[1024,128]{1,0:T(8,128)(2,1)S(1)}, u32[]{:S(2)}, u32[]{:S(2)}) collective-permute-start(bf16[1024,128]{1,0:T(8,128)(2,1)} %refs_5_.1), channel_id=1, source_target_pairs={{0,8},{8,0},{16,24},{24,16},{1,9},{9,1},{17,25},{25,17},{2,10},{10... | collective-permute-start | bytes 786440 | tf_op jit(solution)/shard_map/ppermute | solution.py:477
  5.4 9.2 %collective-permute-start.1 = (bf16[1024,128]{1,0:T(8,128)(2,1)S(1)}, bf16[1024,128]{1,0:T(8,128)(2,1)S(1)}, u32[]{:S(2)}, u32[]{:S(2)}) collective-permute-start(bf16[1024,128]{1,0:T(8,128)(2,1)S(1)} %get-tuple-element.50), channel_id=1, source_target_pairs={{0,1},{1,0},{2,3},{3,2},{4,5},{5,4},{6,7},{7,6},{8,9},{9,8},{10,11... | collective-permute-start | bytes 786440 | tf_op jit(solution)/shard_map/ppermute | solution.py:477
  7.1 9.2 %collective-permute-start.5 = (bf16[1024,128]{1,0:T(8,128)(2,1)S(1)}, bf16[1024,128]{1,0:T(8,128)(2,1)S(1)}, u32[]{:S(2)}, u32[]{:S(2)}) collective-permute-start(bf16[1024,128]{1,0:T(8,128)(2,1)S(1)} %get-tuple-element.48.refs_2_), channel_id=1, source_target_pairs={{0,16},{8,24},{16,0},{24,8},{1,17},{9,25},{17,1},{25,9},{2,18},{10... | collective-permute-start | bytes 786440 | tf_op jit(solution)/shard_map/ppermute | solution.py:477
  10.4 9.9 %collective-permute-start.4 = (bf16[1024,128]{1,0:T(8,128)(2,1)S(1)}, bf16[1024,128]{1,0:T(8,128)(2,1)S(1)}, u32[]{:S(2)}, u32[]{:S(2)}) collective-permute-start(bf16[1024,128]{1,0:T(8,128)(2,1)S(1)} %get-tuple-element.54), channel_id=1, source_target_pairs={{0,1},{1,0},{2,3},{3,2},{4,5},{5,4},{6,7},{7,6},{8,9},{9,8},{10,11... | collective-permute-start | bytes 786440 | tf_op jit(solution)/shard_map/ppermute | solution.py:477
  10.8 10.8 %collective-permute-start.3 = (bf16[1024,128]{1,0:T(8,128)(2,1)S(1)}, bf16[1024,128]{1,0:T(8,128)(2,1)S(1)}, u32[]{:S(2)}, u32[]{:S(2)}) collective-permute-start(bf16[1024,128]{1,0:T(8,128)(2,1)S(1)} %get-tuple-element.48.refs_2_), channel_id=1, source_target_pairs={{0,24},{8,16},{16,8},{24,0},{1,25},{9,17},{17,9},{25,1},{2,26},{10... | collective-permute-start | bytes 786440 | tf_op jit(solution)/shard_map/ppermute | solution.py:477
  17.5 8.4 %collective-permute-start.8 = (bf16[1024,128]{1,0:T(8,128)(2,1)S(1)}, bf16[1024,128]{1,0:T(8,128)(2,1)S(1)}, u32[]{:S(2)}, u32[]{:S(2)}) collective-permute-start(bf16[1024,128]{1,0:T(8,128)(2,1)S(1)} %get-tuple-element.61), channel_id=1, source_target_pairs={{0,1},{1,0},{2,3},{3,2},{4,5},{5,4},{6,7},{7,6},{8,9},{9,8},{10,11... | collective-permute-start | bytes 786440 | tf_op jit(solution)/shard_map/ppermute | solution.py:477
  18.0 7.3 %collective-permute-start.2 = (bf16[512,128]{1,0:T(8,128)(2,1)S(1)}, bf16[512,128]{1,0:T(8,128)(2,1)S(1)}, u32[]{:S(2)}, u32[]{:S(2)}) collective-permute-start(bf16[512,128]{1,0:T(8,128)(2,1)S(1)} %get-tuple-element.52.refs_3_), channel_id=1, source_target_pairs={{0,2},{1,3},{2,0},{3,1},{4,6},{5,7},{6,4},{7,5},{8,10},{9,11},{10,... | collective-permute-start | bytes 393224 | tf_op jit(solution)/shard_map/ppermute | solution.py:477
  22.9 9.6 %collective-permute-start.11 = (bf16[1024,128]{1,0:T(8,128)(2,1)S(1)}, bf16[1024,128]{1,0:T(8,128)(2,1)S(1)}, u32[]{:S(2)}, u32[]{:S(2)}) collective-permute-start(bf16[1024,128]{1,0:T(8,128)(2,1)S(1)} %get-tuple-element.66), channel_id=1, source_target_pairs={{0,1},{1,0},{2,3},{3,2},{4,5},{5,4},{6,7},{7,6},{8,9},{9,8},{10,11... | collective-permute-start | bytes 786440 | tf_op jit(solution)/shard_map/ppermute | solution.py:477
  23.3 7.2 %collective-permute-start.7 = (bf16[512,128]{1,0:T(8,128)(2,1)S(1)}, bf16[512,128]{1,0:T(8,128)(2,1)S(1)}, u32[]{:S(2)}, u32[]{:S(2)}) collective-permute-start(bf16[512,128]{1,0:T(8,128)(2,1)S(1)} %get-tuple-element.56.refs_3_), channel_id=1, source_target_pairs={{0,2},{1,3},{2,0},{3,1},{4,6},{5,7},{6,4},{7,5},{8,10},{9,11},{10,... | collective-permute-start | bytes 393224 | tf_op jit(solution)/shard_map/ppermute | solution.py:477
  26.0 11.0 %collective-permute-start.10 = (bf16[512,128]{1,0:T(8,128)(2,1)S(1)}, bf16[512,128]{1,0:T(8,128)(2,1)S(1)}, u32[]{:S(2)}, u32[]{:S(2)}) collective-permute-start(bf16[512,128]{1,0:T(8,128)(2,1)S(1)} %get-tuple-element.62.refs_2_), channel_id=1, source_target_pairs={{0,2},{1,3},{2,0},{3,1},{4,6},{5,7},{6,4},{7,5},{8,10},{9,11},{10,... | collective-permute-start | bytes 393224 | tf_op jit(solution)/shard_map/ppermute | solution.py:477
  28.7 8.3 %collective-permute-start.6 = (bf16[256,128]{1,0:T(8,128)(2,1)S(1)}, bf16[256,128]{1,0:T(8,128)(2,1)S(1)}, u32[]{:S(2)}, u32[]{:S(2)}) collective-permute-start(bf16[256,128]{1,0:T(8,128)(2,1)S(1)} %get-tuple-element.59.refs_2_), channel_id=1, source_target_pairs={{0,4},{1,5},{2,6},{3,7},{4,0},{5,1},{6,2},{7,3},{8,12},{9,13},{10,... | collective-permute-start | bytes 196616 | tf_op jit(solution)/shard_map/ppermute | solution.py:477
  30.5 7.2 %collective-permute-start.9 = (bf16[256,128]{1,0:T(8,128)(2,1)S(1)}, bf16[256,128]{1,0:T(8,128)(2,1)S(1)}, u32[]{:S(2)}, u32[]{:S(2)}) collective-permute-start(bf16[256,128]{1,0:T(8,128)(2,1)S(1)} %get-tuple-element.64.refs_2_), channel_id=1, source_target_pairs={{0,4},{1,5},{2,6},{3,7},{4,0},{5,1},{6,2},{7,3},{8,12},{9,13},{10,... | collective-permute-start | bytes 196616 | tf_op jit(solution)/shard_map/ppermute | solution.py:477
  47.1 6.8 %collective-permute-start.17 = (bf16[1,128,256]{2,1,0:T(8,128)(2,1)S(1)}, bf16[1,128,256]{2,1,0:T(8,128)(2,1)S(1)}, u32[]{:S(2)}, u32[]{:S(2)}) collective-permute-start(bf16[1,128,256]{2,1,0:T(8,128)(2,1)S(1)} %get-tuple-element.80.refs_0_), channel_id=1, source_target_pairs={{0,4},{1,5},{2,6},{3,7},{4,0},{5,1},{6,2},{7,3},{8,12},{9,13},{10,... | collective-permute-start | bytes 196616 | tf_op jit(solution)/shard_map/ppermute | solution.py:477
  49.5 6.8 %collective-permute-start.16 = (bf16[2,64,512]{2,1,0:T(8,128)(2,1)S(1)}, bf16[2,64,512]{2,1,0:T(8,128)(2,1)S(1)}, u32[]{:S(2)}, u32[]{:S(2)}) collective-permute-start(bf16[2,64,512]{2,1,0:T(8,128)(2,1)S(1)} %get-tuple-element.79.refs_2_), channel_id=1, source_target_pairs={{0,1},{1,0},{2,3},{3,2},{4,5},{5,4},{6,7},{7,6},{8,9},{9,8},{10,11... | collective-permute-start | bytes 393224 | tf_op jit(solution)/shard_map/ppermute | solution.py:477
  51.1 12.6 %collective-permute-start.21 = (bf16[1,256,256]{2,1,0:T(8,128)(2,1)S(1)}, bf16[1,256,256]{2,1,0:T(8,128)(2,1)S(1)}, u32[]{:S(2)}, u32[]{:S(2)}) collective-permute-start(bf16[1,256,256]{2,1,0:T(8,128)(2,1)S(1)} %get-tuple-element.84.refs_0_), channel_id=1, source_target_pairs={{0,4},{1,5},{2,6},{3,7},{4,0},{5,1},{6,2},{7,3},{8,12},{9,13},{10,... | collective-permute-start | bytes 393224 | tf_op jit(solution)/shard_map/ppermute | solution.py:477
  53.9 10.0 %collective-permute-start.20 = (bf16[2,128,256]{2,1,0:T(8,128)(2,1)S(1)}, bf16[2,128,256]{2,1,0:T(8,128)(2,1)S(1)}, u32[]{:S(2)}, u32[]{:S(2)}) collective-permute-start(bf16[2,128,256]{2,1,0:T(8,128)(2,1)S(1)} %shard_map.102.refs_2_.refs_0_), channel_id=1, source_target_pairs={{0,2},{1,3},{2,0},{3,1},{4,6},{5,7},{6,4},{7,5},{8,10},{9,11},{10,... | collective-permute-start | bytes 393224 | tf_op jit(solution)/shard_map/ppermute | solution.py:477
  55.0 11.0 %collective-permute-start.24 = (bf16[2,128,256]{2,1,0:T(8,128)(2,1)S(1)}, bf16[2,128,256]{2,1,0:T(8,128)(2,1)S(1)}, u32[]{:S(2)}, u32[]{:S(2)}) collective-permute-start(bf16[2,128,256]{2,1,0:T(8,128)(2,1)S(1)} %shard_map.101.refs_2_.refs_0_), channel_id=1, source_target_pairs={{0,4},{1,5},{2,6},{3,7},{4,0},{5,1},{6,2},{7,3},{8,12},{9,13},{10,... | collective-permute-start | bytes 393224 | tf_op jit(solution)/shard_map/ppermute | solution.py:477
  56.3 8.5 %collective-permute-start.19 = (bf16[64,512]{1,0:T(8,128)(2,1)S(1)}, bf16[64,512]{1,0:T(8,128)(2,1)S(1)}, u32[]{:S(2)}, u32[]{:S(2)}) collective-permute-start(bf16[64,512]{1,0:T(8,128)(2,1)S(1)} %get-tuple-element.83), channel_id=1, source_target_pairs={{0,16},{8,24},{16,0},{24,8},{1,17},{9,25},{17,1},{25,9},{2,18},{10... | collective-permute-start | bytes 196616 | tf_op jit(solution)/shard_map/ppermute | solution.py:477
  63.8 10.0 %collective-permute-start.23 = (bf16[2,256,256]{2,1,0:T(8,128)(2,1)S(1)}, bf16[2,256,256]{2,1,0:T(8,128)(2,1)S(1)}, u32[]{:S(2)}, u32[]{:S(2)}) collective-permute-start(bf16[2,256,256]{2,1,0:T(8,128)(2,1)S(1)} %shard_map.104.refs_2_.refs_0_), channel_id=1, source_target_pairs={{0,2},{1,3},{2,0},{3,1},{4,6},{5,7},{6,4},{7,5},{8,10},{9,11},{10,... | collective-permute-start | bytes 786440 | tf_op jit(solution)/shard_map/ppermute | solution.py:477
  63.9 10.1 %collective-permute-start.26 = (bf16[4,128,256]{2,1,0:T(8,128)(2,1)S(1)}, bf16[4,128,256]{2,1,0:T(8,128)(2,1)S(1)}, u32[]{:S(2)}, u32[]{:S(2)}) collective-permute-start(bf16[4,128,256]{2,1,0:T(8,128)(2,1)S(1)} %shard_map.105.refs_2_), channel_id=1, source_target_pairs={{0,1},{1,0},{2,3},{3,2},{4,5},{5,4},{6,7},{7,6},{8,9},{9,8},{10,11... | collective-permute-start | bytes 786440 | tf_op jit(solution)/shard_map/ppermute | solution.py:477
  64.8 9.1 %collective-permute-start.22 = (bf16[64,512]{1,0:T(8,128)(2,1)S(1)}, bf16[64,512]{1,0:T(8,128)(2,1)S(1)}, u32[]{:S(2)}, u32[]{:S(2)}) collective-permute-start(bf16[64,512]{1,0:T(8,128)(2,1)S(1)} %shard_map.106.refs_2_.refs_0_), channel_id=1, source_target_pairs={{0,4},{1,5},{2,6},{3,7},{4,0},{5,1},{6,2},{7,3},{8,12},{9,13},{10,... | collective-permute-start | bytes 196616 | tf_op jit(solution)/shard_map/ppermute | solution.py:477
  66.0 14.3 %collective-permute-start.28 = (bf16[4,128,256]{2,1,0:T(8,128)(2,1)S(1)}, bf16[4,128,256]{2,1,0:T(8,128)(2,1)S(1)}, u32[]{:S(2)}, u32[]{:S(2)}) collective-permute-start(bf16[4,128,256]{2,1,0:T(8,128)(2,1)S(1)} %shard_map.107.refs_2_.refs_0_), channel_id=1, source_target_pairs={{0,2},{1,3},{2,0},{3,1},{4,6},{5,7},{6,4},{7,5},{8,10},{9,11},{10,... | collective-permute-start | bytes 786440 | tf_op jit(solution)/shard_map/ppermute | solution.py:477
  73.8 12.3 %collective-permute-start.31 = (bf16[4,256,256]{2,1,0:T(8,128)(2,1)S(1)}, bf16[4,256,256]{2,1,0:T(8,128)(2,1)S(1)}, u32[]{:S(2)}, u32[]{:S(2)}) collective-permute-start(bf16[4,256,256]{2,1,0:T(8,128)(2,1)S(1)} %shard_map.108.refs_2_), channel_id=1, source_target_pairs={{0,1},{1,0},{2,3},{3,2},{4,5},{5,4},{6,7},{7,6},{8,9},{9,8},{10,11... | collective-permute-start | bytes 1572872 | tf_op jit(solution)/shard_map/ppermute | solution.py:477
  81.2 8.7 %collective-permute-start.34 = (bf16[128,1024]{1,0:T(8,128)(2,1)S(1)}, bf16[128,1024]{1,0:T(8,128)(2,1)S(1)}, u32[]{:S(2)}, u32[]{:S(2)}) collective-permute-start(bf16[128,1024]{1,0:T(8,128)(2,1)S(1)} %shard_map.114.refs_2_), channel_id=1, source_target_pairs={{0,16},{8,24},{16,0},{24,8},{1,17},{9,25},{17,1},{25,9},{2,18},{10... | collective-permute-start | bytes 786440 | tf_op jit(solution)/shard_map/ppermute | solution.py:477
  (13 other events, 62.9 us)

commit v9 on v7

--- a/solution.py
+++ b/solution.py
@@ -622,9 +622,9 @@
             arrived.extend(swap(v, "row", 2 * halves[h][p]) for p, v in zip(sent, parts))
 
     weight_core()
-    join("A")
     join("C")
     weight_side()
+    join("A")
     join("M")
     for _ in range(stages - 1):
         join("C")

time: 93.2 us -> 96.6 us (1.036)
  starting transfers between devices: 37.8 us -> 41.7 us
  waiting for transfers between devices: 39 us -> 37.8 us
    ppermute x35, starting transfers between devices: 37.8 us -> 41.7 us  [swap(): return lax.ppermute(v, axis, [(i, i ^ bit) for i in range(size)])]
    ppermute x35, waiting for transfers between devices: 39 us -> 37.8 us  [swap(): return lax.ppermute(v, axis, [(i, i ^ bit) for i in range(size)])]
  transfers between devices with their start and end apart: 35 -> 35, of which waited for: 16 -> 17; matrix products, arithmetic and copies ran while one was open for 0% -> 0% of each run, Pallas kernels for 13% -> 12%
where the time goes in v9:
time: 96.6 us; the launch traced here: 95.7 us
  starting transfers between devices  41.7 us (43%)
  waiting for transfers between devices  37.8 us (39%)
  Pallas kernels  14.6 us (15%)
  between operations  1.54 us (2%)
    ppermute x35, starting transfers between devices, swap(): return lax.ppermute(v, axis, [(i, i ^ bit) for i in range(size)])  41.7 us
    ppermute x35, waiting for transfers between devices, swap(): return lax.ppermute(v, axis, [(i, i ^ bit) for i in range(size)])  37.8 us
    pallas_call x36, Pallas kernels, call(): pl.pallas_call(run, out_shape=tuple(out_shape) if many else out_shape, in...  14.6 us
  transfers between devices with their start and end apart: 35, of which 17 were waited for; matrix products, arithmetic and copies ran while one was open for 0% of the time, Pallas kernels for 12%

profile of v9, /device:TPU:0, one launch (start us, length us, event | category | flops | bytes accessed | tf_op | source)
XLA Modules:
  0.0 95.7 jit_solution(3609139759080926289)
XLA Ops:
  1.8 3.6 %shard_map.85 = (bf16[1024,1024]{1,0:T(8,128)(2,1)S(1)}, bf16[1024,1024]{1,0:T(8,128)(2,1)S(1)}, bf16[1024,128]{1,0:T(8,128)(2,1)S(1)}, bf16[1024,128]{1,0:T(8,128)(2,1)S(1)}) custom-call(s32[1]{0:T(128)} %bitcast.7.refs_0_, s32[1]{0:T(128)} %bitcast.1.refs_1_.refs_0_, s32[1]{0:T(128)} %bitcast.2.refs_2_.refs_0_, s32[2,96]{1,0:T(2,128)} %bitcast.9, ...), custom_call_target="tpu_custom_call" | custom-call | tf_op jit(solution)/shard_map/pallas_call | solution.py:29
  5.4 1.7 %collective-permute-start.1 = (bf16[1024,128]{1,0:T(8,128)(2,1)S(1)}, bf16[1024,128]{1,0:T(8,128)(2,1)S(1)}, u32[]{:S(2)}, u32[]{:S(2)}) collective-permute-start(bf16[1024,128]{1,0:T(8,128)(2,1)S(1)} %get-tuple-element.48), channel_id=1, source_target_pairs={{0,1},{1,0},{2,3},{3,2},{4,5},{5,4},{6,7},{7,6},{8,9},{9,8},{10,11... | collective-permute-start | bytes 786440 | tf_op jit(solution)/shard_map/ppermute | solution.py:472
  7.1 2.1 %collective-permute-start.5 = (bf16[1024,128]{1,0:T(8,128)(2,1)S(1)}, bf16[1024,128]{1,0:T(8,128)(2,1)S(1)}, u32[]{:S(2)}, u32[]{:S(2)}) collective-permute-start(bf16[1024,128]{1,0:T(8,128)(2,1)S(1)} %get-tuple-element.46.refs_2_), channel_id=1, source_target_pairs={{0,16},{8,24},{16,0},{24,8},{1,17},{9,25},{17,1},{25,9},{2,18},{10... | collective-permute-start | bytes 786440 | tf_op jit(solution)/shard_map/ppermute | solution.py:472
  11.0 3.4 %collective-permute-done.1.refs_1_ = bf16[1024,128]{1,0:T(8,128)(2,1)S(1)} collective-permute-done((bf16[1024,128]{1,0:T(8,128)(2,1)S(1)}, bf16[1024,128]{1,0:T(8,128)(2,1)S(1)}, u32[]{:S(2)}, u32[]{:S(2)}) %collective-permute-start.1) | collective-permute-done | bytes 262176 | tf_op jit(solution)/shard_map/ppermute | solution.py:472
  14.5 1.8 %collective-permute-done.5.refs_2_ = bf16[1024,128]{1,0:T(8,128)(2,1)S(1)} collective-permute-done((bf16[1024,128]{1,0:T(8,128)(2,1)S(1)}, bf16[1024,128]{1,0:T(8,128)(2,1)S(1)}, u32[]{:S(2)}, u32[]{:S(2)}) %collective-permute-start.5) | collective-permute-done | bytes 262176 | tf_op jit(solution)/shard_map/ppermute | solution.py:472
  18.0 2.2 %collective-permute-start.2 = (bf16[512,128]{1,0:T(8,128)(2,1)S(1)}, bf16[512,128]{1,0:T(8,128)(2,1)S(1)}, u32[]{:S(2)}, u32[]{:S(2)}) collective-permute-start(bf16[512,128]{1,0:T(8,128)(2,1)S(1)} %get-tuple-element.50.refs_3_), channel_id=1, source_target_pairs={{0,2},{1,3},{2,0},{3,1},{4,6},{5,7},{6,4},{7,5},{8,10},{9,11},{10,... | collective-permute-start | bytes 393224 | tf_op jit(solution)/shard_map/ppermute | solution.py:472
  23.7 2.0 %collective-permute-start.7 = (bf16[512,128]{1,0:T(8,128)(2,1)S(1)}, bf16[512,128]{1,0:T(8,128)(2,1)S(1)}, u32[]{:S(2)}, u32[]{:S(2)}) collective-permute-start(bf16[512,128]{1,0:T(8,128)(2,1)S(1)} %get-tuple-element.54.refs_3_), channel_id=1, source_target_pairs={{0,2},{1,3},{2,0},{3,1},{4,6},{5,7},{6,4},{7,5},{8,10},{9,11},{10,... | collective-permute-start | bytes 393224 | tf_op jit(solution)/shard_map/ppermute | solution.py:472
  26.1 2.6 %collective-permute-start.10 = (bf16[512,128]{1,0:T(8,128)(2,1)S(1)}, bf16[512,128]{1,0:T(8,128)(2,1)S(1)}, u32[]{:S(2)}, u32[]{:S(2)}) collective-permute-start(bf16[512,128]{1,0:T(8,128)(2,1)S(1)} %get-tuple-element.60.refs_2_), channel_id=1, source_target_pairs={{0,2},{1,3},{2,0},{3,1},{4,6},{5,7},{6,4},{7,5},{8,10},{9,11},{10,... | collective-permute-start | bytes 393224 | tf_op jit(solution)/shard_map/ppermute | solution.py:472
  28.7 1.6 %collective-permute-start.6 = (bf16[256,128]{1,0:T(8,128)(2,1)S(1)}, bf16[256,128]{1,0:T(8,128)(2,1)S(1)}, u32[]{:S(2)}, u32[]{:S(2)}) collective-permute-start(bf16[256,128]{1,0:T(8,128)(2,1)S(1)} %get-tuple-element.57.refs_2_), channel_id=1, source_target_pairs={{0,4},{1,5},{2,6},{3,7},{4,0},{5,1},{6,2},{7,3},{8,12},{9,13},{10,... | collective-permute-start | bytes 196616 | tf_op jit(solution)/shard_map/ppermute | solution.py:472
  30.4 2.2 %collective-permute-start.9 = (bf16[256,128]{1,0:T(8,128)(2,1)S(1)}, bf16[256,128]{1,0:T(8,128)(2,1)S(1)}, u32[]{:S(2)}, u32[]{:S(2)}) collective-permute-start(bf16[256,128]{1,0:T(8,128)(2,1)S(1)} %get-tuple-element.62.refs_2_), channel_id=1, source_target_pairs={{0,4},{1,5},{2,6},{3,7},{4,0},{5,1},{6,2},{7,3},{8,12},{9,13},{10,... | collective-permute-start | bytes 196616 | tf_op jit(solution)/shard_map/ppermute | solution.py:472
  32.6 2.5 %collective-permute-start.13 = (bf16[512,128]{1,0:T(8,128)(2,1)S(1)}, bf16[512,128]{1,0:T(8,128)(2,1)S(1)}, u32[]{:S(2)}, u32[]{:S(2)}) collective-permute-start(bf16[512,128]{1,0:T(8,128)(2,1)S(1)} %get-tuple-element.65.refs_2_), channel_id=1, source_target_pairs={{0,2},{1,3},{2,0},{3,1},{4,6},{5,7},{6,4},{7,5},{8,10},{9,11},{10,... | collective-permute-start | bytes 393224 | tf_op jit(solution)/shard_map/ppermute | solution.py:472
  35.2 2.2 %collective-permute-done.9.refs_4_.refs_3_ = bf16[256,128]{1,0:T(8,128)(2,1)S(1)} collective-permute-done((bf16[256,128]{1,0:T(8,128)(2,1)S(1)}, bf16[256,128]{1,0:T(8,128)(2,1)S(1)}, u32[]{:S(2)}, u32[]{:S(2)}) %collective-permute-start.9) | collective-permute-done | bytes 65568 | tf_op jit(solution)/shard_map/ppermute | solution.py:472
  39.0 1.8 %collective-permute-start.14 = (bf16[256,128]{1,0:T(8,128)(2,1)S(1)}, bf16[256,128]{1,0:T(8,128)(2,1)S(1)}, u32[]{:S(2)}, u32[]{:S(2)}) collective-permute-start(bf16[256,128]{1,0:T(8,128)(2,1)S(1)} %get-tuple-element.70.refs_10_), channel_id=1, source_target_pairs={{0,4},{1,5},{2,6},{3,7},{4,0},{5,1},{6,2},{7,3},{8,12},{9,13},{10,... | collective-permute-start | bytes 196616 | tf_op jit(solution)/shard_map/ppermute | solution.py:472
  40.8 2.6 %collective-permute-done.12.refs_5_ = bf16[256,128]{1,0:T(8,128)(2,1)S(1)} collective-permute-done((bf16[256,128]{1,0:T(8,128)(2,1)S(1)}, bf16[256,128]{1,0:T(8,128)(2,1)S(1)}, u32[]{:S(2)}, u32[]{:S(2)}) %collective-permute-start.12) | collective-permute-done | bytes 65568 | tf_op jit(solution)/shard_map/ppermute | solution.py:472
  46.0 1.9 %collective-permute-done.15.refs_2_ = f32[256,512]{1,0:T(8,128)S(1)} collective-permute-done((f32[256,512]{1,0:T(8,128)S(1)}, f32[256,512]{1,0:T(8,128)S(1)}, u32[]{:S(2)}, u32[]{:S(2)}) %collective-permute-start.15) | collective-permute-done | bytes 524320 | tf_op jit(solution)/shard_map/ppermute | solution.py:472
  48.0 2.8 %collective-permute-start.16 = (bf16[2,64,512]{2,1,0:T(8,128)(2,1)S(1)}, bf16[2,64,512]{2,1,0:T(8,128)(2,1)S(1)}, u32[]{:S(2)}, u32[]{:S(2)}) collective-permute-start(bf16[2,64,512]{2,1,0:T(8,128)(2,1)S(1)} %get-tuple-element.77.refs_2_), channel_id=1, source_target_pairs={{0,1},{1,0},{2,3},{3,2},{4,5},{5,4},{6,7},{7,6},{8,9},{9,8},{10,11... | collective-permute-start | bytes 393224 | tf_op jit(solution)/shard_map/ppermute | solution.py:472
  51.9 1.9 %collective-permute-start.20 = (bf16[1,256,256]{2,1,0:T(8,128)(2,1)S(1)}, bf16[1,256,256]{2,1,0:T(8,128)(2,1)S(1)}, u32[]{:S(2)}, u32[]{:S(2)}) collective-permute-start(bf16[1,256,256]{2,1,0:T(8,128)(2,1)S(1)} %get-tuple-element.81.refs_0_), channel_id=1, source_target_pairs={{0,4},{1,5},{2,6},{3,7},{4,0},{5,1},{6,2},{7,3},{8,12},{9,13},{10,... | collective-permute-start | bytes 393224 | tf_op jit(solution)/shard_map/ppermute | solution.py:472
  53.8 4.4 %collective-permute-done.17.refs_1_ = bf16[1,128,256]{2,1,0:T(8,128)(2,1)S(1)} collective-permute-done((bf16[1,128,256]{2,1,0:T(8,128)(2,1)S(1)}, bf16[1,128,256]{2,1,0:T(8,128)(2,1)S(1)}, u32[]{:S(2)}, u32[]{:S(2)}) %collective-permute-start.17) | collective-permute-done | bytes 65568 | tf_op jit(solution)/shard_map/ppermute | solution.py:472
  59.1 3.4 %collective-permute-start.24 = (bf16[2,128,256]{2,1,0:T(8,128)(2,1)S(1)}, bf16[2,128,256]{2,1,0:T(8,128)(2,1)S(1)}, u32[]{:S(2)}, u32[]{:S(2)}) collective-permute-start(bf16[2,128,256]{2,1,0:T(8,128)(2,1)S(1)} %shard_map.103.refs_2_.refs_0_), channel_id=1, source_target_pairs={{0,4},{1,5},{2,6},{3,7},{4,0},{5,1},{6,2},{7,3},{8,12},{9,13},{10,... | collective-permute-start | bytes 393224 | tf_op jit(solution)/shard_map/ppermute | solution.py:472
  64.0 4.0 %collective-permute-done.19.refs_1_ = bf16[2,128,256]{2,1,0:T(8,128)(2,1)S(1)} collective-permute-done((bf16[2,128,256]{2,1,0:T(8,128)(2,1)S(1)}, bf16[2,128,256]{2,1,0:T(8,128)(2,1)S(1)}, u32[]{:S(2)}, u32[]{:S(2)}) %collective-permute-start.19) | collective-permute-done | bytes 131104 | tf_op jit(solution)/shard_map/ppermute | solution.py:472
  68.7 2.7 %collective-permute-start.28 = (bf16[4,128,256]{2,1,0:T(8,128)(2,1)S(1)}, bf16[4,128,256]{2,1,0:T(8,128)(2,1)S(1)}, u32[]{:S(2)}, u32[]{:S(2)}) collective-permute-start(bf16[4,128,256]{2,1,0:T(8,128)(2,1)S(1)} %shard_map.107.refs_2_.refs_0_), channel_id=1, source_target_pairs={{0,2},{1,3},{2,0},{3,1},{4,6},{5,7},{6,4},{7,5},{8,10},{9,11},{10,... | collective-permute-start | bytes 786440 | tf_op jit(solution)/shard_map/ppermute | solution.py:472
  71.4 3.6 %collective-permute-done.23.refs_1_ = bf16[2,256,256]{2,1,0:T(8,128)(2,1)S(1)} collective-permute-done((bf16[2,256,256]{2,1,0:T(8,128)(2,1)S(1)}, bf16[2,256,256]{2,1,0:T(8,128)(2,1)S(1)}, u32[]{:S(2)}, u32[]{:S(2)}) %collective-permute-start.23) | collective-permute-done | bytes 262176 | tf_op jit(solution)/shard_map/ppermute | solution.py:472
  77.6 5.2 %collective-permute-done.25.refs_1_ = f32[64,512]{1,0:T(8,128)S(1)} collective-permute-done((f32[64,512]{1,0:T(8,128)S(1)}, f32[64,512]{1,0:T(8,128)S(1)}, u32[]{:S(2)}, u32[]{:S(2)}) %collective-permute-start.25) | collective-permute-done | bytes 131104 | tf_op jit(solution)/shard_map/ppermute | solution.py:472
  89.6 2.6 %collective-permute-done.30.refs_1_ = bf16[2,64,512]{2,1,0:T(8,128)(2,1)S(1)} collective-permute-done((bf16[2,64,512]{2,1,0:T(8,128)(2,1)S(1)}, bf16[2,64,512]{2,1,0:T(8,128)(2,1)S(1)}, u32[]{:S(2)}, u32[]{:S(2)}) %collective-permute-start.30) | collective-permute-done | bytes 131104 | tf_op jit(solution)/shard_map/ppermute | solution.py:472
  (86 shorter events, 29.1 us)
Async XLA Ops:
  0.6 8.5 %collective-permute-start = (bf16[1024,128]{1,0:T(8,128)(2,1)}, bf16[1024,128]{1,0:T(8,128)(2,1)S(1)}, u32[]{:S(2)}, u32[]{:S(2)}) collective-permute-start(bf16[1024,128]{1,0:T(8,128)(2,1)} %refs_5_.1), channel_id=1, source_target_pairs={{0,8},{8,0},{16,24},{24,16},{1,9},{9,1},{17,25},{25,17},{2,10},{10... | collective-permute-start | bytes 786440 | tf_op jit(solution)/shard_map/ppermute | solution.py:472
  5.4 9.0 %collective-permute-start.1 = (bf16[1024,128]{1,0:T(8,128)(2,1)S(1)}, bf16[1024,128]{1,0:T(8,128)(2,1)S(1)}, u32[]{:S(2)}, u32[]{:S(2)}) collective-permute-start(bf16[1024,128]{1,0:T(8,128)(2,1)S(1)} %get-tuple-element.48), channel_id=1, source_target_pairs={{0,1},{1,0},{2,3},{3,2},{4,5},{5,4},{6,7},{7,6},{8,9},{9,8},{10,11... | collective-permute-start | bytes 786440 | tf_op jit(solution)/shard_map/ppermute | solution.py:472
  7.1 9.2 %collective-permute-start.5 = (bf16[1024,128]{1,0:T(8,128)(2,1)S(1)}, bf16[1024,128]{1,0:T(8,128)(2,1)S(1)}, u32[]{:S(2)}, u32[]{:S(2)}) collective-permute-start(bf16[1024,128]{1,0:T(8,128)(2,1)S(1)} %get-tuple-element.46.refs_2_), channel_id=1, source_target_pairs={{0,16},{8,24},{16,0},{24,8},{1,17},{9,25},{17,1},{25,9},{2,18},{10... | collective-permute-start | bytes 786440 | tf_op jit(solution)/shard_map/ppermute | solution.py:472
  10.5 9.8 %collective-permute-start.4 = (bf16[1024,128]{1,0:T(8,128)(2,1)S(1)}, bf16[1024,128]{1,0:T(8,128)(2,1)S(1)}, u32[]{:S(2)}, u32[]{:S(2)}) collective-permute-start(bf16[1024,128]{1,0:T(8,128)(2,1)S(1)} %get-tuple-element.52), channel_id=1, source_target_pairs={{0,1},{1,0},{2,3},{3,2},{4,5},{5,4},{6,7},{7,6},{8,9},{9,8},{10,11... | collective-permute-start | bytes 786440 | tf_op jit(solution)/shard_map/ppermute | solution.py:472
  10.9 11.1 %collective-permute-start.3 = (bf16[1024,128]{1,0:T(8,128)(2,1)S(1)}, bf16[1024,128]{1,0:T(8,128)(2,1)S(1)}, u32[]{:S(2)}, u32[]{:S(2)}) collective-permute-start(bf16[1024,128]{1,0:T(8,128)(2,1)S(1)} %get-tuple-element.46.refs_2_), channel_id=1, source_target_pairs={{0,24},{8,16},{16,8},{24,0},{1,25},{9,17},{17,9},{25,1},{2,26},{10... | collective-permute-start | bytes 786440 | tf_op jit(solution)/shard_map/ppermute | solution.py:472
  17.5 8.5 %collective-permute-start.8 = (bf16[1024,128]{1,0:T(8,128)(2,1)S(1)}, bf16[1024,128]{1,0:T(8,128)(2,1)S(1)}, u32[]{:S(2)}, u32[]{:S(2)}) collective-permute-start(bf16[1024,128]{1,0:T(8,128)(2,1)S(1)} %get-tuple-element.59), channel_id=1, source_target_pairs={{0,1},{1,0},{2,3},{3,2},{4,5},{5,4},{6,7},{7,6},{8,9},{9,8},{10,11... | collective-permute-start | bytes 786440 | tf_op jit(solution)/shard_map/ppermute | solution.py:472
  18.0 7.6 %collective-permute-start.2 = (bf16[512,128]{1,0:T(8,128)(2,1)S(1)}, bf16[512,128]{1,0:T(8,128)(2,1)S(1)}, u32[]{:S(2)}, u32[]{:S(2)}) collective-permute-start(bf16[512,128]{1,0:T(8,128)(2,1)S(1)} %get-tuple-element.50.refs_3_), channel_id=1, source_target_pairs={{0,2},{1,3},{2,0},{3,1},{4,6},{5,7},{6,4},{7,5},{8,10},{9,11},{10,... | collective-permute-start | bytes 393224 | tf_op jit(solution)/shard_map/ppermute | solution.py:472
  23.2 9.4 %collective-permute-start.11 = (bf16[1024,128]{1,0:T(8,128)(2,1)S(1)}, bf16[1024,128]{1,0:T(8,128)(2,1)S(1)}, u32[]{:S(2)}, u32[]{:S(2)}) collective-permute-start(bf16[1024,128]{1,0:T(8,128)(2,1)S(1)} %get-tuple-element.64), channel_id=1, source_target_pairs={{0,1},{1,0},{2,3},{3,2},{4,5},{5,4},{6,7},{7,6},{8,9},{9,8},{10,11... | collective-permute-start | bytes 786440 | tf_op jit(solution)/shard_map/ppermute | solution.py:472
  26.1 9.1 %collective-permute-start.10 = (bf16[512,128]{1,0:T(8,128)(2,1)S(1)}, bf16[512,128]{1,0:T(8,128)(2,1)S(1)}, u32[]{:S(2)}, u32[]{:S(2)}) collective-permute-start(bf16[512,128]{1,0:T(8,128)(2,1)S(1)} %get-tuple-element.60.refs_2_), channel_id=1, source_target_pairs={{0,2},{1,3},{2,0},{3,1},{4,6},{5,7},{6,4},{7,5},{8,10},{9,11},{10,... | collective-permute-start | bytes 393224 | tf_op jit(solution)/shard_map/ppermute | solution.py:472
  30.4 7.0 %collective-permute-start.9 = (bf16[256,128]{1,0:T(8,128)(2,1)S(1)}, bf16[256,128]{1,0:T(8,128)(2,1)S(1)}, u32[]{:S(2)}, u32[]{:S(2)}) collective-permute-start(bf16[256,128]{1,0:T(8,128)(2,1)S(1)} %get-tuple-element.62.refs_2_), channel_id=1, source_target_pairs={{0,4},{1,5},{2,6},{3,7},{4,0},{5,1},{6,2},{7,3},{8,12},{9,13},{10,... | collective-permute-start | bytes 196616 | tf_op jit(solution)/shard_map/ppermute | solution.py:472
  48.0 11.1 %collective-permute-start.16 = (bf16[2,64,512]{2,1,0:T(8,128)(2,1)S(1)}, bf16[2,64,512]{2,1,0:T(8,128)(2,1)S(1)}, u32[]{:S(2)}, u32[]{:S(2)}) collective-permute-start(bf16[2,64,512]{2,1,0:T(8,128)(2,1)S(1)} %get-tuple-element.77.refs_2_), channel_id=1, source_target_pairs={{0,1},{1,0},{2,3},{3,2},{4,5},{5,4},{6,7},{7,6},{8,9},{9,8},{10,11... | collective-permute-start | bytes 393224 | tf_op jit(solution)/shard_map/ppermute | solution.py:472
  50.8 7.4 %collective-permute-start.17 = (bf16[1,128,256]{2,1,0:T(8,128)(2,1)S(1)}, bf16[1,128,256]{2,1,0:T(8,128)(2,1)S(1)}, u32[]{:S(2)}, u32[]{:S(2)}) collective-permute-start(bf16[1,128,256]{2,1,0:T(8,128)(2,1)S(1)} %get-tuple-element.78.refs_0_), channel_id=1, source_target_pairs={{0,4},{1,5},{2,6},{3,7},{4,0},{5,1},{6,2},{7,3},{8,12},{9,13},{10,... | collective-permute-start | bytes 196616 | tf_op jit(solution)/shard_map/ppermute | solution.py:472
  51.3 7.8 %collective-permute-start.21 = (bf16[1,128,256]{2,1,0:T(8,128)(2,1)S(1)}, bf16[1,128,256]{2,1,0:T(8,128)(2,1)S(1)}, u32[]{:S(2)}, u32[]{:S(2)}) collective-permute-start(bf16[1,128,256]{2,1,0:T(8,128)(2,1)S(1)} %get-tuple-element.82.refs_0_), channel_id=1, source_target_pairs={{0,1},{1,0},{2,3},{3,2},{4,5},{5,4},{6,7},{7,6},{8,9},{9,8},{10,11... | collective-permute-start | bytes 196616 | tf_op jit(solution)/shard_map/ppermute | solution.py:472
  51.9 11.9 %collective-permute-start.20 = (bf16[1,256,256]{2,1,0:T(8,128)(2,1)S(1)}, bf16[1,256,256]{2,1,0:T(8,128)(2,1)S(1)}, u32[]{:S(2)}, u32[]{:S(2)}) collective-permute-start(bf16[1,256,256]{2,1,0:T(8,128)(2,1)S(1)} %get-tuple-element.81.refs_0_), channel_id=1, source_target_pairs={{0,4},{1,5},{2,6},{3,7},{4,0},{5,1},{6,2},{7,3},{8,12},{9,13},{10,... | collective-permute-start | bytes 393224 | tf_op jit(solution)/shard_map/ppermute | solution.py:472
  58.3 9.7 %collective-permute-start.19 = (bf16[2,128,256]{2,1,0:T(8,128)(2,1)S(1)}, bf16[2,128,256]{2,1,0:T(8,128)(2,1)S(1)}, u32[]{:S(2)}, u32[]{:S(2)}) collective-permute-start(bf16[2,128,256]{2,1,0:T(8,128)(2,1)S(1)} %shard_map.101.refs_2_.refs_0_), channel_id=1, source_target_pairs={{0,2},{1,3},{2,0},{3,1},{4,6},{5,7},{6,4},{7,5},{8,10},{9,11},{10,... | collective-permute-start | bytes 393224 | tf_op jit(solution)/shard_map/ppermute | solution.py:472
  59.1 9.6 %collective-permute-start.24 = (bf16[2,128,256]{2,1,0:T(8,128)(2,1)S(1)}, bf16[2,128,256]{2,1,0:T(8,128)(2,1)S(1)}, u32[]{:S(2)}, u32[]{:S(2)}) collective-permute-start(bf16[2,128,256]{2,1,0:T(8,128)(2,1)S(1)} %shard_map.103.refs_2_.refs_0_), channel_id=1, source_target_pairs={{0,4},{1,5},{2,6},{3,7},{4,0},{5,1},{6,2},{7,3},{8,12},{9,13},{10,... | collective-permute-start | bytes 393224 | tf_op jit(solution)/shard_map/ppermute | solution.py:472
  63.9 11.1 %collective-permute-start.23 = (bf16[2,256,256]{2,1,0:T(8,128)(2,1)S(1)}, bf16[2,256,256]{2,1,0:T(8,128)(2,1)S(1)}, u32[]{:S(2)}, u32[]{:S(2)}) collective-permute-start(bf16[2,256,256]{2,1,0:T(8,128)(2,1)S(1)} %shard_map.104.refs_2_.refs_0_), channel_id=1, source_target_pairs={{0,2},{1,3},{2,0},{3,1},{4,6},{5,7},{6,4},{7,5},{8,10},{9,11},{10,... | collective-permute-start | bytes 786440 | tf_op jit(solution)/shard_map/ppermute | solution.py:472
  68.0 8.7 %collective-permute-start.26 = (bf16[4,128,256]{2,1,0:T(8,128)(2,1)S(1)}, bf16[4,128,256]{2,1,0:T(8,128)(2,1)S(1)}, u32[]{:S(2)}, u32[]{:S(2)}) collective-permute-start(bf16[4,128,256]{2,1,0:T(8,128)(2,1)S(1)} %shard_map.105.refs_2_), channel_id=1, source_target_pairs={{0,1},{1,0},{2,3},{3,2},{4,5},{5,4},{6,7},{7,6},{8,9},{9,8},{10,11... | collective-permute-start | bytes 786440 | tf_op jit(solution)/shard_map/ppermute | solution.py:472
  68.1 7.3 %collective-permute-start.22 = (bf16[64,512]{1,0:T(8,128)(2,1)S(1)}, bf16[64,512]{1,0:T(8,128)(2,1)S(1)}, u32[]{:S(2)}, u32[]{:S(2)}) collective-permute-start(bf16[64,512]{1,0:T(8,128)(2,1)S(1)} %shard_map.106.refs_2_.refs_0_), channel_id=1, source_target_pairs={{0,4},{1,5},{2,6},{3,7},{4,0},{5,1},{6,2},{7,3},{8,12},{9,13},{10,... | collective-permute-start | bytes 196616 | tf_op jit(solution)/shard_map/ppermute | solution.py:472
  68.7 15.4 %collective-permute-start.28 = (bf16[4,128,256]{2,1,0:T(8,128)(2,1)S(1)}, bf16[4,128,256]{2,1,0:T(8,128)(2,1)S(1)}, u32[]{:S(2)}, u32[]{:S(2)}) collective-permute-start(bf16[4,128,256]{2,1,0:T(8,128)(2,1)S(1)} %shard_map.107.refs_2_.refs_0_), channel_id=1, source_target_pairs={{0,2},{1,3},{2,0},{3,1},{4,6},{5,7},{6,4},{7,5},{8,10},{9,11},{10,... | collective-permute-start | bytes 786440 | tf_op jit(solution)/shard_map/ppermute | solution.py:472
  75.1 13.1 %collective-permute-start.31 = (bf16[4,256,256]{2,1,0:T(8,128)(2,1)S(1)}, bf16[4,256,256]{2,1,0:T(8,128)(2,1)S(1)}, u32[]{:S(2)}, u32[]{:S(2)}) collective-permute-start(bf16[4,256,256]{2,1,0:T(8,128)(2,1)S(1)} %shard_map.108.refs_2_), channel_id=1, source_target_pairs={{0,1},{1,0},{2,3},{3,2},{4,5},{5,4},{6,7},{7,6},{8,9},{9,8},{10,11... | collective-permute-start | bytes 1572872 | tf_op jit(solution)/shard_map/ppermute | solution.py:472
  75.5 7.3 %collective-permute-start.25 = (f32[64,512]{1,0:T(8,128)S(1)}, f32[64,512]{1,0:T(8,128)S(1)}, u32[]{:S(2)}, u32[]{:S(2)}) collective-permute-start(f32[64,512]{1,0:T(8,128)S(1)} %shard_map.109.refs_4_.refs_0_), channel_id=1, source_target_pairs={{0,2},{1,3},{2,0},{3,1},{4,6},{5,7},{6,4},{7,5},{8,10},{9,11},{10,... | collective-permute-start | bytes 393224 | tf_op jit(solution)/shard_map/ppermute | solution.py:472
  77.5 7.5 %collective-permute-start.29 = (bf16[128,1024]{1,0:T(8,128)(2,1)S(1)}, bf16[128,1024]{1,0:T(8,128)(2,1)S(1)}, u32[]{:S(2)}, u32[]{:S(2)}) collective-permute-start(bf16[128,1024]{1,0:T(8,128)(2,1)S(1)} %shard_map.110.refs_2_), channel_id=1, source_target_pairs={{0,8},{8,0},{16,24},{24,16},{1,9},{9,1},{17,25},{25,17},{2,10},{10... | collective-permute-start | bytes 786440 | tf_op jit(solution)/shard_map/ppermute | solution.py:472
  85.0 7.8 %collective-permute-start.34 = (bf16[128,1024]{1,0:T(8,128)(2,1)S(1)}, bf16[128,1024]{1,0:T(8,128)(2,1)S(1)}, u32[]{:S(2)}, u32[]{:S(2)}) collective-permute-start(bf16[128,1024]{1,0:T(8,128)(2,1)S(1)} %shard_map.114.refs_2_), channel_id=1, source_target_pairs={{0,16},{8,24},{16,0},{24,8},{1,17},{9,25},{17,1},{25,9},{2,18},{10... | collective-permute-start | bytes 786440 | tf_op jit(solution)/shard_map/ppermute | solution.py:472
  (13 other events, 63.1 us)
